TPU v7x, 32 devices: a whole 2x2x4 slice. The times are simulated.
32 devices in a mesh: dp: 8 (over y, x, core), tensor: 4 (over z).
Axes of the slice: x: 2, y: 2, z: 4, core: 2. Of those that a mesh axis runs over, the one named last changes fastest.
Arguments:
- hidden_in: bfloat16 [8192, 2048], P(('dp', 'tensor')), may hold values from -6 to 6
- gain_attn: bfloat16 [2048], replicated, may hold values from 0.5 to 1.5
- w_query: bfloat16 [2048, 2048], P(None, 'tensor'), may hold values from -0.125 to 0.125
- w_key: bfloat16 [2048, 1024], P(None, 'tensor'), may hold values from -0.125 to 0.125
- w_value: bfloat16 [2048, 1024], P(None, 'tensor'), may hold values from -0.125 to 0.125
- w_out: bfloat16 [2048, 2048], P('tensor'), may hold values from -0.5 to 0.5
- gain_ffn: bfloat16 [2048], replicated, may hold values from 0.5 to 1.5
- w_gate: bfloat16 [2048, 8192], P(None, 'tensor'), may hold values from -0.125 to 0.125
- w_up: bfloat16 [2048, 8192], P(None, 'tensor'), may hold values from -0.125 to 0.125
- w_down: bfloat16 [8192, 2048], P('tensor'), may hold values from -0.0625 to 0.0625
- segments: int32 [8192], P('dp'), may hold values from 3 to 7, as said below
- parents: int32 [64], P('dp'), may hold values from 0 to 6, as said below
- cotangent: bfloat16 [8192, 2048], P(('dp', 'tensor')), may hold values from -6 to 6
Outputs:
- output: bfloat16 [8192, 2048], P(('dp', 'tensor'))
- input_grad: bfloat16 [8192, 2048], P(('dp', 'tensor'))
- gain_attn_grad: float32 [2048], P('dp')
- w_query_grad: float32 [2048, 2048], P('dp', 'tensor')
- w_key_grad: float32 [2048, 1024], P('dp', 'tensor')
- w_value_grad: float32 [2048, 1024], P('dp', 'tensor')
- w_out_grad: float32 [2048, 2048], P('tensor', 'dp')
- gain_ffn_grad: float32 [2048], P('dp')
- w_gate_grad: float32 [2048, 8192], P('dp', 'tensor')
- w_up_grad: float32 [2048, 8192], P('dp', 'tensor')
- w_down_grad: float32 [8192, 2048], P('tensor', 'dp')
Inputs may be any that keep to these rules, and one draw needn't show every extreme that they name: `segments`: each tree is whole aligned blocks of 128 tokens inside one group of 1024 tokens and holds 4 to 8 blocks; some tree holds exactly 8 blocks. Every token of a tree carries the index, within its group of 8 blocks, of the tree's last block. `parents`: A tree's first block has 0; every other block names an earlier block of its own tree.
All inputs are finite; a program needn't handle non-finite values.
Results may differ from a plain program's by a relative error of at most 0.025.
Values may be sent and summed in bfloat16 or wider, within the bound.
A program may use at most 256 MiB of HBM per device.

v0:
```python
import jax
import jax.numpy as jnp
from jax import lax
from jax.sharding import PartitionSpec as P

HD = 128
BLK = 128
MAXB = 8


NORM_EPS = 1e-05
ROPE_BASE = 1000000.0
HIGHEST = lax.Precision.HIGHEST


def tree_tables(segment_ids, parent_ids):
    block_count = parent_ids.shape[0]
    first_ids = segment_ids.reshape(block_count, -1)[:, 0]
    block_iota = jnp.arange(block_count, dtype=jnp.int32)
    same_tree = first_ids[:, None] == first_ids[None, :]
    tree_start = jnp.min(jnp.where(same_tree, block_iota[None, :], block_count), axis=1)
    parent_block = tree_start + parent_ids
    climb_step = (block_iota[None, :] == parent_block[:, None]).astype(jnp.float32)

    def climb(step_index, reach_now):
        return jnp.minimum(reach_now + jnp.dot(reach_now, climb_step, precision=HIGHEST), 1.0)

    ancestry = lax.fori_loop(0, MAXB - 1, climb, jnp.eye(block_count, dtype=jnp.float32))
    return (ancestry, jnp.sum(ancestry, axis=1) - 1.0)


def rope_tables(depth):
    token_total = depth.shape[0] * BLK
    offsets = (jnp.arange(token_total, dtype=jnp.int32) % BLK).astype(jnp.float32)
    places = jnp.repeat(depth, BLK) * BLK + offsets
    freq_index = jnp.arange(HD // 2, dtype=jnp.int32).astype(jnp.float32)
    inverse_freq = ROPE_BASE ** (-2.0 * freq_index / HD)
    angles = places[:, None] * inverse_freq[None, :]
    angles = jnp.concatenate([angles, angles], axis=1)
    return (jnp.cos(angles)[:, None, :], jnp.sin(angles)[:, None, :])


def rotate(heads_in, cosine, sine):
    half_width = heads_in.shape[-1] // 2
    turned = jnp.concatenate([-heads_in[..., half_width:], heads_in[..., :half_width]], axis=-1)
    return heads_in * cosine + turned * sine


def rotate_back(grads_in, cosine, sine):
    half_width = grads_in.shape[-1] // 2
    scaled = grads_in * sine
    return grads_in * cosine + jnp.concatenate(
        [scaled[..., half_width:], -scaled[..., :half_width]], axis=-1
    )


def visible(ancestry, first_row, block_rows, token_total):
    sub_table = lax.dynamic_slice_in_dim(ancestry, first_row // BLK, block_rows // BLK, 0)
    spread_table = jnp.broadcast_to(
        sub_table[:, None, :, None], (block_rows // BLK, BLK, sub_table.shape[1], BLK)
    )
    row_ids = first_row + jnp.arange(block_rows, dtype=jnp.int32)
    col_ids = jnp.arange(token_total, dtype=jnp.int32)
    return (spread_table.reshape(block_rows, token_total) > 0.5) & (
        col_ids[None, :] <= row_ids[:, None]
    )


def normalize(rows_wide, gain_wide):
    inverse = lax.rsqrt(jnp.mean(rows_wide * rows_wide, axis=-1, keepdims=True) + NORM_EPS)
    scaled_rows = rows_wide * inverse
    return (scaled_rows, inverse, (scaled_rows * gain_wide).astype(jnp.bfloat16))


def norm_back(normed_grad, scaled_rows, inverse, gain_wide):
    weighted = normed_grad * gain_wide
    row_grad = inverse * (
        weighted - scaled_rows * jnp.mean(weighted * scaled_rows, axis=-1, keepdims=True)
    )
    return (row_grad, jnp.sum(normed_grad * scaled_rows, axis=0))


def spread_rows(local_rows, weight_cols):
    gathered = lax.all_gather(local_rows, "tensor", axis=0, tiled=True)
    return (gathered, jnp.dot(gathered, weight_cols, preferred_element_type=jnp.float32))


def weight_grad(kept_rows, row_grads):
    return lax.dot_general(
        kept_rows, row_grads, (((0,), (0,)), ((), ())), preferred_element_type=jnp.float32
    )


def branch_sum(source_rows, weight_rows):
    return lax.psum_scatter(
        jnp.dot(source_rows, weight_rows, preferred_element_type=jnp.float32).astype(jnp.bfloat16),
        "tensor",
        scatter_dimension=0,
        tiled=True,
    ).astype(jnp.float32)


def input_sum(row_grads, weight_cols):
    return lax.psum_scatter(
        lax.dot_general(
            row_grads, weight_cols, (((1,), (1,)), ((), ())), preferred_element_type=jnp.float32
        ).astype(jnp.bfloat16),
        "tensor",
        scatter_dimension=0,
        tiled=True,
    ).astype(jnp.float32)


def collect(grad_rows):
    return lax.all_gather(grad_rows, "tensor", axis=0, tiled=True)


def attend_forward(queries, key_rows, value_rows, ancestry):
    token_total, head_count, head_width = queries.shape
    block_rows = min(512, token_total)
    repeat_count = head_count // key_rows.shape[1]
    keys_wide = jnp.repeat(key_rows, repeat_count, axis=1)
    values_wide = jnp.repeat(value_rows, repeat_count, axis=1)
    scale = HD ** (-0.5)

    def one_block(block_index):
        query_block = lax.dynamic_slice_in_dim(queries, block_index * block_rows, block_rows, 0)
        scores = (
            jnp.einsum("qhd,khd->hqk", query_block, keys_wide, preferred_element_type=jnp.float32)
            * scale
        )
        allowed = visible(ancestry, block_index * block_rows, block_rows, token_total)
        scores = jnp.where(allowed[None], scores, -1e30)
        row_top = jnp.max(scores, axis=-1, keepdims=True)
        exp_scores = jnp.exp(scores - row_top)
        row_mass = jnp.sum(exp_scores, axis=-1, keepdims=True)
        soft_low = (exp_scores / row_mass).astype(jnp.bfloat16)
        block_out = jnp.einsum(
            "hqk,khd->qhd", soft_low, values_wide, preferred_element_type=jnp.float32
        )
        return (block_out.astype(jnp.bfloat16), (row_top + jnp.log(row_mass))[..., 0])

    block_count = token_total // block_rows
    mixed_heads, log_mass = lax.map(one_block, jnp.arange(block_count, dtype=jnp.int32))
    return (mixed_heads.reshape(token_total, head_count * head_width), log_mass)


def attend_backward(queries, key_rows, value_rows, ancestry, log_mass, mixed_grad):
    token_total, head_count, head_width = queries.shape
    key_heads = key_rows.shape[1]
    block_rows = min(512, token_total)
    repeat_count = head_count // key_heads
    keys_wide = jnp.repeat(key_rows, repeat_count, axis=1)
    values_wide = jnp.repeat(value_rows, repeat_count, axis=1)
    scale = HD ** (-0.5)
    out_grad = mixed_grad.reshape(token_total, head_count, head_width)

    def one_block(running, block_index):
        key_sum, value_sum = running
        query_block = lax.dynamic_slice_in_dim(queries, block_index * block_rows, block_rows, 0)
        grad_block = lax.dynamic_slice_in_dim(out_grad, block_index * block_rows, block_rows, 0)
        scores = (
            jnp.einsum("qhd,khd->hqk", query_block, keys_wide, preferred_element_type=jnp.float32)
            * scale
        )
        allowed = visible(ancestry, block_index * block_rows, block_rows, token_total)
        soft_wide = jnp.where(
            allowed[None], jnp.exp(scores - log_mass[block_index][..., None]), 0.0
        )
        soft_low = soft_wide.astype(jnp.bfloat16)
        value_sum = value_sum + jnp.einsum(
            "hqk,qhd->khd", soft_low, grad_block, preferred_element_type=jnp.float32
        )
        soft_grad = jnp.einsum(
            "qhd,khd->hqk", grad_block, values_wide, preferred_element_type=jnp.float32
        )
        row_dot = jnp.sum(soft_wide * soft_grad, axis=-1, keepdims=True)
        score_grad = (soft_wide * (soft_grad - row_dot)).astype(jnp.bfloat16)
        query_part = (
            jnp.einsum("hqk,khd->qhd", score_grad, keys_wide, preferred_element_type=jnp.float32)
            * scale
        )
        key_sum = (
            key_sum
            + jnp.einsum(
                "hqk,qhd->khd", score_grad, query_block, preferred_element_type=jnp.float32
            )
            * scale
        )
        return ((key_sum, value_sum), query_part)

    zero_heads = jnp.zeros((token_total, head_count, head_width), jnp.float32)
    block_count = token_total // block_rows
    (key_sum, value_sum), query_parts = lax.scan(
        one_block, (zero_heads, zero_heads), jnp.arange(block_count, dtype=jnp.int32)
    )
    key_grad = key_sum.reshape(token_total, key_heads, repeat_count, head_width).sum(axis=2)
    value_grad = value_sum.reshape(token_total, key_heads, repeat_count, head_width).sum(axis=2)
    return (query_parts.reshape(token_total, head_count, head_width), key_grad, value_grad)


def shards(
    hidden_in,
    gain_attn,
    w_query,
    w_key,
    w_value,
    w_out,
    gain_ffn,
    w_gate,
    w_up,
    w_down,
    segments,
    parents,
    cotangent,
):
    token_total = segments.shape[0]
    query_cols = w_query.shape[1]
    key_cols = w_key.shape[1]
    unit_cols = w_gate.shape[1]
    ancestry, depth = tree_tables(segments, parents)
    cosine, sine = rope_tables(depth)
    w_project = jnp.concatenate([w_query, w_key, w_value], axis=1)
    w_gate_up = jnp.concatenate([w_gate, w_up], axis=1)
    gain_attn_wide = gain_attn.astype(jnp.float32)
    gain_ffn_wide = gain_ffn.astype(jnp.float32)
    rows_wide = hidden_in.astype(jnp.float32)
    scaled_attn, inverse_attn, normed_attn = normalize(rows_wide, gain_attn_wide)
    kept_attn, projected = spread_rows(normed_attn, w_project)
    queries = rotate(
        projected[:, :query_cols].reshape(token_total, query_cols // HD, HD), cosine, sine
    ).astype(jnp.bfloat16)
    key_rows = rotate(
        projected[:, query_cols : query_cols + key_cols].reshape(token_total, key_cols // HD, HD),
        cosine,
        sine,
    ).astype(jnp.bfloat16)
    value_rows = (
        projected[:, query_cols + key_cols :]
        .reshape(token_total, key_cols // HD, HD)
        .astype(jnp.bfloat16)
    )
    mixed_heads, log_mass = attend_forward(queries, key_rows, value_rows, ancestry)
    middle = rows_wide + branch_sum(mixed_heads, w_out)
    scaled_ffn, inverse_ffn, normed_ffn = normalize(middle, gain_ffn_wide)
    kept_ffn, gate_up = spread_rows(normed_ffn, w_gate_up)
    gate_pre = gate_up[:, :unit_cols]
    up_pre = gate_up[:, unit_cols:]
    gate_sigmoid = jax.nn.sigmoid(gate_pre)
    gate_silu = gate_pre * gate_sigmoid
    hidden_act = (gate_silu * up_pre).astype(jnp.bfloat16)
    output = (middle + branch_sum(hidden_act, w_down)).astype(jnp.bfloat16)
    ffn_out_grad = collect(cotangent)
    act_grad = lax.dot_general(
        ffn_out_grad, w_down, (((1,), (1,)), ((), ())), preferred_element_type=jnp.float32
    )
    w_down_grad = lax.dot_general(
        hidden_act, ffn_out_grad, (((0,), (0,)), ((), ())), preferred_element_type=jnp.float32
    )
    gate_grad = act_grad * up_pre * gate_sigmoid * (1.0 + gate_pre * (1.0 - gate_sigmoid))
    up_grad = act_grad * gate_silu
    gate_up_grad = jnp.concatenate([gate_grad, up_grad], axis=1).astype(jnp.bfloat16)
    gate_up_wgrad = weight_grad(kept_ffn, gate_up_grad)
    w_gate_grad = gate_up_wgrad[:, :unit_cols]
    w_up_grad = gate_up_wgrad[:, unit_cols:]
    ffn_in_grad = input_sum(gate_up_grad, w_gate_up)
    middle_back, gain_ffn_part = norm_back(ffn_in_grad, scaled_ffn, inverse_ffn, gain_ffn_wide)
    middle_grad = cotangent.astype(jnp.float32) + middle_back
    branch_grad = collect(middle_grad.astype(jnp.bfloat16))
    mixed_grad = lax.dot_general(
        branch_grad, w_out, (((1,), (1,)), ((), ())), preferred_element_type=jnp.float32
    ).astype(jnp.bfloat16)
    w_out_grad = lax.dot_general(
        mixed_heads, branch_grad, (((0,), (0,)), ((), ())), preferred_element_type=jnp.float32
    )
    query_rot_grad, key_rot_grad, value_sum_grad = attend_backward(
        queries, key_rows, value_rows, ancestry, log_mass, mixed_grad
    )
    project_grad = jnp.concatenate(
        [
            rotate_back(query_rot_grad, cosine, sine).reshape(token_total, query_cols),
            rotate_back(key_rot_grad, cosine, sine).reshape(token_total, key_cols),
            value_sum_grad.reshape(token_total, key_cols),
        ],
        axis=1,
    ).astype(jnp.bfloat16)
    project_wgrad = weight_grad(kept_attn, project_grad)
    w_query_grad = project_wgrad[:, :query_cols]
    w_key_grad = project_wgrad[:, query_cols : query_cols + key_cols]
    w_value_grad = project_wgrad[:, query_cols + key_cols :]
    attn_in_grad = input_sum(project_grad, w_project)
    input_back, gain_attn_part = norm_back(attn_in_grad, scaled_attn, inverse_attn, gain_attn_wide)
    input_grad = (middle_grad + input_back).astype(jnp.bfloat16)
    gain_totals = lax.psum(jnp.stack([gain_attn_part, gain_ffn_part]), "tensor")
    (
        gain_attn_grad,
        w_query_grad,
        w_key_grad,
        w_value_grad,
        w_out_grad,
        gain_ffn_grad,
        w_gate_grad,
        w_up_grad,
        w_down_grad,
    ) = (
        lax.psum_scatter(
            gain_totals[0].astype(jnp.bfloat16), "dp", scatter_dimension=0, tiled=True
        ).astype(jnp.float32),
        lax.psum_scatter(
            w_query_grad.astype(jnp.bfloat16), "dp", scatter_dimension=0, tiled=True
        ).astype(jnp.float32),
        lax.psum_scatter(
            w_key_grad.astype(jnp.bfloat16), "dp", scatter_dimension=0, tiled=True
        ).astype(jnp.float32),
        lax.psum_scatter(
            w_value_grad.astype(jnp.bfloat16), "dp", scatter_dimension=0, tiled=True
        ).astype(jnp.float32),
        lax.psum_scatter(
            w_out_grad.astype(jnp.bfloat16), "dp", scatter_dimension=1, tiled=True
        ).astype(jnp.float32),
        lax.psum_scatter(
            gain_totals[1].astype(jnp.bfloat16), "dp", scatter_dimension=0, tiled=True
        ).astype(jnp.float32),
        lax.psum_scatter(
            w_gate_grad.astype(jnp.bfloat16), "dp", scatter_dimension=0, tiled=True
        ).astype(jnp.float32),
        lax.psum_scatter(
            w_up_grad.astype(jnp.bfloat16), "dp", scatter_dimension=0, tiled=True
        ).astype(jnp.float32),
        lax.psum_scatter(
            w_down_grad.astype(jnp.bfloat16), "dp", scatter_dimension=1, tiled=True
        ).astype(jnp.float32),
    )
    return (
        output,
        input_grad,
        gain_attn_grad,
        w_query_grad,
        w_key_grad,
        w_value_grad,
        w_out_grad,
        gain_ffn_grad,
        w_gate_grad,
        w_up_grad,
        w_down_grad,
    )


def solution(mesh):
    return jax.shard_map(
        shards,
        mesh=mesh,
        in_specs=(
            P(("dp", "tensor"), None),
            P(),
            P(None, "tensor"),
            P(None, "tensor"),
            P(None, "tensor"),
            P("tensor", None),
            P(),
            P(None, "tensor"),
            P(None, "tensor"),
            P("tensor", None),
            P("dp"),
            P("dp"),
            P(("dp", "tensor"), None),
        ),
        out_specs=(
            P(("dp", "tensor"), None),
            P(("dp", "tensor"), None),
            P("dp"),
            P("dp", "tensor"),
            P("dp", "tensor"),
            P("dp", "tensor"),
            P("tensor", "dp"),
            P("dp"),
            P("dp", "tensor"),
            P("dp", "tensor"),
            P("tensor", "dp"),
        ),
        check_vma=False,
    )
```

profile of v0, /device:TPU:0, one launch (start us, length us, event | category | flops | bytes accessed | tf_op | source)
XLA Modules:
  0.0 1170.3 jit_solution(5736524670511958972)
XLA Ops:
  10.2 2.5 fusion.65
  16.8 3.5 constant_dynamic-update-slice_fusion.2
  22.6 2.5 constant_dynamic-update-slice_fusion
  25.1 71.3 %all-gather.5.cloned.1.call-done = bf16[1024,2048]{1,0:T(8,128)(2,1)} async-done(((bf16[256,2048]{1,0:T(8,128)(2,1)}), bf16[1024,2048]{1,0:T(8,128)(2,1)}) %all-gather.5.cloned.1.call-update) | async-done | bytes 4194320 | tf_op jit(solution)/shard_map/all_gather | solution.py:84
  96.4 7.6 fusion.98
  117.3 31.4 %while.44 = (s32[]{:T(128)}, bf16[2,512,4,128]{3,2,1,0:T(4,128)(2,1)}, f32[2,4,512]{2,1,0:T(4,128)S(1)}, s32[2]{0:T(128)S(1)}, f32[8,8]{1,0:T(8,128)S(1)}, /*ind...) while((s32[]{:T(128)}, ...), condition=%wide.region_8.9_spmd.clone, body=%wide.region_5.8_spmd.clone.sunk | while | flops 1100216832 | bytes 48304812 | solution.py:144
  122.6 3.1 fusion.153
  125.8 2.4 fusion.154
  128.2 3.2 fusion.155
  138.2 3.1 fusion.153
  143.7 3.2 fusion.155
  149.5 5.6 convolution_convert_fusion.3
  155.8 74.8 %reduce-scatter.12.cloned.1.call-done = bf16[256,2048]{1,0:T(8,128)(2,1)} async-done(((bf16[1024,2048]{1,0:T(8,128)(2,1)}), bf16[256,2048]{1,0:T(8,128)(2,1)}) %reduce-scatter.12.cloned.1.call-update) | async-done | bytes 1048592 | tf_op jit(solution)/shard_map/reduce_scatter | solution.py:95
  232.3 2.6 multiply_convert_fusion.4
  235.5 8.6 constant_dynamic-update-slice_fusion.4
  244.1 8.6 constant_dynamic-update-slice_fusion.3
  252.7 63.6 %all-gather.7.cloned.1.call-done = bf16[1024,2048]{1,0:T(8,128)(2,1)} async-done(((bf16[256,2048]{1,0:T(8,128)(2,1)}), bf16[1024,2048]{1,0:T(8,128)(2,1)}) %all-gather.7.cloned.1.call-update) | async-done | bytes 4194320 | tf_op jit(solution)/shard_map/all_gather | solution.py:84
  316.3 23.4 %fusion.99 = f32[1024,4096]{1,0:T(8,128)} fusion(bf16[1024,2048]{1,0:T(8,128)(2,1)} %all-gather.7.cloned.1.call-done, bf16[2048,4096]{1,0:T(8,128)(2,1)} %constant_dynamic-update-slice_fusion.3), kind=kOutput, calls=%fused_computation.171 | convolution fusion | flops 17179869184 | bytes 37748736 | tf_op jit(solution)/shard_map/dot_general | solution.py:85
  339.7 57.4 %all-gather.9.cloned.1.call-done = bf16[1024,2048]{1,0:T(8,128)(2,1)} async-done(((bf16[256,2048]{1,0:T(8,128)(2,1)}), bf16[1024,2048]{1,0:T(8,128)(2,1)}) %all-gather.9.cloned.1.call-update) | async-done | bytes 4194320 | tf_op jit(solution)/shard_map/all_gather | solution.py:115
  397.2 21.7 %multiply_convert_fusion.2 = (bf16[1024,2048]{1,0:T(8,128)(2,1)}, bf16[1024,2048]{1,0:T(8,128)(2,1)}, bf16[1024,2048]{1,0:T(8,128)(2,1)}) fusion(f32[1024,4096]{1,0:T(8,128)} %fusion.99, bf16[1024,2048]{1,0:T(8,128)(2,1)} %all-gather.9.cloned.1.call-done, bf16[2048,2048]{1,0:T(8,128)(2,1)} %param.28), kind=kOutput, calls=%fused_computation.63 | convolution fusion | flops 8621391872 | bytes 41943040 | tf_op jit(solution)/shard_map/dot_general | solution.py:254
  418.8 23.9 %fusion.50 = bf16[1024,2048]{1,0:T(8,128)(2,1)} fusion(bf16[2048,4096]{1,0:T(8,128)(2,1)} %constant_dynamic-update-slice_fusion.3, bf16[1024,2048]{1,0:T(8,128)(2,1)} %get-tuple-element.501, bf16[1024,2048]{1,0:T(8,128)(2,1)} %get-tuple-element.500), kind=kOutput, calls=%fused_computation.69 | convolution fusion | flops 17198743552 | bytes 29360128 | tf_op jit(solution)/shard_map/dot_general | solution.py:105
  442.9 75.2 %reduce-scatter.16.cloned.1.call-done = bf16[256,2048]{1,0:T(8,128)(2,1)} async-done(((bf16[1024,2048]{1,0:T(8,128)(2,1)}), bf16[256,2048]{1,0:T(8,128)(2,1)}) %reduce-scatter.16.cloned.1.call-update) | async-done | bytes 1048592 | tf_op jit(solution)/shard_map/reduce_scatter | solution.py:104
  518.1 3.1 fusion.64
  521.8 3.9 fusion.93
  525.7 25.2 %convolution_convert_fusion = bf16[2048,4096]{1,0:T(8,128)(2,1)} fusion(bf16[1024,2048]{1,0:T(8,128)(2,1)} %all-gather.7.cloned.1.call-done, bf16[1024,2048]{1,0:T(8,128)(2,1)} %get-tuple-element.501, bf16[1024,2048]{1,0:T(8,128)(2,1)} %get-tuple-element.500), kind=kOutput, calls=%fused_computation.60 | convolution fusion | flops 17205035008 | bytes 29360128 | tf_op jit(solution)/shard_map/dot_general | solution.py:89
  551.0 11.9 %fusion.94 = (bf16[2048,2048]{1,0:T(8,128)(2,1)}, bf16[2048,2048]{1,0:T(8,128)(2,1)}) fusion(bf16[2048,4096]{1,0:T(8,128)(2,1)} %convolution_convert_fusion), kind=kLoop, calls=%fused_computation.166 | loop fusion | bytes 33554432 | tf_op jit(solution)/shard_map/slice | solution.py:265
  565.6 2.9 copy.95
  568.5 14.1 %convolution_convert_fusion.1 = bf16[2048,2048]{1,0:T(8,128)(2,1)} fusion(bf16[1024,2048]{1,0:T(8,128)(2,1)} %get-tuple-element.504, bf16[1024,2048]{1,0:T(8,128)(2,1)} %all-gather.9.cloned.1.call-done), kind=kOutput, calls=%fused_computation.67 | convolution fusion | flops 8594128896 | bytes 16777216 | tf_op jit(solution)/shard_map/dot_general | solution.py:257
  582.7 24.4 %all-gather.11.cloned.1.call-done = bf16[1024,2048]{1,0:T(8,128)(2,1)} async-done(((bf16[256,2048]{1,0:T(8,128)(2,1)}), bf16[1024,2048]{1,0:T(8,128)(2,1)}) %all-gather.11.cloned.1.call-update) | async-done | bytes 4194320 | tf_op jit(solution)/shard_map/all_gather | solution.py:115
  607.1 5.5 convolution_convert_fusion.7
  612.6 73.7 %while.45 = (s32[]{:T(128)}, f32[1024,4,128]{0,2,1:T(8,128)}, f32[1024,4,128]{0,2,1:T(8,128)}, f32[2,512,4,128]{3,1,2,0:T(8,128)}, s32[2]{0:T(128)S(1)}, /*index...) while((s32[]{:T(128)}, f32[1024,4,128]{0,2,1:T(8,128)}, ...), condition=%wide.region_16.17_spmd.clone, body=%wide.region_14.16_spmd.clone.sunk | while | flops 2719742464 | bytes 172028880 | solution.py:194
  615.6 6.9 fusion.165
  626.5 6.1 multiply_reduce_fusion.3
  632.6 3.8 multiply_convert_fusion.6
  636.4 4.8 bitcast_add_fusion.4
  641.2 5.3 bitcast_add_fusion.5
  652.5 5.5 fusion.165
  662.0 6.1 multiply_reduce_fusion.3
  668.7 3.7 multiply_convert_fusion.6
  672.5 5.6 bitcast_add_fusion.4
  678.1 5.3 bitcast_add_fusion.5
  686.4 3.2 copy.96
  689.6 2.7 copy.94
  701.2 3.1 copy.97
  707.8 2.9 copy.98
  710.7 3.6 fusion.70
  715.0 5.1 convolution_convert_fusion.4
  724.4 3.1 slice.106
  727.6 6.2 convolution_convert_fusion.6
  733.9 9.2 convolution_convert_fusion.5
  743.2 14.1 %convolution_convert_fusion.2 = bf16[1024,2048]{1,0:T(8,128)(2,1)} fusion(bf16[1024,2048]{1,0:T(8,128)(2,1)} %get-tuple-element.504, bf16[2048,2048]{1,0:T(8,128)(2,1)} %param.28), kind=kOutput, calls=%fused_computation.70 | convolution fusion | flops 8592031744 | bytes 16777216 | tf_op jit(solution)/shard_map/dot_general | solution.py:96
  759.2 2.8 convert_element_type.197
  762.0 2.9 convert_element_type.198
  764.9 65.4 %reduce-scatter.32.cloned.1.call-done = bf16[2048,256]{1,0:T(8,128)(2,1)} async-done(((bf16[2048,2048]{1,0:T(8,128)(2,1)}), bf16[2048,256]{1,0:T(8,128)(2,1)}) %reduce-scatter.32.cloned.1.call-update) | async-done | bytes 1048592 | tf_op jit(solution)/shard_map/reduce_scatter | solution.py:330
  830.3 2.7 convert_element_type.200
  833.0 36.7 %reduce-scatter.22.cloned.1.call-done = bf16[256,256]{1,0:T(8,128)(2,1)} async-done(((bf16[2048,256]{1,0:T(8,128)(2,1)}), bf16[256,256]{1,0:T(8,128)(2,1)}) %reduce-scatter.22.cloned.1.call-update) | async-done | bytes 131088 | tf_op jit(solution)/shard_map/reduce_scatter | solution.py:312
  871.4 38.5 %reduce-scatter.24.cloned.1.call-done = bf16[256,256]{1,0:T(8,128)(2,1)} async-done(((bf16[2048,256]{1,0:T(8,128)(2,1)}), bf16[256,256]{1,0:T(8,128)(2,1)}) %reduce-scatter.24.cloned.1.call-update) | async-done | bytes 131088 | tf_op jit(solution)/shard_map/reduce_scatter | solution.py:315
  911.5 43.1 %reduce-scatter.20.cloned.1.call-done = bf16[256,512]{1,0:T(8,128)(2,1)} async-done(((bf16[2048,512]{1,0:T(8,128)(2,1)}), bf16[256,512]{1,0:T(8,128)(2,1)}) %reduce-scatter.20.cloned.1.call-update) | async-done | bytes 262160 | tf_op jit(solution)/shard_map/reduce_scatter | solution.py:309
  956.5 42.8 %reduce-scatter.26.cloned.1.call-done = bf16[512,256]{1,0:T(8,128)(2,1)} async-done(((bf16[512,2048]{1,0:T(8,128)(2,1)}), bf16[512,256]{1,0:T(8,128)(2,1)}) %reduce-scatter.26.cloned.1.call-update) | async-done | bytes 262160 | tf_op jit(solution)/shard_map/reduce_scatter | solution.py:318
  1001.0 77.3 %reduce-scatter.18.cloned.1.call-done = bf16[256,2048]{1,0:T(8,128)(2,1)} async-done(((bf16[1024,2048]{1,0:T(8,128)(2,1)}), bf16[256,2048]{1,0:T(8,128)(2,1)}) %reduce-scatter.18.cloned.1.call-update) | async-done | bytes 1048592 | tf_op jit(solution)/shard_map/reduce_scatter | solution.py:104
  1080.4 18.4 %psum.7 = bf16[2,2048]{1,0:T(2,128)(2,1)S(1)} all-reduce(f32[2,2048]{1,0:T(2,128)S(1)} %pad_maximum_fusion.10), channel_id=1, replica_groups=mesh['dp'=8,'tensor'=4] {'tensor'}, use_global_device_ids=true, to_apply=%region_23.24 | all-reduce | flops 4096 | bytes 24576 | tf_op jit(solution)/shard_map/psum | solution.py:294
  1098.8 12.1 %all-reduce.2 = (bf16[2048]{0:T(1024)(128)(2,1)S(1)}, bf16[2048]{0:T(1024)(128)(2,1)S(1)}) all-reduce(bf16[2048]{0:T(1024)(128)(2,1)S(1)} %get-tuple-element.449, bf16[2048]{0:T(1024)(128)(2,1)S(1)} %get-tuple-element.448), channel_id=6, replica_groups=mesh['dp'=8,'tensor'=4] {'dp'}, use_global_device_ids=true, to_apply=%region_24.25.clone | all-reduce | flops 4096 | bytes 16384
  1112.3 45.8 %reduce-scatter.14.cloned.1.call-done = bf16[256,2048]{1,0:T(8,128)(2,1)} async-done(((bf16[1024,2048]{1,0:T(8,128)(2,1)}), bf16[256,2048]{1,0:T(8,128)(2,1)}) %reduce-scatter.14.cloned.1.call-update) | async-done | bytes 1048592 | tf_op jit(solution)/shard_map/reduce_scatter | solution.py:95
  1158.0 5.5 fusion.60
  (267 shorter events, 89.5 us)
Async XLA Ops:
  7.2 142.4 %copy-start = (bf16[512,2048]{1,0:T(8,128)(2,1)S(1)}, bf16[512,2048]{1,0:T(8,128)(2,1)}, u32[]{:S(2)}) copy-start(bf16[512,2048]{1,0:T(8,128)(2,1)} %param.24) | copy-start | bytes 6291460
  7.2 5.6 copy-start.41
  7.2 5.9 copy-start.45
  7.2 89.1 %all-gather.5.cloned.1.call-start = ((), (), s32[]{:S(2)}) async-start(), calls=%async_computation.11 | async-start | bytes 5242880 | tf_op jit(solution)/shard_map/all_gather | solution.py:84
  12.7 217.9 %reduce-scatter.12.cloned.1.call-start = ((), (), s32[]{:S(2)}) async-start(), calls=%async_computation.12 | async-start | bytes 5242880 | tf_op jit(solution)/shard_map/reduce_scatter | solution.py:95
  16.8 94.8 %copy-start.9 = (f32[1024,128]{0,1:T(8,128)}, f32[1024,128]{0,1:T(8,128)S(1)}, u32[]{:S(2)}) copy-start(f32[1024,128]{0,1:T(8,128)S(1)} %get-tuple-element.518) | copy-start | bytes 1572868
  16.8 94.8 %copy-start.11 = (f32[1024,128]{0,1:T(8,128)}, f32[1024,128]{0,1:T(8,128)S(1)}, u32[]{:S(2)}) copy-start(f32[1024,128]{0,1:T(8,128)S(1)} %get-tuple-element.517) | copy-start | bytes 1572868
  125.7 2.4 copy-start.8
  128.2 3.3 copy-start.43
  141.3 2.4 copy-start.8
  143.7 3.3 copy-start.43
  148.7 6.4 copy-start.23
  148.8 6.4 copy-start.31
  155.1 75.5 %copy-start.5 = (bf16[256,2048]{1,0:T(8,128)(2,1)S(1)}, bf16[256,2048]{1,0:T(8,128)(2,1)}, u32[]{:S(2)}) copy-start(bf16[256,2048]{1,0:T(8,128)(2,1)} %param.19) | copy-start | bytes 3145732
  155.2 161.2 %all-gather.7.cloned.1.call-start = ((), (), s32[]{:S(2)}) async-start(), calls=%async_computation.13 | async-start | bytes 5242880 | tf_op jit(solution)/shard_map/all_gather | solution.py:84
  155.8 365.4 %copy-start.27 = (f32[2048]{0:T(1024)}, f32[2048]{0:T(1024)S(1)}, u32[]{:S(2)}) copy-start(f32[2048]{0:T(1024)S(1)} %convert_element_type.174) | copy-start | bytes 24580
  232.3 288.9 %copy-start.34 = (f32[256]{0:T(256)}, f32[256]{0:T(256)S(1)}, u32[]{:S(2)}) copy-start(f32[256]{0:T(256)S(1)} %add_rsqrt_fusion) | copy-start | bytes 3076
  234.9 162.2 %all-gather.9.cloned.1.call-start = ((), (), s32[]{:S(2)}) async-start(), calls=%async_computation.15 | async-start | bytes 5242880 | tf_op jit(solution)/shard_map/all_gather | solution.py:115
  235.5 282.6 %reduce-scatter.16.cloned.1.call-start = ((), (), s32[]{:S(2)}) async-start(), calls=%async_computation.16 | async-start | bytes 5242880 | tf_op jit(solution)/shard_map/reduce_scatter | solution.py:104
  442.7 164.4 %all-gather.11.cloned.1.call-start = ((), (), s32[]{:S(2)}) async-start(), calls=%async_computation.17 | async-start | bytes 5242880 | tf_op jit(solution)/shard_map/all_gather | solution.py:115
  525.7 233.5 %reduce-scatter.28.cloned.1.call-start = ((), (), s32[]{:S(2)}) async-start(), calls=%async_computation.23 | async-start | bytes 9437184 | tf_op jit(solution)/shard_map/reduce_scatter | solution.py:324
  562.9 199.1 %reduce-scatter.30.cloned.1.call-start = ((), (), s32[]{:S(2)}) async-start(), calls=%async_computation.24 | async-start | bytes 9437184 | tf_op jit(solution)/shard_map/reduce_scatter | solution.py:327
  563.6 266.7 %reduce-scatter.32.cloned.1.call-start = ((), (), s32[]{:S(2)}) async-start(), calls=%async_computation.25 | async-start | bytes 9437184 | tf_op jit(solution)/shard_map/reduce_scatter | solution.py:330
  582.6 30.0 %copy-start.24 = (f32[8,8]{1,0:T(8,128)S(1)}, f32[8,8]{1,0:T(8,128)}, u32[]{:S(2)}) copy-start(f32[8,8]{1,0:T(8,128)} %copy-done.23) | copy-start | bytes 772
  582.6 30.0 %copy-start.32 = (f32[2,4,512]{2,1,0:T(4,128)S(1)}, f32[2,4,512]{2,1,0:T(4,128)}, u32[]{:S(2)}) copy-start(f32[2,4,512]{2,1,0:T(4,128)} %copy-done.31) | copy-start | bytes 49156
  582.7 287.1 %reduce-scatter.22.cloned.1.call-start = ((), (), s32[]{:S(2)}) async-start(), calls=%async_computation.20 | async-start | bytes 1179648 | tf_op jit(solution)/shard_map/reduce_scatter | solution.py:312
  614.2 8.2 copy-start.3
  626.5 6.1 slice-start
  626.5 6.1 slice-start.1
  636.4 4.8 copy-start.18
  636.4 4.8 copy-start.20
  641.2 5.4 copy-start.1
  641.2 5.4 copy-start.4
  641.2 6.1 copy-start.15
  646.6 2.0 copy-start.21
  651.1 6.9 copy-start.3
  661.9 6.1 slice-start
  661.9 6.8 slice-start.1
  672.5 5.6 copy-start.18
  672.5 5.6 copy-start.20
  678.0 5.3 copy-start.1
  678.0 5.3 copy-start.4
  678.1 5.7 copy-start.15
  686.3 3.2 copy-start.17
  686.4 5.9 copy-start.2
  686.4 5.9 copy-start.22
  692.2 3.9 copy-start.10
  693.9 3.9 copy-start.13
  710.6 3.6 copy-start.25
  710.7 3.7 copy-start.26
  710.7 4.4 copy-start.42
  720.2 1.9 copy-start.19
  723.6 186.2 %reduce-scatter.24.cloned.1.call-start = ((), (), s32[]{:S(2)}) async-start(), calls=%async_computation.21 | async-start | bytes 1179648 | tf_op jit(solution)/shard_map/reduce_scatter | solution.py:315
  724.4 230.3 %reduce-scatter.20.cloned.1.call-start = ((), (), s32[]{:S(2)}) async-start(), calls=%async_computation.19 | async-start | bytes 2359296 | tf_op jit(solution)/shard_map/reduce_scatter | solution.py:309
  727.6 271.6 %reduce-scatter.26.cloned.1.call-start = ((), (), s32[]{:S(2)}) async-start(), calls=%async_computation.22 | async-start | bytes 2359296 | tf_op jit(solution)/shard_map/reduce_scatter | solution.py:318
  733.9 344.4 %reduce-scatter.18.cloned.1.call-start = ((), (), s32[]{:S(2)}) async-start(), calls=%async_computation.18 | async-start | bytes 5242880 | tf_op jit(solution)/shard_map/reduce_scatter | solution.py:104
  743.2 414.9 %reduce-scatter.14.cloned.1.call-start = ((), (), s32[]{:S(2)}) async-start(), calls=%async_computation.14 | async-start | bytes 5242880 | tf_op jit(solution)/shard_map/reduce_scatter | solution.py:95
  762.0 316.3 %copy-start.6 = (bf16[256,2048]{1,0:T(8,128)(2,1)S(1)}, bf16[256,2048]{1,0:T(8,128)(2,1)}, u32[]{:S(2)}) copy-start(bf16[256,2048]{1,0:T(8,128)(2,1)} %param.19) | copy-start | bytes 3145732
  762.0 316.3 %copy-start.30 = (f32[2048]{0:T(1024)S(1)}, f32[2048]{0:T(1024)}, u32[]{:S(2)}) copy-start(f32[2048]{0:T(1024)} %copy-done.29) | copy-start | bytes 24580
  762.0 316.3 %copy-start.37 = (f32[256]{0:T(256)S(1)}, f32[256]{0:T(256)}, u32[]{:S(2)}) copy-start(f32[256]{0:T(256)} %copy-done.36) | copy-start | bytes 3076
  764.9 315.4 %copy-start.33 = (f32[2048]{0:T(1024)S(1)}, f32[2048]{0:T(1024)}, u32[]{:S(2)}) copy-start(f32[2048]{0:T(1024)} %get-tuple-element.444) | copy-start | bytes 24580
  764.9 393.1 %copy-start.28 = (f32[2048]{0:T(1024)S(1)}, f32[2048]{0:T(1024)}, u32[]{:S(2)}) copy-start(f32[2048]{0:T(1024)} %copy-done.27) | copy-start | bytes 24580
  764.9 393.1 %copy-start.35 = (f32[256]{0:T(256)S(1)}, f32[256]{0:T(256)}, u32[]{:S(2)}) copy-start(f32[256]{0:T(256)} %copy-done.34) | copy-start | bytes 3076
  764.9 393.1 %copy-start.39 = (f32[256]{0:T(256)S(1)}, f32[256]{0:T(256)}, u32[]{:S(2)}) copy-start(f32[256]{0:T(256)} %copy-done.38) | copy-start | bytes 3076
  (13 other events, 14.1 us)
Sparse Core Ops, SparseCore 0:
  12.8 83.4 all-gather.4
  155.3 75.2 reduce-scatter.11
  235.0 81.2 all-gather.6
  317.8 79.2 all-gather.8
  442.8 75.2 reduce-scatter.15
  525.8 81.2 all-gather.10
  610.6 69.7 reduce-scatter.27
  684.3 71.2 reduce-scatter.29
  759.0 71.2 reduce-scatter.31
  833.7 36.0 reduce-scatter.21
  873.8 36.0 reduce-scatter.23
  913.4 41.2 reduce-scatter.19
  957.9 41.2 reduce-scatter.25
  1001.5 76.7 reduce-scatter.17
  1080.4 77.5 reduce-scatter.13
where the time goes:
time: 1180 us; the launch traced here: 1170 us
  waiting for transfers between devices  718 us (61%)
  matrix products  224 us (19%)
  local copies, waits for them, and re-layouts  99.4 us (8%)
  other arithmetic  74 us (6%)
  blocking collectives  30.6 us (3%)
  between operations  15.3 us (1%)
    reduce_scatter x2, waiting for transfers between devices, input_sum(): lax.psum_scatter(lax.dot_general(row_grads, weight_cols, (((1,), (1,)), (...  152 us
    all_gather x2, waiting for transfers between devices, spread_rows(): gathered = lax.all_gather(local_rows, 'tensor', axis=0, tiled=True)  135 us
    reduce_scatter x2, waiting for transfers between devices, branch_sum(): lax.psum_scatter(jnp.dot(source_rows, weight_rows, preferred_element_type...  121 us
    all_gather x2, waiting for transfers between devices, collect(): return lax.all_gather(grad_rows, 'tensor', axis=0, tiled=True)  81.9 us
    reduce_scatter x1, waiting for transfers between devices, shards(): lax.psum_scatter(w_down_grad.astype(jnp.bfloat16), 'dp', scatter_dimensio...  65.4 us
    reduce_scatter x1, waiting for transfers between devices, shards(): lax.psum_scatter(w_query_grad.astype(jnp.bfloat16), 'dp', scatter_dimensi...  43.1 us
    reduce_scatter x1, waiting for transfers between devices, shards(): lax.psum_scatter(w_out_grad.astype(jnp.bfloat16), 'dp', scatter_dimension...  42.8 us
    reduce_scatter x1, waiting for transfers between devices, shards(): lax.psum_scatter(w_value_grad.astype(jnp.bfloat16), 'dp', scatter_dimensi...  38.5 us
  transfers between devices with their start and end apart: 15, of which 13 were waited for; matrix products, arithmetic and copies ran while one was open for 22% of the time, Pallas kernels for 0%

commit v1 on v0

v1 whole, which is shorter than its diff:
```python
import functools
import math

import jax
import jax.numpy as jnp
from jax import lax
from jax.experimental import pallas as pl
from jax.experimental.pallas import tpu as pltpu
from jax.sharding import PartitionSpec as P

HD = 128
BLK = 128
NORM_EPS = 1e-05
ROPE_BASE = 1000000.0
SCALE = HD ** (-0.5)
SCALE2 = SCALE * math.log2(math.e)
NEG = -1e30
BF = jnp.bfloat16
F32 = jnp.float32
VMEM_LIMIT = 56 * 1024 * 1024


def mm(a, b):
    return jnp.dot(a, b, preferred_element_type=F32)


def mm_bt(a, b):
    return lax.dot_general(a, b, (((1,), (1,)), ((), ())), preferred_element_type=F32)


def mm_at(a, b):
    return lax.dot_general(a, b, (((0,), (0,)), ((), ())), preferred_element_type=F32)


def tree_tables(segment_ids, parent_ids):
    block_count = parent_ids.shape[0]
    first_ids = segment_ids.reshape(block_count, -1)[:, 0]
    block_iota = jnp.arange(block_count, dtype=jnp.int32)
    same_tree = first_ids[:, None] == first_ids[None, :]
    tree_start = jnp.min(jnp.where(same_tree, block_iota[None, :], block_count), axis=1)
    parent_block = tree_start + parent_ids
    step = (block_iota[None, :] == parent_block[:, None]) | (
        block_iota[None, :] == block_iota[:, None]
    )
    for _ in range(3):
        step = jnp.any(step[:, :, None] & step[None, :, :], axis=1)
    ancestry = step.astype(F32)
    return ancestry, jnp.sum(ancestry, axis=1) - 1.0


def rope_tables(depth):
    token_total = depth.shape[0] * BLK
    offsets = (jnp.arange(token_total, dtype=jnp.int32) % BLK).astype(F32)
    places = jnp.repeat(depth, BLK) * BLK + offsets
    freq_index = jnp.arange(HD // 2, dtype=jnp.int32).astype(F32)
    inverse_freq = ROPE_BASE ** (-2.0 * freq_index / HD)
    angles = places[:, None] * inverse_freq[None, :]
    cosine, sine = jnp.cos(angles), jnp.sin(angles)
    return jnp.concatenate([cosine, cosine], axis=1), jnp.concatenate([-sine, sine], axis=1)


def head_cols(h):
    return slice(h * HD, (h + 1) * HD)


def causal_tile(rep):
    rows = lax.broadcasted_iota(jnp.int32, (BLK, BLK), 0)
    cols = lax.broadcasted_iota(jnp.int32, (BLK, BLK), 1)
    tile = cols <= rows
    return jnp.concatenate([tile] * rep, axis=0) if rep > 1 else tile


def stack_heads(ref, rows, first, rep):
    parts = [ref[rows, head_cols(first + i)] for i in range(rep)]
    return jnp.concatenate(parts, axis=0) if rep > 1 else parts[0]


def attn_fwd_kernel(x_ref, wq_ref, wk_ref, wv_ref, cos_ref, sin_ref, bias_ref, q_ref, k_ref, v_ref, m_ref, lse_ref):
    tokens = x_ref.shape[0]
    heads = wq_ref.shape[1] // HD
    kv_heads = wk_ref.shape[1] // HD
    rep = heads // kv_heads
    for r in range(tokens // 256):
        rows = slice(r * 256, (r + 1) * 256)
        x = x_ref[rows, :]
        cosine, sine = cos_ref[rows, :], sin_ref[rows, :]
        for w_ref, out_ref, count in ((wq_ref, q_ref, heads), (wk_ref, k_ref, kv_heads)):
            raw = mm(x, w_ref[...])
            for h in range(count):
                u = raw[:, head_cols(h)]
                out_ref[rows, head_cols(h)] = (u * cosine + pltpu.roll(u, HD // 2, 1) * sine).astype(BF)
        v_ref[rows, :] = mm(x, wv_ref[...]).astype(BF)
    causal = causal_tile(rep)
    for g in range(kv_heads):
        for b in range(tokens // BLK):
            rows = slice(b * BLK, (b + 1) * BLK)
            q = stack_heads(q_ref, rows, g * rep, rep)
            s_diag = jnp.where(causal, mm_bt(q, k_ref[rows, head_cols(g)]) * SCALE2, NEG)
            top = jnp.max(s_diag, axis=1, keepdims=True)
            if b:
                past = slice(0, b * BLK)
                s_past = mm_bt(q, k_ref[past, head_cols(g)]) * SCALE2 + bias_ref[b : b + 1, past]
                top = jnp.maximum(top, jnp.max(s_past, axis=1, keepdims=True))
            e_diag = jnp.exp2(s_diag - top)
            mass = jnp.sum(e_diag, axis=1, keepdims=True)
            out = mm(e_diag.astype(BF), v_ref[rows, head_cols(g)])
            if b:
                e_past = jnp.exp2(s_past - top)
                mass = mass + jnp.sum(e_past, axis=1, keepdims=True)
                out = out + mm(e_past.astype(BF), v_ref[past, head_cols(g)])
            out = (out / mass).astype(BF)
            lse = jnp.broadcast_to(top + jnp.log2(mass), (rep * BLK, HD))
            for i in range(rep):
                m_ref[rows, head_cols(g * rep + i)] = out[i * BLK : (i + 1) * BLK]
                lse_ref[rows, head_cols(g * rep + i)] = lse[i * BLK : (i + 1) * BLK]


def attn_bwd_kernel(q_ref, k_ref, v_ref, o_ref, lse_ref, do_ref, cos_ref, sin_ref, bias_ref, d_ref, dk_acc, dv_acc):
    tokens = q_ref.shape[0]
    heads = q_ref.shape[1] // HD
    kv_heads = k_ref.shape[1] // HD
    rep = heads // kv_heads
    causal = causal_tile(rep)

    def turn_back(grad, rows):
        return (grad * cos_ref[rows, :] - pltpu.roll(grad, HD // 2, 1) * sin_ref[rows, :]).astype(BF)

    for g in range(kv_heads):
        for b in range(tokens // BLK - 1, -1, -1):
            rows = slice(b * BLK, (b + 1) * BLK)
            q = stack_heads(q_ref, rows, g * rep, rep)
            do = stack_heads(do_ref, rows, g * rep, rep)
            o = stack_heads(o_ref, rows, g * rep, rep)
            lse = stack_heads(lse_ref, rows, g * rep, rep)[:, :1]
            delta = jnp.sum(do.astype(F32) * o.astype(F32), axis=1, keepdims=True)
            k_d = k_ref[rows, head_cols(g)]
            p = jnp.where(causal, jnp.exp2(mm_bt(q, k_d) * SCALE2 - lse), 0.0)
            ds = (p * (mm_bt(do, v_ref[rows, head_cols(g)]) - delta)).astype(BF)
            dq = mm(ds, k_d)
            dk = mm_at(ds, q)
            dv = mm_at(p.astype(BF), do)
            if b < tokens // BLK - 1:
                dk = dk + dk_acc[rows, :]
                dv = dv + dv_acc[rows, :]
            d_ref[rows, head_cols(heads + g)] = turn_back(dk * SCALE, rows)
            d_ref[rows, head_cols(heads + kv_heads + g)] = dv.astype(BF)
            if b:
                past = slice(0, b * BLK)
                k_p = k_ref[past, head_cols(g)]
                p = jnp.exp2(mm_bt(q, k_p) * SCALE2 + (bias_ref[b : b + 1, past] - lse))
                ds = (p * (mm_bt(do, v_ref[past, head_cols(g)]) - delta)).astype(BF)
                dq = dq + mm(ds, k_p)
                dk = mm_at(ds, q)
                dv = mm_at(p.astype(BF), do)
                if b < tokens // BLK - 1:
                    dk = dk + dk_acc[past, :]
                    dv = dv + dv_acc[past, :]
                dk_acc[past, :] = dk
                dv_acc[past, :] = dv
            dq = dq * SCALE
            for i in range(rep):
                d_ref[rows, head_cols(g * rep + i)] = turn_back(dq[i * BLK : (i + 1) * BLK], rows)


def send(src, dst, send_sem, recv_sem, rank):
    return pltpu.make_async_remote_copy(
        src_ref=src,
        dst_ref=dst,
        send_sem=send_sem,
        recv_sem=recv_sem,
        device_id={"tensor": rank},
        device_id_type=pl.DeviceIdType.MESH,
    )


def line_barrier(t, n):
    barrier = pltpu.get_barrier_semaphore()

    @pl.when(t > 0)
    def _():
        pl.semaphore_signal(barrier, inc=1, device_id={"tensor": t - 1}, device_id_type=pl.DeviceIdType.MESH)

    @pl.when(t < n - 1)
    def _():
        pl.semaphore_signal(barrier, inc=1, device_id={"tensor": t + 1}, device_id_type=pl.DeviceIdType.MESH)

    is_end = (t == 0) | (t == n - 1)

    @pl.when(is_end)
    def _():
        pl.semaphore_wait(barrier, 1)

    @pl.when(jnp.logical_not(is_end))
    def _():
        pl.semaphore_wait(barrier, 2)


def arrival_order(t, n):
    near = jnp.minimum(t, n - 1 - t)
    order = [t]
    for i in range(1, n):
        both = t - (i + 1) // 2 if i % 2 else t + i // 2
        one_side = jnp.where(t > n - 1 - t, t - (i - near), t + (i - near))
        order.append(jnp.where(i <= 2 * near, both, one_side))
    return order


def ffn_kernel(
    n,
    own_ref,
    cot_ref,
    wg_hbm,
    wu_hbm,
    wd_hbm,
    h_out,
    gg_out,
    ug_out,
    n_out,
    fb_out,
    fi_out,
    wg_ref,
    wu_ref,
    wd_ref,
    n_buf,
    c_buf,
    h_st,
    gg_st,
    ug_st,
    fb_st,
    fi_part,
    got,
    fb_acc,
    fi_acc,
    w_sem,
    c_sem,
    st_sem,
    n_sem,
    ag_send,
    ag_recv,
    rs_send,
    rs_recv,
):
    t = lax.axis_index("tensor")
    rows, width = own_ref.shape
    units = wg_ref.shape[1]
    tile = min(512, units)
    tiles = units // tile
    parts = rs_send.shape[2]
    part_rows = rows // parts
    order = arrival_order(t, n)
    is_mid = (t > 0) & (t < n - 1)

    def load_weights(j):
        cols = pl.ds(j * tile, tile)
        return [
            pltpu.make_async_copy(wg_hbm.at[:, cols], wg_ref.at[:, cols], w_sem.at[0, j]),
            pltpu.make_async_copy(wu_hbm.at[:, cols], wu_ref.at[:, cols], w_sem.at[1, j]),
            pltpu.make_async_copy(wd_hbm.at[cols, :], wd_ref.at[cols, :], w_sem.at[2, j]),
        ]

    def load_cot(i):
        return pltpu.make_async_copy(cot_ref.at[order[i]], c_buf.at[i % 2], c_sem.at[i % 2])

    def gather(s, to_right, src=None):
        return send(
            n_buf.at[s] if src is None else src,
            n_buf.at[s],
            ag_send.at[0 if to_right else 1, s],
            ag_recv.at[s],
            t + 1 if to_right else t - 1,
        )

    def keep_rows(i):
        return pltpu.make_async_copy(own_ref if i == 0 else n_buf.at[order[i]], n_out.at[order[i]], n_sem.at[i])

    def scatter(s, c, to_right):
        d, slot = (0, s - 1) if to_right else (1, n - 2 - s)
        piece = pl.ds(c * part_rows, part_rows)
        return send(
            fi_part.at[s, piece],
            got.at[d, slot, piece],
            rs_send.at[d, slot, c],
            rs_recv.at[d, slot, c],
            t + 1 if to_right else t - 1,
        )

    for copy in load_weights(0):
        copy.start()
    load_cot(0).start()
    line_barrier(t, n)

    @pl.when(t < n - 1)
    def _():
        gather(t, True, own_ref).start()

    @pl.when(t > 0)
    def _():
        gather(t, False, own_ref).start()

    for j in range(1, tiles):
        for copy in load_weights(j):
            copy.start()
    keep_rows(0).start()

    def arrive(i):
        s = order[i]
        gather(s, True).wait_recv()

        @pl.when((s < t) & (t < n - 1))
        def _():
            gather(s, True).start()

        @pl.when((s > t) & (t > 0))
        def _():
            gather(s, False).start()

        keep_rows(i).start()

    def stage_out(i):
        slot = i % 2
        return [
            pltpu.make_async_copy(st.at[slot], out.at[order[i]], st_sem.at[k, slot])
            for k, (st, out) in enumerate(((h_st, h_out), (gg_st, gg_out), (ug_st, ug_out), (fb_st, fb_out)))
        ]

    for i in range(n):
        s = order[i]
        slot = i % 2
        if i == 1:
            arrive(1)
            if n > 2:
                pl.when(is_mid)(functools.partial(arrive, 2))
        elif i > 1:
            pl.when(jnp.logical_not(is_mid))(functools.partial(arrive, i))
        if i + 1 < n:
            load_cot(i + 1).start()
        load_cot(i).wait()
        if i >= 2:
            for copy in stage_out(i - 2):
                copy.wait()
        x_ref = own_ref if i == 0 else n_buf.at[s]
        fb_acc[...] = jnp.zeros_like(fb_acc)
        fi_acc[...] = jnp.zeros_like(fi_acc)

        def one_tile(j, carry):
            if i == 0:
                for copy in load_weights(j):
                    copy.wait()
            if 2 <= i < n - 1:
                pl.when(is_mid & (j == tiles // 2))(functools.partial(arrive, i + 1))
            cols = pl.ds(pl.multiple_of(j * tile, tile), tile)
            x = x_ref[...]
            wg, wu, wd = wg_ref[:, cols], wu_ref[:, cols], wd_ref[cols, :]
            gate = mm(x, wg)
            up = mm(x, wu)
            act_grad = mm_bt(c_buf[slot], wd)
            sig = jax.nn.sigmoid(gate)
            silu = gate * sig
            h = (silu * up).astype(BF)
            gg = (act_grad * up * (sig * (1.0 + gate * (1.0 - sig)))).astype(BF)
            ug = (act_grad * silu).astype(BF)
            h_st[slot, :, cols] = h
            gg_st[slot, :, cols] = gg
            ug_st[slot, :, cols] = ug
            for k in range(0, width, 512):
                piece = slice(k, k + 512)
                fb_acc[:, piece] += mm(h, wd_ref[cols, piece])
                fi_acc[:, piece] += mm_bt(gg, wg_ref[piece, cols]) + mm_bt(ug, wu_ref[piece, cols])
            return carry

        lax.fori_loop(0, tiles, one_tile, 0)
        fb_st[slot] = fb_acc[...].astype(BF)
        for copy in stage_out(i):
            copy.start()
        if i == 0:
            fi_out[...] = fi_acc[...]
        else:
            fi_part[s] = fi_acc[...].astype(BF)

            @pl.when(t == 0)
            def _():
                for c in range(parts):
                    scatter(i, c, True).start()

            @pl.when(t == n - 1)
            def _():
                for c in range(parts):
                    scatter(n - 1 - i, c, False).start()

    for index in range(1, n):
        for c in range(parts):
            piece = pl.ds(c * part_rows, part_rows)
            for to_right in (True, False):
                s = index if to_right else n - 1 - index
                d = 0 if to_right else 1
                has_source = t > 0 if to_right else t < n - 1
                beyond = s > t if to_right else s < t

                @pl.when(has_source & beyond)
                def _():
                    scatter(s, c, to_right).wait_recv()
                    total = fi_part[s, piece].astype(F32) + got[d, index - 1, piece].astype(F32)
                    fi_part[s, piece] = total.astype(BF)
                    scatter(s, c, to_right).start()

                @pl.when(has_source & (s == t))
                def _():
                    scatter(s, c, to_right).wait_recv()
                    fi_out[piece] += got[d, index - 1, piece].astype(F32)

    for i in range(max(0, n - 2), n):
        for copy in stage_out(i):
            copy.wait()
    for i in range(n):
        keep_rows(i).wait()
    for s in range(n):
        for to_right in (True, False):
            goes_on = t < n - 1 if to_right else t > 0

            @pl.when(goes_on & (s <= t if to_right else s >= t))
            def _():
                gather(s, to_right).wait_send()

            @pl.when(goes_on & (s > t if to_right else s < t))
            def _():
                for c in range(parts):
                    scatter(s, c, to_right).wait_send()


def ffn_call(n, own_rows, cot_all, w_gate, w_up, w_down):
    rows, width = own_rows.shape
    units = w_gate.shape[1]
    tile = min(512, units)
    tiles = units // tile
    parts = max(1, rows // 64)
    tall = jax.ShapeDtypeStruct((n, rows, units), BF)
    wide = jax.ShapeDtypeStruct((n, rows, width), BF)
    any_spec = pl.BlockSpec(memory_space=pl.ANY)
    vmem_spec = pl.BlockSpec(memory_space=pltpu.VMEM)
    dma = pltpu.SemaphoreType.DMA
    return pl.pallas_call(
        functools.partial(ffn_kernel, n),
        out_shape=[tall, tall, tall, wide, wide, jax.ShapeDtypeStruct((rows, width), F32)],
        in_specs=[vmem_spec] + [any_spec] * 4,
        out_specs=[any_spec] * 5 + [vmem_spec],
        scratch_shapes=[
            pltpu.VMEM((width, units), BF),
            pltpu.VMEM((width, units), BF),
            pltpu.VMEM((units, width), BF),
            pltpu.VMEM((n, rows, width), BF),
            pltpu.VMEM((2, rows, width), BF),
            pltpu.VMEM((2, rows, units), BF),
            pltpu.VMEM((2, rows, units), BF),
            pltpu.VMEM((2, rows, units), BF),
            pltpu.VMEM((2, rows, width), BF),
            pltpu.VMEM((n, rows, width), BF),
            pltpu.VMEM((2, n - 1, rows, width), BF),
            pltpu.VMEM((rows, width), F32),
            pltpu.VMEM((rows, width), F32),
            dma((3, tiles)),
            dma((2,)),
            dma((4, 2)),
            dma((n,)),
            dma((2, n)),
            dma((n,)),
            dma((2, n - 1, parts)),
            dma((2, n - 1, parts)),
        ],
        compiler_params=pltpu.CompilerParams(
            vmem_limit_bytes=63 * 1024 * 1024, collective_id=1, has_side_effects=True
        ),
        cost_estimate=pl.CostEstimate(
            flops=12 * n * rows * width * units, bytes_accessed=6 * width * units, transcendentals=0
        ),
        name="ffn",
    )(own_rows, cot_all, w_gate, w_up, w_down)


def full_call(kernel, out_shapes, args, scratch=(), flops=0, name=None):
    spec = pl.BlockSpec(memory_space=pltpu.VMEM)
    return pl.pallas_call(
        kernel,
        out_shape=out_shapes,
        in_specs=[spec] * len(args),
        out_specs=[spec] * len(out_shapes),
        scratch_shapes=list(scratch),
        compiler_params=pltpu.CompilerParams(vmem_limit_bytes=VMEM_LIMIT),
        cost_estimate=pl.CostEstimate(flops=flops, bytes_accessed=flops // 400, transcendentals=0),
        name=name,
    )(*args)


def normalize(rows_wide, gain_wide):
    inverse = lax.rsqrt(jnp.mean(rows_wide * rows_wide, axis=-1, keepdims=True) + NORM_EPS)
    scaled_rows = rows_wide * inverse
    return scaled_rows, inverse, (scaled_rows * gain_wide).astype(BF)


def norm_back(normed_grad, scaled_rows, inverse, gain_wide):
    weighted = normed_grad * gain_wide
    return inverse * (weighted - scaled_rows * jnp.mean(weighted * scaled_rows, axis=-1, keepdims=True))


def pairs(n, bit):
    return [(i, i ^ bit) for i in range(n)]


def pick(array, index, axis):
    return lax.dynamic_index_in_dim(array, index, axis, keepdims=False)


def dp_scatter(give, keep, n_dp):
    me = lax.axis_index("dp")
    total = keep + lax.ppermute(give, "dp", pairs(n_dp, 1))
    if n_dp != 8:
        bit = 2
        while total.shape[0] > 1:
            parts = total.reshape(-1, 2, *total.shape[1:])
            mine = (me // bit) % 2
            total = pick(parts, mine, 1) + lax.ppermute(pick(parts, 1 - mine, 1), "dp", pairs(n_dp, bit))
            bit *= 2
        return total[0].astype(F32)
    x, y = (me // 2) % 2, me // 4
    cols = total.shape[-1] // 2
    parts = total.reshape(2, 2, *total.shape[1:])
    a, b = parts[..., :cols], parts[..., cols:]
    got_a = lax.ppermute(pick(a, 1 - x, 1), "dp", pairs(n_dp, 2))
    got_b = lax.ppermute(pick(b, 1 - y, 0), "dp", pairs(n_dp, 4))
    a = pick(a, x, 1) + got_a
    b = pick(b, y, 0) + got_b
    got_a = lax.ppermute(pick(a, 1 - y, 0), "dp", pairs(n_dp, 4))
    got_b = lax.ppermute(pick(b, 1 - x, 0), "dp", pairs(n_dp, 2))
    a = pick(a, y, 0).astype(F32) + got_a.astype(F32)
    b = pick(b, x, 0).astype(F32) + got_b.astype(F32)
    return jnp.concatenate([a, b], axis=-1)


def core_split(rows, n_dp):
    tokens, width = rows.shape
    core = lax.axis_index("dp") % 2
    parts = rows.reshape(tokens, n_dp // 2, 2, width // n_dp)
    return [pick(parts, c, 2).reshape(tokens, width // 2) for c in (1 - core, core)]


def grad_scatter(split_rows, cols, n_dp):
    give, keep = [
        mm_at(part, cols).astype(BF).reshape(n_dp // 2, 2 * part.shape[1] // n_dp, cols.shape[1])
        for part in split_rows
    ]
    return dp_scatter(give, keep, n_dp)


def after(value, *others):
    return lax.optimization_barrier((value, *others))[0]


def shards(n_dp, n_t, hidden_in, gain_attn, w_query, w_key, w_value, w_out, gain_ffn, w_gate, w_up, w_down, segments, parents, cotangent):
    tokens = segments.shape[0]
    own, width = hidden_in.shape
    q_cols, kv_cols, units = w_query.shape[1], w_key.shape[1], w_gate.shape[1]
    heads = q_cols // HD
    me_t = lax.axis_index("tensor")
    me_dp = lax.axis_index("dp")
    gain_attn_wide = gain_attn.astype(F32)
    gain_ffn_wide = gain_ffn.astype(F32)

    def ring(value, shift):
        return lax.ppermute(value, "tensor", [(i, (i + shift) % n_t) for i in range(n_t)])

    rows_wide = hidden_in.astype(F32)
    scaled_attn, inverse_attn, normed_attn = normalize(rows_wide, gain_attn_wide)
    x_all = lax.all_gather(normed_attn, "tensor", axis=0, tiled=True)

    share = q_cols // n_dp
    w_share = lax.dynamic_slice_in_dim(w_out, me_dp * share, share, 0)
    w_share = jnp.stack([ring(w_share, d) for d in range(1, n_t)])
    w_rest = lax.all_gather(after(w_share, x_all), "dp", axis=1, tiled=True)
    cot_all = lax.all_gather(after(cotangent, w_rest), "tensor", axis=0, tiled=True)

    ancestry, depth = tree_tables(segments, parents)
    cosine, sine = rope_tables(depth)
    bias = jnp.where(jnp.repeat(ancestry, BLK, axis=1) > 0.5, 0.0, NEG)

    queries, keys, values, mixed, lse = full_call(
        attn_fwd_kernel,
        [
            jax.ShapeDtypeStruct((tokens, q_cols), BF),
            jax.ShapeDtypeStruct((tokens, kv_cols), BF),
            jax.ShapeDtypeStruct((tokens, kv_cols), BF),
            jax.ShapeDtypeStruct((tokens, q_cols), BF),
            jax.ShapeDtypeStruct((tokens, q_cols), F32),
        ],
        (x_all, w_query, w_key, w_value, cosine, sine, bias),
        flops=2 * tokens * width * (q_cols + 2 * kv_cols) + 4 * heads * tokens * tokens * HD,
        name="attn_fwd",
    )

    mixed_blocks = mixed.reshape(n_t, own, q_cols)
    mixed_own = [pick(mixed_blocks, me_t, 0)] + [
        ring(pick(mixed_blocks, (me_t + d) % n_t, 0), d) for d in range(1, n_t)
    ]
    w_rest = w_rest.reshape(n_t - 1, q_cols, width)
    w_pieces = [w_out] + [w_rest[d] for d in range(n_t - 1)]
    branch = mm(mixed_own[0], w_pieces[0])
    for d in range(1, n_t):
        branch = branch + mm(mixed_own[d], w_pieces[d])
    middle = rows_wide + branch
    scaled_ffn, inverse_ffn, normed_ffn = normalize(middle, gain_ffn_wide)

    h_all, gg_all, ug_all, n_all, fb_part, ffn_in_grad = ffn_call(
        n_t, normed_ffn, cot_all.reshape(n_t, own, width), w_gate, w_up, w_down
    )
    h_all, gg_all, ug_all = [a.reshape(tokens, units) for a in (h_all, gg_all, ug_all)]
    n_all = n_all.reshape(tokens, width)
    fb_sum = lax.psum_scatter(fb_part.reshape(tokens, width), "tensor", scatter_dimension=0, tiled=True)
    output = (middle + fb_sum.astype(F32)).astype(BF)

    cot_split = core_split(cot_all.reshape(tokens, width), n_dp)
    normed_split = core_split(n_all, n_dp)
    w_down_grad = grad_scatter(cot_split, h_all, n_dp).T
    w_gate_grad = grad_scatter(normed_split, gg_all, n_dp)
    w_up_grad = grad_scatter(normed_split, ug_all, n_dp)

    middle_grad = cotangent.astype(F32) + norm_back(ffn_in_grad, scaled_ffn, inverse_ffn, gain_ffn_wide)
    branch_grad = middle_grad.astype(BF)
    mixed_grads = [mm_bt(branch_grad, w_pieces[d]).astype(BF) for d in range(n_t)]
    mixed_grads = [mixed_grads[0]] + [ring(mixed_grads[d], n_t - d) for d in range(1, n_t)]
    mixed_grad = jnp.roll(jnp.concatenate(mixed_grads, axis=0), me_t * own, axis=0)

    (project_grad,) = full_call(
        attn_bwd_kernel,
        [jax.ShapeDtypeStruct((tokens, q_cols + 2 * kv_cols), BF)],
        (queries, keys, values, mixed, lse, mixed_grad, cosine, sine, bias),
        scratch=[pltpu.VMEM((tokens, HD), F32)] * 2,
        flops=10 * heads * tokens * tokens * HD,
        name="attn_bwd",
    )
    dq, dk, dv = (
        project_grad[:, :q_cols],
        project_grad[:, q_cols : q_cols + kv_cols],
        project_grad[:, q_cols + kv_cols :],
    )
    w_project = jnp.concatenate([w_query, w_key, w_value], axis=1)
    attn_in_part = mm_bt(project_grad, w_project).astype(BF)
    attn_in_grad = lax.psum_scatter(attn_in_part, "tensor", scatter_dimension=0, tiled=True).astype(F32)

    mixed_wide = jnp.concatenate(mixed_own, axis=1)
    out_grad = grad_scatter(core_split(branch_grad, n_dp), mixed_wide, n_dp)
    out_parts = out_grad.reshape(-1, n_t, q_cols)
    w_out_grad = out_parts[:, 0]
    for d in range(1, n_t):
        w_out_grad = w_out_grad + ring(out_parts[:, d].astype(BF), n_t - d).astype(F32)
    w_out_grad = w_out_grad.T

    project_wgrad = grad_scatter(core_split(x_all, n_dp), project_grad, n_dp)
    w_query_grad = project_wgrad[:, :q_cols]
    w_key_grad = project_wgrad[:, q_cols : q_cols + kv_cols]
    w_value_grad = project_wgrad[:, q_cols + kv_cols :]

    def own_rows(array):
        return lax.dynamic_slice_in_dim(array, me_dp * (width // n_dp), width // n_dp, 0).astype(F32)

    gain_sums = jnp.stack(
        [
            jnp.sum(own_rows(w_project) * project_wgrad, axis=1),
            jnp.sum(own_rows(w_gate) * w_gate_grad, axis=1) + jnp.sum(own_rows(w_up) * w_up_grad, axis=1),
        ]
    )
    bit = 1
    while bit < n_t:
        gain_sums = gain_sums + lax.ppermute(gain_sums, "tensor", pairs(n_t, bit))
        bit *= 2
    gain_attn_grad = gain_sums[0] / own_rows(gain_attn)
    gain_ffn_grad = gain_sums[1] / own_rows(gain_ffn)

    input_grad = (middle_grad + norm_back(attn_in_grad, scaled_attn, inverse_attn, gain_attn_wide)).astype(BF)
    return (
        output,
        input_grad,
        gain_attn_grad,
        w_query_grad,
        w_key_grad,
        w_value_grad,
        w_out_grad,
        gain_ffn_grad,
        w_gate_grad,
        w_up_grad,
        w_down_grad,
    )


def solution(mesh):
    return jax.shard_map(
        functools.partial(shards, mesh.shape["dp"], mesh.shape["tensor"]),
        mesh=mesh,
        in_specs=(
            P(("dp", "tensor"), None),
            P(),
            P(None, "tensor"),
            P(None, "tensor"),
            P(None, "tensor"),
            P("tensor", None),
            P(),
            P(None, "tensor"),
            P(None, "tensor"),
            P("tensor", None),
            P("dp"),
            P("dp"),
            P(("dp", "tensor"), None),
        ),
        out_specs=(
            P(("dp", "tensor"), None),
            P(("dp", "tensor"), None),
            P("dp"),
            P("dp", "tensor"),
            P("dp", "tensor"),
            P("dp", "tensor"),
            P("tensor", "dp"),
            P("dp"),
            P("dp", "tensor"),
            P("dp", "tensor"),
            P("tensor", "dp"),
        ),
        check_vma=False,
    )
```

time: 1180 us -> 812 us (0.69)
  waiting for transfers between devices: 718 us -> 238 us
  Pallas kernels: 0 us -> 211 us
  matrix products: 224 us -> 76.7 us
  starting transfers between devices: 0.99 us -> 49.2 us
  local copies, waits for them, and re-layouts: 99.4 us -> 145 us
  blocking collectives: 30.6 us -> 0 us
    reduce_scatter x11 -> x2, waiting for transfers between devices: 500 us -> 0.02 us  [the longest x1 0.02 us: shards(): lax.psum_scatter(fb_part.reshape(tokens, width), 'tensor', scatter_dimens...]
    pallas_call x0 -> x3, Pallas kernels: none -> 211 us  [the longest x1 180 us: ffn_call(): pl.pallas_call(functools.partial(ffn_kernel, n), out_shape=[tall, tall, t...]
    dot_general x33 -> x19, matrix products: 224 us -> 76.7 us  [the longest x10 51.7 us: mm_at(): lax.dot_general(a, b, (((0,), (0,)), ((), ())), preferred_element_type=F32)]
    ppermute x0 -> x39, waiting for transfers between devices: none -> 126 us  [the longest x12 47.4 us: ring(): lax.ppermute(value, 'tensor', [(i, (i + shift) % n_t) for i in range(n_t)])]
    all_gather x4 -> x3, waiting for transfers between devices: 217 us -> 112 us  [the longest x1 50.3 us: shards(): x_all = lax.all_gather(normed_attn, 'tensor', axis=0, tiled=True)]
    ppermute x0 -> x39, starting transfers between devices: none -> 49 us  [the longest x12 19.3 us: ring(): lax.ppermute(value, 'tensor', [(i, (i + shift) % n_t) for i in range(n_t)])]
    dynamic_slice x4 -> x14, local copies, waits for them, and re-layouts: 2.53 us -> 40.6 us  [the longest x12 37.3 us: pick(): return lax.dynamic_index_in_dim(array, index, axis, keepdims=False)]
    unnamed x79 -> x144, local copies, waits for them, and re-layouts: 26.8 us -> 63.6 us
  transfers between devices with their start and end apart: 15 -> 44, of which waited for: 13 -> 17; matrix products, arithmetic and copies ran while one was open for 22% -> 30% of each run, Pallas kernels for 0% -> 2%
where the time goes in v1:
time: 812 us; the launch traced here: 799 us
  waiting for transfers between devices  238 us (29%)
  Pallas kernels  211 us (26%)
  local copies, waits for them, and re-layouts  145 us (18%)
  matrix products  76.7 us (9%)
  other arithmetic  64.3 us (8%)
  starting transfers between devices  49.2 us (6%)
  between operations  15.3 us (2%)
    pallas_call x1, Pallas kernels, ffn_call(): pl.pallas_call(functools.partial(ffn_kernel, n), out_shape=[tall, tall, t...  180 us
    unnamed x144, local copies, waits for them, and re-layouts  63.6 us
    dot_general x10, matrix products, mm_at(): lax.dot_general(a, b, (((0,), (0,)), ((), ())), preferred_element_type=F32)  51.7 us
    all_gather x1, waiting for transfers between devices, shards(): x_all = lax.all_gather(normed_attn, 'tensor', axis=0, tiled=True)  50.3 us
    all_gather x1, waiting for transfers between devices, shards(): w_rest = lax.all_gather(after(w_share, x_all), 'dp', axis=1, tiled=True)  48.8 us
    ppermute x12, waiting for transfers between devices, ring(): lax.ppermute(value, 'tensor', [(i, (i + shift) % n_t) for i in range(n_t)])  47.4 us
    ppermute x5, waiting for transfers between devices, dp_scatter(): got_b = lax.ppermute(pick(b, 1 - y, 0), 'dp', pairs(n_dp, 4))  37.3 us
    dynamic_slice x12, local copies, waits for them, and re-layouts, pick(): return lax.dynamic_index_in_dim(array, index, axis, keepdims=False)  37.3 us
  transfers between devices with their start and end apart: 44, of which 17 were waited for; matrix products, arithmetic and copies ran while one was open for 30% of the time, Pallas kernels for 2%

profile of v1, /device:TPU:0, one launch (start us, length us, event | category | flops | bytes accessed | tf_op | source)
XLA Modules:
  0.0 799.0 jit_solution(8023509636051369223)
XLA Ops:
  10.0 2.5 fusion.4
  13.7 5.1 collective-permute-start.3
  19.8 6.9 collective-permute-done.3
  26.7 31.3 %collective-permute-done.2 = bf16[64,2048]{1,0:T(8,128)(2,1)S(1)} collective-permute-done((bf16[64,2048]{1,0:T(8,128)(2,1)S(1)}, bf16[64,2048]{1,0:T(8,128)(2,1)S(1)}, u32[]{:S(2)}, u32[]{:S(2)}) %collective-permute-start.2) | collective-permute-done | bytes 262176 | tf_op jit(solution)/shard_map/ppermute | solution.py:568
  59.0 50.3 %all-gather.4.cloned.1.call-done.x_ref = bf16[1024,2048]{1,0:T(8,128)(2,1)} async-done(((bf16[256,2048]{1,0:T(8,128)(2,1)}), bf16[1024,2048]{1,0:T(8,128)(2,1)}) %all-gather.4.cloned.1.call-update) | async-done | bytes 4194320 | tf_op jit(solution)/shard_map/all_gather | solution.py:572
  109.6 48.8 %all-gather.6.cloned.1.call-done = bf16[3,512,2048]{2,1,0:T(8,128)(2,1)} async-done(((bf16[3,64,2048]{2,1,0:T(8,128)(2,1)}), bf16[3,512,2048]{2,1,0:T(8,128)(2,1)}) %all-gather.6.cloned.1.call-update) | async-done | bytes 6291472 | tf_op jit(solution)/shard_map/all_gather | solution.py:577
  168.8 15.9 %attn_fwd.1 = (bf16[1024,512]{1,0:T(8,128)(2,1)}, bf16[1024,256]{1,0:T(8,128)(2,1)}, bf16[1024,256]{1,0:T(8,128)(2,1)}, bf16[1024,512]{1,0:T(8,128)(2,1)}, f32[1024,512]{1,0:T(8,128)}) custom-call(bf16[1024,2048]{1,0:T(8,128)(2,1)} %all-gather.4.cloned.1.call-done.x_ref, bf16[2048,512]{1,0:T(8,128)(2,1)} %wq_ref.1, bf16[2048,256]{1,0:T(8,128)(2,1)} %wk_ref.1, ...), custom_call_target="tpu_custom_call" | custom-call | flops 6442450944 | bytes 16106127 | tf_op jit(solution)/shard_map/attn_fwd/pallas_call | solution.py:481
  184.7 2.1 dynamic-slice_bitcast_fusion.17
  186.8 3.3 collective-permute-start.5
  191.5 7.8 reshape.296
  199.3 11.2 %constant_dynamic-slice_fusion.14 = (bf16[1024,4,1,256]{3,2,1,0:T(2,128)(2,1)}, bf16[1024,4,1,256]{3,2,1,0:T(2,128)(2,1)}) fusion(bf16[1024,4,2,256]{3,2,1,0:T(2,128)(2,1)} %reshape.296, s32[]{:T(128)S(6)} %select_n.192, s32[]{:T(128)S(6)} %select_n.191), kind=kLoop, calls=%fused_computation.136 | loop fusion | bytes 8388616 | tf_op jit(solution)/shard_map/jit(dynamic_index_in_dim)/dynamic_slice | solution.py:509
  210.6 10.5 %copy.71 = bf16[1024,4,1,256]{0,3,1,2:T(8,128)(2,1)} copy(bf16[1024,4,1,256]{3,2,1,0:T(2,128)(2,1)} %get-tuple-element.48) | data formatting | bytes 4194304
  221.1 10.7 %copy.72 = bf16[1024,4,1,256]{0,3,1,2:T(8,128)(2,1)} copy(bf16[1024,4,1,256]{3,2,1,0:T(2,128)(2,1)} %get-tuple-element.47) | data formatting | bytes 4194304
  231.8 2.4 fusion.42
  234.3 2.4 convolution_add_fusion.1
  237.5 9.2 %collective-permute-done.4 = bf16[256,512]{1,0:T(8,128)(2,1)S(1)} collective-permute-done((bf16[256,512]{1,0:T(8,128)(2,1)S(1)}, bf16[256,512]{1,0:T(8,128)(2,1)S(1)}, u32[]{:S(2)}, u32[]{:S(2)}) %collective-permute-start.4) | collective-permute-done | bytes 262176 | tf_op jit(solution)/shard_map/ppermute | solution.py:568
  250.3 13.0 %all-gather.8.cloned.1.call-done = bf16[1024,2048]{0,1:T(8,128)(2,1)} async-done(((bf16[256,2048]{0,1:T(8,128)(2,1)}), bf16[1024,2048]{0,1:T(8,128)(2,1)}) %all-gather.8.cloned.1.call-update) | async-done | bytes 4194320 | tf_op jit(solution)/shard_map/all_gather | solution.py:578
  263.2 6.4 copy.58
  269.7 179.7 %ffn.1 = (bf16[4,256,2048]{2,1,0:T(8,128)(2,1)}, bf16[4,256,2048]{2,1,0:T(8,128)(2,1)}, bf16[4,256,2048]{2,1,0:T(8,128)(2,1)}, bf16[4,256,2048]{2,1,0:T(8,128)(2...) custom-call(bf16[256,2048]{1,0:T(8,128)(2,1)} %multiply_convert_fusion.own_ref, bf16[4,256,2048]{2,1,0:T(8,128)(2,1)} %bitcast.222, ...), custom_call_target="tpu_custom_call" | custom-call | flops 51539607552 | bytes 25165824 | tf_op jit(solution)/shard_map/ffn/pallas_call | solution.py:441
  449.4 2.8 multiply_reduce_fusion.2
  454.8 2.3 fusion.17
  457.2 2.3 fusion.16
  460.6 2.3 fusion.15
  465.8 8.0 reshape_reshape.3
  478.9 2.3 constant_dynamic-slice_fusion.16.do_ref
  481.2 15.1 %attn_bwd.1 = bf16[1024,1024]{1,0:T(8,128)(2,1)} custom-call(bf16[1024,512]{1,0:T(8,128)(2,1)} %get-tuple-element.29.q_ref, bf16[1024,256]{1,0:T(8,128)(2,1)} %get-tuple-element.30.k_ref, bf16[1024,256]{1,0:T(8,128)(2,1)} %get-tuple-element.31.v_ref, bf16[1024,512]{1,0:T(8,128)(2,1)} %get-tuple-element.24.o_ref, f32[1024,512]{1,0:T(8,128)} %get-tuple-element.32.lse_ref, ...), custom_call_target="tpu_custom_call" | custom-call | flops 5368709120 | bytes 13421772 | tf_op jit(solution)/shard_map/attn_bwd/pallas_call | solution.py:481
  496.3 9.8 %convolution_convert_fusion.8 = bf16[1024,2048]{1,0:T(8,128)(2,1)} fusion(bf16[1024,1024]{1,0:T(8,128)(2,1)} %attn_bwd.1, bf16[2048,1024]{1,0:T(8,128)(2,1)} %constant_dynamic-update-slice_fusion.8), kind=kOutput, calls=%fused_computation.8 | convolution fusion | flops 4297064448 | bytes 10485760 | tf_op jit(solution)/shard_map/dot_general | solution.py:28
  506.1 11.3 %constant_dynamic-slice_fusion.12 = (bf16[1024,4,1,256]{3,2,1,0:T(2,128)(2,1)}, bf16[1024,4,1,256]{3,2,1,0:T(2,128)(2,1)}) fusion(bf16[1024,4,2,256]{3,2,1,0:T(2,128)(2,1)} %reshape_reshape.3, s32[]{:T(128)S(6)} %select_n.192, s32[]{:T(128)S(6)} %select_n.191), kind=kLoop, calls=%fused_computation.134 | loop fusion | bytes 8388616 | tf_op jit(solution)/shard_map/jit(dynamic_index_in_dim)/dynamic_slice | solution.py:509
  518.3 10.5 %copy.73 = bf16[1024,4,1,256]{0,3,1,2:T(8,128)(2,1)} copy(bf16[1024,4,1,256]{3,2,1,0:T(2,128)(2,1)} %get-tuple-element.54) | data formatting | bytes 4194304
  528.8 9.0 %copy.74 = bf16[1024,4,1,256]{0,3,1,2:T(8,128)(2,1)S(1)} copy(bf16[1024,4,1,256]{3,2,1,0:T(2,128)(2,1)} %get-tuple-element.53) | data formatting | bytes 4194304
  537.8 8.4 %convolution_convert_fusion.6 = bf16[1024,2048]{1,0:T(8,128)(2,1)} fusion(bf16[1024,1024]{0,1:T(8,128)(2,1)S(1)} %bitcast.230, bf16[1024,2048]{1,0:T(8,128)(2,1)} %bitcast.255), kind=kOutput, calls=%fused_computation.6 | convolution fusion | flops 4297064448 | bytes 10485760 | tf_op jit(solution)/shard_map/dot_general | solution.py:32
  546.2 6.1 convolution_convert_fusion.4
  552.8 2.2 constant_dynamic-slice_fusion.10
  556.1 9.5 %convolution_convert_fusion.7 = bf16[1024,2048]{1,0:T(8,128)(2,1)} fusion(bf16[1024,1024]{0,1:T(8,128)(2,1)} %bitcast.226, bf16[1024,2048]{1,0:T(8,128)(2,1)} %bitcast.256), kind=kOutput, calls=%fused_computation.7 | convolution fusion | flops 4297064448 | bytes 10485760 | tf_op jit(solution)/shard_map/dot_general | solution.py:32
  565.6 2.3 convolution_convert_fusion.9
  568.1 3.2 convolution_convert_fusion
  574.6 6.1 convolution_convert_fusion.5
  580.7 2.3 convolution_convert_fusion.10
  586.3 6.5 convolution_convert_fusion.2
  593.6 4.7 collective-permute-done.12
  599.7 6.1 convolution_convert_fusion.3
  605.7 2.0 copy.75
  609.0 2.5 collective-permute-done.10
  614.2 3.7 collective-permute-done.13
  620.8 3.6 collective-permute-done.11
  626.7 4.1 add.342
  636.6 4.1 add.347
  645.9 4.1 add.356
  654.1 5.4 add.364
  664.3 2.3 copy.66
  667.9 2.8 constant_dynamic-slice_fusion.1
  670.7 2.2 copy.82
  689.0 14.9 %collective-permute-done.29 = bf16[2,256,1024]{1,2,0:T(8,128)(2,1)} collective-permute-done((bf16[2,256,1024]{1,2,0:T(8,128)(2,1)}, bf16[2,256,1024]{1,2,0:T(8,128)(2,1)}, u32[]{:S(2)}, u32[]{:S(2)}) %collective-permute-start.29) | collective-permute-done | bytes 1048608 | tf_op jit(solution)/shard_map/ppermute | solution.py:528
  708.6 17.7 %collective-permute-done.37 = bf16[2,256,1024]{1,2,0:T(8,128)(2,1)S(1)} collective-permute-done((bf16[2,256,1024]{1,2,0:T(8,128)(2,1)S(1)}, bf16[2,256,1024]{1,2,0:T(8,128)(2,1)S(1)}, u32[]{:S(2)}, u32[]{:S(2)}) %collective-permute-start.37) | collective-permute-done | bytes 1048608 | tf_op jit(solution)/shard_map/ppermute | solution.py:528
  729.8 8.7 %collective-permute-done.18 = bf16[256,1024]{1,0:T(8,128)(2,1)S(1)} collective-permute-done((bf16[256,1024]{1,0:T(8,128)(2,1)S(1)}, bf16[256,1024]{1,0:T(8,128)(2,1)S(1)}, u32[]{:S(2)}, u32[]{:S(2)}) %collective-permute-start.18) | collective-permute-done | bytes 524320 | tf_op jit(solution)/shard_map/ppermute | solution.py:532
  741.4 2.8 multiply_reduce_fusion.1
  744.2 5.5 collective-permute-done.23
  751.7 2.8 multiply_reduce_fusion
  755.8 5.1 collective-permute-done.30
  762.9 2.0 collective-permute-start.32
  764.9 3.9 collective-permute-done.38
  768.8 2.7 collective-permute-start.31
  773.7 8.1 %collective-permute-done.25 = f32[2,256]{1,0:T(2,128)S(1)} collective-permute-done((f32[2,256]{1,0:T(2,128)S(1)}, f32[2,256]{1,0:T(2,128)S(1)}, u32[]{:S(2)}, u32[]{:S(2)}) %collective-permute-start.25) | collective-permute-done | bytes 2080 | tf_op jit(solution)/shard_map/ppermute | solution.py:671
  787.3 5.0 fusion.9
  (309 shorter events, 115.1 us)
Async XLA Ops:
  7.2 102.0 %all-gather.4.cloned.1.call-start = ((), (), s32[]{:S(2)}) async-start(), calls=%async_computation.2 | async-start | bytes 5242880 | tf_op jit(solution)/shard_map/all_gather | solution.py:572
  12.5 96.8 %copy-start.55 = (s32[1024]{0:T(1024)S(1)}, s32[1024]{0:T(1024)}, u32[]{:S(2)}) copy-start(s32[1024]{0:T(1024)} %param.23) | copy-start | bytes 12292
  12.5 97.1 %copy-start.56 = (s32[8]{0:T(128)S(1)}, s32[8]{0:T(128)}, u32[]{:S(2)}) copy-start(s32[8]{0:T(128)} %param.24) | copy-start | bytes 100
  12.5 145.9 %copy-start.7 = (bf16[256,2048]{1,0:T(8,128)(2,1)S(1)}, bf16[256,2048]{1,0:T(8,128)(2,1)}, u32[]{:S(2)}) copy-start(bf16[256,2048]{1,0:T(8,128)(2,1)} %param.25) | copy-start | bytes 3145732
  12.6 145.8 %all-gather.6.cloned.1.call-start = ((), (), s32[]{:S(2)}) async-start(), calls=%async_computation.3 | async-start | bytes 7077888 | tf_op jit(solution)/shard_map/all_gather | solution.py:577
  13.7 13.0 %collective-permute-start.3 = (bf16[64,2048]{1,0:T(8,128)(2,1)S(1)}, bf16[64,2048]{1,0:T(8,128)(2,1)S(1)}, u32[]{:S(2)}, u32[]{:S(2)}) collective-permute-start(bf16[64,2048]{1,0:T(8,128)(2,1)S(1)} %constant_dynamic-slice_fusion.17), channel_id=1, source_target_pairs={{0,3},{1,0},{2,1},{3,2},{4,7},{5,4},{6,5},{7,6},{8,11},{9,8},{10,9... | collective-permute-start | bytes 786440 | tf_op jit(solution)/shard_map/ppermute | solution.py:568
  18.8 39.2 %collective-permute-start.2 = (bf16[64,2048]{1,0:T(8,128)(2,1)S(1)}, bf16[64,2048]{1,0:T(8,128)(2,1)S(1)}, u32[]{:S(2)}, u32[]{:S(2)}) collective-permute-start(bf16[64,2048]{1,0:T(8,128)(2,1)S(1)} %constant_dynamic-slice_fusion.17), channel_id=1, source_target_pairs={{0,2},{1,3},{2,0},{3,1},{4,6},{5,7},{6,4},{7,5},{8,10},{9,11},{10,... | collective-permute-start | bytes 786440 | tf_op jit(solution)/shard_map/ppermute | solution.py:568
  18.8 39.2 %collective-permute-start.1 = (bf16[64,2048]{1,0:T(8,128)(2,1)S(1)}, bf16[64,2048]{1,0:T(8,128)(2,1)S(1)}, u32[]{:S(2)}, u32[]{:S(2)}) collective-permute-start(bf16[64,2048]{1,0:T(8,128)(2,1)S(1)} %constant_dynamic-slice_fusion.17), channel_id=1, source_target_pairs={{0,1},{1,2},{2,3},{3,0},{4,5},{5,6},{6,7},{7,4},{8,9},{9,10},{10,1... | collective-permute-start | bytes 786440 | tf_op jit(solution)/shard_map/ppermute | solution.py:568
  59.0 101.4 %copy-start.54 = (bf16[2048]{0:T(1024)(128)(2,1)S(1)}, bf16[2048]{0:T(1024)(128)(2,1)}, u32[]{:S(2)}) copy-start(bf16[2048]{0:T(1024)(128)(2,1)} %param.19) | copy-start | bytes 12292
  109.2 154.0 %all-gather.8.cloned.1.call-start = ((), (), s32[]{:S(2)}) async-start(), calls=%async_computation.4 | async-start | bytes 5242880 | tf_op jit(solution)/shard_map/all_gather | solution.py:578
  159.7 625.7 %reduce-scatter.5.cloned.1.call-start = ((), (), s32[]{:S(2)}) async-start(), calls=%async_computation.6 | async-start | bytes 5242880 | tf_op jit(solution)/shard_map/reduce_scatter | solution.py:645
  160.4 291.8 %copy-start.44 = (f32[2048]{0:T(1024)}, f32[2048]{0:T(1024)S(1)}, u32[]{:S(2)}) copy-start(f32[2048]{0:T(1024)S(1)} %convert_element_type.227) | copy-start | bytes 24580
  186.8 49.9 %collective-permute-start.5 = (bf16[256,512]{1,0:T(8,128)(2,1)}, bf16[256,512]{1,0:T(8,128)(2,1)S(1)}, u32[]{:S(2)}, u32[]{:S(2)}) collective-permute-start(bf16[256,512]{1,0:T(8,128)(2,1)} %get-tuple-element.73), channel_id=1, source_target_pairs={{0,3},{1,0},{2,1},{3,2},{4,7},{5,4},{6,5},{7,6},{8,11},{9,8},{10,9... | collective-permute-start | bytes 786440 | tf_op jit(solution)/shard_map/ppermute | solution.py:568
  190.1 44.1 %collective-permute-start = (bf16[256,512]{1,0:T(8,128)(2,1)}, bf16[256,512]{1,0:T(8,128)(2,1)S(1)}, u32[]{:S(2)}, u32[]{:S(2)}) collective-permute-start(bf16[256,512]{1,0:T(8,128)(2,1)} %get-tuple-element.74), channel_id=1, source_target_pairs={{0,1},{1,2},{2,3},{3,0},{4,5},{5,6},{6,7},{7,4},{8,9},{9,10},{10,1... | collective-permute-start | bytes 786440 | tf_op jit(solution)/shard_map/ppermute | solution.py:568
  190.4 56.3 %collective-permute-start.4 = (bf16[256,512]{1,0:T(8,128)(2,1)S(1)}, bf16[256,512]{1,0:T(8,128)(2,1)S(1)}, u32[]{:S(2)}, u32[]{:S(2)}) collective-permute-start(bf16[256,512]{1,0:T(8,128)(2,1)S(1)} %get-tuple-element.72), channel_id=1, source_target_pairs={{0,2},{1,3},{2,0},{3,1},{4,6},{5,7},{6,4},{7,5},{8,10},{9,11},{10,... | collective-permute-start | bytes 786440 | tf_op jit(solution)/shard_map/ppermute | solution.py:568
  221.1 15.7 %slice-start = ((s8[6291456]{0:T(1024)(128)(4,1)}), s8[2097152]{0:T(1024)(128)(4,1)S(1)}, s32[]{:S(2)}) async-start(s8[6291456]{0:T(1024)(128)(4,1)} %bitcast.215), calls=%async_computation.7 | async-start | bytes 4194304
  247.7 204.5 %copy-start.48 = (f32[256]{0:T(256)}, f32[256]{0:T(256)S(1)}, u32[]{:S(2)}) copy-start(f32[256]{0:T(256)S(1)} %add_rsqrt_fusion) | copy-start | bytes 3076
  457.2 16.6 %collective-permute-start.6 = (bf16[256,512]{1,0:T(8,128)(2,1)S(1)}, bf16[256,512]{1,0:T(8,128)(2,1)S(1)}, u32[]{:S(2)}, u32[]{:S(2)}) collective-permute-start(bf16[256,512]{1,0:T(8,128)(2,1)S(1)} %fusion.17), channel_id=1, source_target_pairs={{0,3},{1,0},{2,1},{3,2},{4,7},{5,4},{6,5},{7,6},{8,11},{9,8},{10,9... | collective-permute-start | bytes 786440 | tf_op jit(solution)/shard_map/ppermute | solution.py:568
  459.6 14.9 %collective-permute-start.7 = (bf16[256,512]{1,0:T(8,128)(2,1)S(1)}, bf16[256,512]{1,0:T(8,128)(2,1)S(1)}, u32[]{:S(2)}, u32[]{:S(2)}) collective-permute-start(bf16[256,512]{1,0:T(8,128)(2,1)S(1)} %fusion.16), channel_id=1, source_target_pairs={{0,2},{1,3},{2,0},{3,1},{4,6},{5,7},{6,4},{7,5},{8,10},{9,11},{10,... | collective-permute-start | bytes 786440 | tf_op jit(solution)/shard_map/ppermute | solution.py:568
  462.9 12.3 %collective-permute-start.8 = (bf16[256,512]{1,0:T(8,128)(2,1)S(1)}, bf16[256,512]{1,0:T(8,128)(2,1)S(1)}, u32[]{:S(2)}, u32[]{:S(2)}) collective-permute-start(bf16[256,512]{1,0:T(8,128)(2,1)S(1)} %fusion.15), channel_id=1, source_target_pairs={{0,1},{1,2},{2,3},{3,0},{4,5},{5,6},{6,7},{7,4},{8,9},{9,10},{10,1... | collective-permute-start | bytes 786440 | tf_op jit(solution)/shard_map/ppermute | solution.py:568
  506.1 281.2 %reduce-scatter.3.cloned.1.call-start = ((), (), s32[]{:S(2)}) async-start(), calls=%async_computation.5 | async-start | bytes 5242880 | tf_op jit(solution)/shard_map/reduce_scatter | solution.py:615
  546.2 80.5 %collective-permute-start.14 = (bf16[4,256,2048]{2,1,0:T(8,128)(2,1)}, bf16[4,256,2048]{2,1,0:T(8,128)(2,1)}, u32[]{:S(2)}, u32[]{:S(2)}) collective-permute-start(bf16[4,256,2048]{2,1,0:T(8,128)(2,1)} %bitcast.34), channel_id=1, source_target_pairs={{0,4},{4,0},{8,12},{12,8},{16,20},{20,16},{24,28},{28,24},{1,5},{5... | collective-permute-start | bytes 12582920 | tf_op jit(solution)/shard_map/ppermute | solution.py:514
  552.3 84.3 %collective-permute-start.19 = (bf16[4,256,2048]{2,1,0:T(8,128)(2,1)}, bf16[4,256,2048]{2,1,0:T(8,128)(2,1)}, u32[]{:S(2)}, u32[]{:S(2)}) collective-permute-start(bf16[4,256,2048]{2,1,0:T(8,128)(2,1)} %bitcast.46), channel_id=1, source_target_pairs={{0,4},{4,0},{8,12},{12,8},{16,20},{20,16},{24,28},{28,24},{1,5},{5... | collective-permute-start | bytes 12582920 | tf_op jit(solution)/shard_map/ppermute | solution.py:514
  567.9 15.1 %collective-permute-start.9 = (bf16[4,256,1024]{2,1,0:T(8,128)(2,1)S(1)}, bf16[4,256,1024]{2,1,0:T(8,128)(2,1)S(1)}, u32[]{:S(2)}, u32[]{:S(2)}) collective-permute-start(bf16[4,256,1024]{2,1,0:T(8,128)(2,1)S(1)} %bitcast.250), channel_id=1, source_target_pairs={{0,4},{4,0},{8,12},{12,8},{16,20},{20,16},{24,28},{28,24},{1,5},{5... | collective-permute-start | bytes 6291464 | tf_op jit(solution)/shard_map/ppermute | solution.py:514
  571.3 73.3 %collective-permute-start.26 = (bf16[4,256,2048]{2,1,0:T(8,128)(2,1)}, bf16[4,256,2048]{2,1,0:T(8,128)(2,1)}, u32[]{:S(2)}, u32[]{:S(2)}) collective-permute-start(bf16[4,256,2048]{2,1,0:T(8,128)(2,1)} %bitcast.61), channel_id=1, source_target_pairs={{0,4},{4,0},{8,12},{12,8},{16,20},{20,16},{24,28},{28,24},{1,5},{5... | collective-permute-start | bytes 12582920 | tf_op jit(solution)/shard_map/ppermute | solution.py:514
  584.3 13.9 %collective-permute-start.12 = (bf16[2,256,512]{2,1,0:T(8,128)(2,1)S(1)}, bf16[2,256,512]{2,1,0:T(8,128)(2,1)S(1)}, u32[]{:S(2)}, u32[]{:S(2)}) collective-permute-start(bf16[2,256,512]{2,1,0:T(8,128)(2,1)S(1)} %dynamic-slice_bitcast_fusion.12), channel_id=1, source_target_pairs={{0,16},{4,20},{8,24},{12,28},{16,0},{20,4},{24,8},{28,12},{1,17},{... | collective-permute-start | bytes 1572872 | tf_op jit(solution)/shard_map/ppermute | solution.py:528
  592.7 60.8 %collective-permute-start.34 = (bf16[4,256,2048]{2,1,0:T(8,128)(2,1)}, bf16[4,256,2048]{2,1,0:T(8,128)(2,1)}, u32[]{:S(2)}, u32[]{:S(2)}) collective-permute-start(bf16[4,256,2048]{2,1,0:T(8,128)(2,1)} %bitcast.83), channel_id=1, source_target_pairs={{0,4},{4,0},{8,12},{12,8},{16,20},{20,16},{24,28},{28,24},{1,5},{5... | collective-permute-start | bytes 12582920 | tf_op jit(solution)/shard_map/ppermute | solution.py:514
  598.2 13.3 %collective-permute-start.10 = (bf16[2,256,512]{2,1,0:T(8,128)(2,1)}, bf16[2,256,512]{2,1,0:T(8,128)(2,1)}, u32[]{:S(2)}, u32[]{:S(2)}) collective-permute-start(bf16[2,256,512]{2,1,0:T(8,128)(2,1)} %dynamic-slice_bitcast_fusion.13), channel_id=1, source_target_pairs={{0,8},{4,12},{8,0},{12,4},{16,24},{20,28},{24,16},{28,20},{1,9},{5... | collective-permute-start | bytes 1572872 | tf_op jit(solution)/shard_map/ppermute | solution.py:527
  607.7 11.7 %copy-start.33 = (bf16[256,4,1,256]{0,3,1,2:T(8,128)(2,1)S(1)}, bf16[256,4,1,256]{0,3,1,2:T(8,128)(2,1)}, u32[]{:S(2)}) copy-start(bf16[256,4,1,256]{0,3,1,2:T(8,128)(2,1)} %copy.75) | copy-start | bytes 1572868
  607.7 11.7 %copy-start.37 = (bf16[256,512]{1,0:T(8,128)(2,1)S(1)}, bf16[256,512]{1,0:T(8,128)(2,1)}, u32[]{:S(2)}) copy-start(bf16[256,512]{1,0:T(8,128)(2,1)} %copy-done.35) | copy-start | bytes 786436
  607.7 11.7 %copy-start.40 = (bf16[256,512]{1,0:T(8,128)(2,1)S(1)}, bf16[256,512]{1,0:T(8,128)(2,1)}, u32[]{:S(2)}) copy-start(bf16[256,512]{1,0:T(8,128)(2,1)} %copy-done.38) | copy-start | bytes 786436
  611.5 6.4 collective-permute-start.13
  618.0 6.4 collective-permute-start.11
  632.6 45.8 %collective-permute-start.17 = (bf16[2,256,1024]{2,1,0:T(8,128)(2,1)}, bf16[2,256,1024]{2,1,0:T(8,128)(2,1)}, u32[]{:S(2)}, u32[]{:S(2)}) collective-permute-start(bf16[2,256,1024]{2,1,0:T(8,128)(2,1)} %dynamic-slice_bitcast_fusion.2), channel_id=1, source_target_pairs={{0,16},{4,20},{8,24},{12,28},{16,0},{20,4},{24,8},{28,12},{1,17},{... | collective-permute-start | bytes 3145736 | tf_op jit(solution)/shard_map/ppermute | solution.py:528
  635.0 46.2 %collective-permute-start.15 = (bf16[2,256,1024]{2,1,0:T(8,128)(2,1)}, bf16[2,256,1024]{2,1,0:T(8,128)(2,1)}, u32[]{:S(2)}, u32[]{:S(2)}) collective-permute-start(bf16[2,256,1024]{2,1,0:T(8,128)(2,1)} %dynamic-slice_bitcast_fusion.3), channel_id=1, source_target_pairs={{0,8},{4,12},{8,0},{12,4},{16,24},{20,28},{24,16},{28,20},{1,9},{5... | collective-permute-start | bytes 3145736 | tf_op jit(solution)/shard_map/ppermute | solution.py:527
  642.5 41.3 %collective-permute-start.22 = (bf16[2,256,1024]{2,1,0:T(8,128)(2,1)}, bf16[2,256,1024]{2,1,0:T(8,128)(2,1)}, u32[]{:S(2)}, u32[]{:S(2)}) collective-permute-start(bf16[2,256,1024]{2,1,0:T(8,128)(2,1)} %dynamic-slice_bitcast_fusion), channel_id=1, source_target_pairs={{0,16},{4,20},{8,24},{12,28},{16,0},{20,4},{24,8},{28,12},{1,17},{... | collective-permute-start | bytes 3145736 | tf_op jit(solution)/shard_map/ppermute | solution.py:528
  644.6 41.9 %collective-permute-start.20 = (bf16[2,256,1024]{2,1,0:T(8,128)(2,1)}, bf16[2,256,1024]{2,1,0:T(8,128)(2,1)}, u32[]{:S(2)}, u32[]{:S(2)}) collective-permute-start(bf16[2,256,1024]{2,1,0:T(8,128)(2,1)} %dynamic-slice_bitcast_fusion.1), channel_id=1, source_target_pairs={{0,8},{4,12},{8,0},{12,4},{16,24},{20,28},{24,16},{28,20},{1,9},{5... | collective-permute-start | bytes 3145736 | tf_op jit(solution)/shard_map/ppermute | solution.py:527
  653.6 50.3 %collective-permute-start.29 = (bf16[2,256,1024]{1,2,0:T(8,128)(2,1)}, bf16[2,256,1024]{1,2,0:T(8,128)(2,1)}, u32[]{:S(2)}, u32[]{:S(2)}) collective-permute-start(bf16[2,256,1024]{1,2,0:T(8,128)(2,1)} %bitcast.68), channel_id=1, source_target_pairs={{0,16},{4,20},{8,24},{12,28},{16,0},{20,4},{24,8},{28,12},{1,17},{... | collective-permute-start | bytes 3145736 | tf_op jit(solution)/shard_map/ppermute | solution.py:528
  678.4 28.4 %collective-permute-start.27 = (bf16[2,256,1024]{1,2,0:T(8,128)(2,1)}, bf16[2,256,1024]{1,2,0:T(8,128)(2,1)S(1)}, u32[]{:S(2)}, u32[]{:S(2)}) collective-permute-start(bf16[2,256,1024]{1,2,0:T(8,128)(2,1)} %bitcast.235), channel_id=1, source_target_pairs={{0,8},{4,12},{8,0},{12,4},{16,24},{20,28},{24,16},{28,20},{1,9},{5... | collective-permute-start | bytes 3145736 | tf_op jit(solution)/shard_map/ppermute | solution.py:527
  681.3 45.0 %collective-permute-start.37 = (bf16[2,256,1024]{1,2,0:T(8,128)(2,1)S(1)}, bf16[2,256,1024]{1,2,0:T(8,128)(2,1)S(1)}, u32[]{:S(2)}, u32[]{:S(2)}) collective-permute-start(bf16[2,256,1024]{1,2,0:T(8,128)(2,1)S(1)} %bitcast.234), channel_id=1, source_target_pairs={{0,16},{4,20},{8,24},{12,28},{16,0},{20,4},{24,8},{28,12},{1,17},{... | collective-permute-start | bytes 3145736 | tf_op jit(solution)/shard_map/ppermute | solution.py:528
  683.9 43.9 %collective-permute-start.35 = (bf16[2,256,1024]{1,2,0:T(8,128)(2,1)S(1)}, bf16[2,256,1024]{1,2,0:T(8,128)(2,1)S(1)}, u32[]{:S(2)}, u32[]{:S(2)}) collective-permute-start(bf16[2,256,1024]{1,2,0:T(8,128)(2,1)S(1)} %bitcast.233), channel_id=1, source_target_pairs={{0,8},{4,12},{8,0},{12,4},{16,24},{20,28},{24,16},{28,20},{1,9},{5... | collective-permute-start | bytes 3145736 | tf_op jit(solution)/shard_map/ppermute | solution.py:527
  686.5 51.9 %collective-permute-start.18 = (bf16[256,1024]{1,0:T(8,128)(2,1)S(1)}, bf16[256,1024]{1,0:T(8,128)(2,1)S(1)}, u32[]{:S(2)}, u32[]{:S(2)}) collective-permute-start(bf16[256,1024]{1,0:T(8,128)(2,1)S(1)} %dynamic-slice_bitcast_fusion.10), channel_id=1, source_target_pairs={{0,8},{4,12},{8,0},{12,4},{16,24},{20,28},{24,16},{28,20},{1,9},{5... | collective-permute-start | bytes 1572872 | tf_op jit(solution)/shard_map/ppermute | solution.py:532
  688.8 16.5 %copy-start.21 = (bf16[1,2,256,1024]{2,3,1,0:T(8,128)(2,1)S(1)}, bf16[1,2,256,1024]{2,3,1,0:T(8,128)(2,1)}, u32[]{:S(2)}) copy-start(bf16[1,2,256,1024]{2,3,1,0:T(8,128)(2,1)} %copy.67) | copy-start | bytes 3145732
  689.0 19.5 %copy-start.20 = (bf16[2,1,256,1024]{2,3,0,1:T(8,128)(2,1)S(1)}, bf16[2,1,256,1024]{2,3,0,1:T(8,128)(2,1)}, u32[]{:S(2)}) copy-start(bf16[2,1,256,1024]{2,3,0,1:T(8,128)(2,1)} %copy.65) | copy-start | bytes 3145732
  703.9 36.4 %collective-permute-start.16 = (bf16[256,1024]{1,0:T(8,128)(2,1)S(1)}, bf16[256,1024]{1,0:T(8,128)(2,1)S(1)}, u32[]{:S(2)}, u32[]{:S(2)}) collective-permute-start(bf16[256,1024]{1,0:T(8,128)(2,1)S(1)} %dynamic-slice_bitcast_fusion.11), channel_id=1, source_target_pairs={{0,16},{4,20},{8,24},{12,28},{16,0},{20,4},{24,8},{28,12},{1,17},{... | collective-permute-start | bytes 1572872 | tf_op jit(solution)/shard_map/ppermute | solution.py:531
  706.7 21.0 %copy-start.19 = (bf16[1,2,256,1024]{2,3,1,0:T(8,128)(2,1)S(1)}, bf16[1,2,256,1024]{2,3,1,0:T(8,128)(2,1)}, u32[]{:S(2)}) copy-start(bf16[1,2,256,1024]{2,3,1,0:T(8,128)(2,1)} %copy.81) | copy-start | bytes 3145732
  706.8 42.9 %collective-permute-start.23 = (bf16[256,1024]{1,0:T(8,128)(2,1)S(1)}, bf16[256,1024]{1,0:T(8,128)(2,1)S(1)}, u32[]{:S(2)}, u32[]{:S(2)}) collective-permute-start(bf16[256,1024]{1,0:T(8,128)(2,1)S(1)} %dynamic-slice_bitcast_fusion.8), channel_id=1, source_target_pairs={{0,8},{4,12},{8,0},{12,4},{16,24},{20,28},{24,16},{28,20},{1,9},{5... | collective-permute-start | bytes 1572872 | tf_op jit(solution)/shard_map/ppermute | solution.py:532
  726.3 25.3 %collective-permute-start.21 = (bf16[256,1024]{1,0:T(8,128)(2,1)S(1)}, bf16[256,1024]{1,0:T(8,128)(2,1)S(1)}, u32[]{:S(2)}, u32[]{:S(2)}) collective-permute-start(bf16[256,1024]{1,0:T(8,128)(2,1)S(1)} %dynamic-slice_bitcast_fusion.9), channel_id=1, source_target_pairs={{0,16},{4,20},{8,24},{12,28},{16,0},{20,4},{24,8},{28,12},{1,17},{... | collective-permute-start | bytes 1572872 | tf_op jit(solution)/shard_map/ppermute | solution.py:531
  727.8 33.1 %collective-permute-start.30 = (bf16[256,1024]{0,1:T(8,128)(2,1)S(1)}, bf16[256,1024]{0,1:T(8,128)(2,1)S(1)}, u32[]{:S(2)}, u32[]{:S(2)}) collective-permute-start(bf16[256,1024]{0,1:T(8,128)(2,1)S(1)} %dynamic-slice_bitcast_fusion.6), channel_id=1, source_target_pairs={{0,8},{4,12},{8,0},{12,4},{16,24},{20,28},{24,16},{28,20},{1,9},{5... | collective-permute-start | bytes 1572872 | tf_op jit(solution)/shard_map/ppermute | solution.py:532
  738.5 22.6 %collective-permute-start.28 = (bf16[256,1024]{0,1:T(8,128)(2,1)S(1)}, bf16[256,1024]{0,1:T(8,128)(2,1)S(1)}, u32[]{:S(2)}, u32[]{:S(2)}) collective-permute-start(bf16[256,1024]{0,1:T(8,128)(2,1)S(1)} %dynamic-slice_bitcast_fusion.7), channel_id=1, source_target_pairs={{0,16},{4,20},{8,24},{12,28},{16,0},{20,4},{24,8},{28,12},{1,17},{... | collective-permute-start | bytes 1572872 | tf_op jit(solution)/shard_map/ppermute | solution.py:531
  740.3 28.4 %collective-permute-start.38 = (bf16[256,1024]{0,1:T(8,128)(2,1)S(1)}, bf16[256,1024]{0,1:T(8,128)(2,1)S(1)}, u32[]{:S(2)}, u32[]{:S(2)}) collective-permute-start(bf16[256,1024]{0,1:T(8,128)(2,1)S(1)} %dynamic-slice_bitcast_fusion.4), channel_id=1, source_target_pairs={{0,8},{4,12},{8,0},{12,4},{16,24},{20,28},{24,16},{28,20},{1,9},{5... | collective-permute-start | bytes 1572872 | tf_op jit(solution)/shard_map/ppermute | solution.py:532
  749.7 21.9 %collective-permute-start.36 = (bf16[256,1024]{0,1:T(8,128)(2,1)S(1)}, bf16[256,1024]{0,1:T(8,128)(2,1)S(1)}, u32[]{:S(2)}, u32[]{:S(2)}) collective-permute-start(bf16[256,1024]{0,1:T(8,128)(2,1)S(1)} %dynamic-slice_bitcast_fusion.5), channel_id=1, source_target_pairs={{0,16},{4,20},{8,24},{12,28},{16,0},{20,4},{24,8},{28,12},{1,17},{... | collective-permute-start | bytes 1572872 | tf_op jit(solution)/shard_map/ppermute | solution.py:531
  754.6 17.1 %collective-permute-start.24 = (f32[2,256]{1,0:T(2,128)S(1)}, f32[2,256]{1,0:T(2,128)S(1)}, u32[]{:S(2)}, u32[]{:S(2)}) collective-permute-start(f32[2,256]{1,0:T(2,128)S(1)} %pad_maximum_fusion.9), channel_id=1, source_target_pairs={{0,1},{1,0},{2,3},{3,2},{4,5},{5,4},{6,7},{7,6},{8,9},{9,8},{10,11... | collective-permute-start | bytes 6152 | tf_op jit(solution)/shard_map/ppermute | solution.py:671
  761.5 23.0 %collective-permute-start.33 = (bf16[256,512]{0,1:T(8,128)(2,1)S(1)}, bf16[256,512]{0,1:T(8,128)(2,1)S(1)}, u32[]{:S(2)}, u32[]{:S(2)}) collective-permute-start(bf16[256,512]{0,1:T(8,128)(2,1)S(1)} %get-tuple-element.68), channel_id=1, source_target_pairs={{0,1},{1,2},{2,3},{3,0},{4,5},{5,6},{6,7},{7,4},{8,9},{9,10},{10,1... | collective-permute-start | bytes 786440 | tf_op jit(solution)/shard_map/ppermute | solution.py:568
  762.9 21.6 %collective-permute-start.32 = (bf16[256,512]{0,1:T(8,128)(2,1)S(1)}, bf16[256,512]{0,1:T(8,128)(2,1)S(1)}, u32[]{:S(2)}, u32[]{:S(2)}) collective-permute-start(bf16[256,512]{0,1:T(8,128)(2,1)S(1)} %get-tuple-element.69), channel_id=1, source_target_pairs={{0,2},{1,3},{2,0},{3,1},{4,6},{5,7},{6,4},{7,5},{8,10},{9,11},{10,... | collective-permute-start | bytes 786440 | tf_op jit(solution)/shard_map/ppermute | solution.py:568
  768.8 15.8 %collective-permute-start.31 = (bf16[256,512]{0,1:T(8,128)(2,1)S(1)}, bf16[256,512]{0,1:T(8,128)(2,1)S(1)}, u32[]{:S(2)}, u32[]{:S(2)}) collective-permute-start(bf16[256,512]{0,1:T(8,128)(2,1)S(1)} %get-tuple-element.67), channel_id=1, source_target_pairs={{0,3},{1,0},{2,1},{3,2},{4,7},{5,4},{6,5},{7,6},{8,11},{9,8},{10,9... | collective-permute-start | bytes 786440 | tf_op jit(solution)/shard_map/ppermute | solution.py:568
  771.7 13.7 %copy-start.4 = (bf16[256,2048]{1,0:T(8,128)(2,1)S(1)}, bf16[256,2048]{1,0:T(8,128)(2,1)}, u32[]{:S(2)}) copy-start(bf16[256,2048]{1,0:T(8,128)(2,1)} %param.13) | copy-start | bytes 3145732
  771.7 13.7 %copy-start.47 = (f32[2048]{0:T(1024)S(1)}, f32[2048]{0:T(1024)}, u32[]{:S(2)}) copy-start(f32[2048]{0:T(1024)} %copy-done.46) | copy-start | bytes 24580
  771.7 13.7 %copy-start.51 = (f32[256]{0:T(256)S(1)}, f32[256]{0:T(256)}, u32[]{:S(2)}) copy-start(f32[256]{0:T(256)} %copy-done.50) | copy-start | bytes 3076
  771.8 10.1 %collective-permute-start.25 = (f32[2,256]{1,0:T(2,128)S(1)}, f32[2,256]{1,0:T(2,128)S(1)}, u32[]{:S(2)}, u32[]{:S(2)}) collective-permute-start(f32[2,256]{1,0:T(2,128)S(1)} %fusion.33), channel_id=1, source_target_pairs={{0,2},{1,3},{2,0},{3,1},{4,6},{5,7},{6,4},{7,5},{8,10},{9,11},{10,... | collective-permute-start | bytes 6152 | tf_op jit(solution)/shard_map/ppermute | solution.py:671
  773.7 13.6 %copy-start.2 = (f32[256,2048]{1,0:T(8,128)S(1)}, f32[256,2048]{1,0:T(8,128)}, u32[]{:S(2)}) copy-start(f32[256,2048]{1,0:T(8,128)} %copy-done) | copy-start | bytes 6291460
  773.7 13.6 %copy-start.45 = (f32[2048]{0:T(1024)S(1)}, f32[2048]{0:T(1024)}, u32[]{:S(2)}) copy-start(f32[2048]{0:T(1024)} %copy-done.44) | copy-start | bytes 24580
  773.7 13.6 %copy-start.49 = (f32[256]{0:T(256)S(1)}, f32[256]{0:T(256)}, u32[]{:S(2)}) copy-start(f32[256]{0:T(256)} %copy-done.48) | copy-start | bytes 3076
  773.7 13.6 %copy-start.53 = (f32[256]{0:T(256)S(1)}, f32[256]{0:T(256)}, u32[]{:S(2)}) copy-start(f32[256]{0:T(256)} %copy-done.52) | copy-start | bytes 3076
  (43 other events, 165.8 us)
Sparse Core Ops, SparseCore 0:
  12.7 96.4 all-gather.3
  111.7 46.6 all-gather.5
  160.0 103.2 all-gather.7
  506.2 77.2 reduce-scatter.4
  607.8 76.3 reduce-scatter.2

commit v2 on v1

v2 whole, which is shorter than its diff:
```python
import functools
import math
import types

import jax
import jax.numpy as jnp
from jax import lax
from jax.experimental import pallas as pl
from jax.experimental.pallas import tpu as pltpu
from jax.sharding import PartitionSpec as P

HD = 128
BLK = 128
NORM_EPS = 1e-05
ROPE_BASE = 1000000.0
SCALE = HD ** (-0.5)
SCALE2 = SCALE * math.log2(math.e)
NEG = -1e30
BF = jnp.bfloat16
F32 = jnp.float32
VMEM_LIMIT = 56 * 1024 * 1024


def mm(a, b):
    return jnp.dot(a, b, preferred_element_type=F32)


def mm_bt(a, b):
    return lax.dot_general(a, b, (((1,), (1,)), ((), ())), preferred_element_type=F32)


def mm_at(a, b):
    return lax.dot_general(a, b, (((0,), (0,)), ((), ())), preferred_element_type=F32)


def tree_tables(segment_ids, parent_ids):
    block_count = parent_ids.shape[0]
    first_ids = segment_ids.reshape(block_count, -1)[:, 0]
    block_iota = jnp.arange(block_count, dtype=jnp.int32)
    same_tree = first_ids[:, None] == first_ids[None, :]
    tree_start = jnp.min(jnp.where(same_tree, block_iota[None, :], block_count), axis=1)
    parent_block = tree_start + parent_ids
    step = (block_iota[None, :] == parent_block[:, None]) | (
        block_iota[None, :] == block_iota[:, None]
    )
    for _ in range(3):
        step = jnp.any(step[:, :, None] & step[None, :, :], axis=1)
    ancestry = step.astype(F32)
    return ancestry, jnp.sum(ancestry, axis=1) - 1.0


def rope_tables(depth):
    token_total = depth.shape[0] * BLK
    offsets = (jnp.arange(token_total, dtype=jnp.int32) % BLK).astype(F32)
    places = jnp.repeat(depth, BLK) * BLK + offsets
    freq_index = jnp.arange(HD // 2, dtype=jnp.int32).astype(F32)
    inverse_freq = ROPE_BASE ** (-2.0 * freq_index / HD)
    angles = places[:, None] * inverse_freq[None, :]
    cosine, sine = jnp.cos(angles), jnp.sin(angles)
    return jnp.concatenate([cosine, cosine], axis=1), jnp.concatenate([-sine, sine], axis=1)


def head_cols(h):
    return slice(h * HD, (h + 1) * HD)


def causal_tile(rep):
    rows = lax.broadcasted_iota(jnp.int32, (BLK, BLK), 0)
    cols = lax.broadcasted_iota(jnp.int32, (BLK, BLK), 1)
    tile = cols <= rows
    return jnp.concatenate([tile] * rep, axis=0) if rep > 1 else tile


def stack_heads(ref, rows, first, rep):
    parts = [ref[rows, head_cols(first + i)] for i in range(rep)]
    return jnp.concatenate(parts, axis=0) if rep > 1 else parts[0]


def attend_block(b, q_ref, k_ref, v_ref, bias_ref, m_ref, lse_ref, causal, rep):
    rows = slice(b * BLK, (b + 1) * BLK)
    past = slice(0, b * BLK)
    for g in range(k_ref.shape[1] // HD):
        q = stack_heads(q_ref, rows, g * rep, rep)
        s_diag = jnp.where(causal, mm_bt(q, k_ref[rows, head_cols(g)]) * SCALE2, NEG)
        top = jnp.max(s_diag, axis=1, keepdims=True)
        if b:
            s_past = mm_bt(q, k_ref[past, head_cols(g)]) * SCALE2 + bias_ref[b : b + 1, past]
            top = jnp.maximum(top, jnp.max(s_past, axis=1, keepdims=True))
        e_diag = jnp.exp2(s_diag - top)
        mass = jnp.sum(e_diag, axis=1, keepdims=True)
        out = mm(e_diag.astype(BF), v_ref[rows, head_cols(g)])
        if b:
            e_past = jnp.exp2(s_past - top)
            mass = mass + jnp.sum(e_past, axis=1, keepdims=True)
            out = out + mm(e_past.astype(BF), v_ref[past, head_cols(g)])
        out = (out / mass).astype(BF)
        lse = top + jnp.log2(mass)
        for i in range(rep):
            h = g * rep + i
            m_ref[rows, head_cols(h)] = out[i * BLK : (i + 1) * BLK]
            lse_ref[rows, h : h + 1] = lse[i * BLK : (i + 1) * BLK]


def copy_to(src, dst, send_sem, recv_sem, **where):
    return pltpu.make_async_remote_copy(
        src_ref=src,
        dst_ref=dst,
        send_sem=send_sem,
        recv_sem=recv_sem,
        device_id=where,
        device_id_type=pl.DeviceIdType.MESH,
    )


def group_barrier(masks, n, d, t):
    barrier = pltpu.get_barrier_semaphore()
    for k in range(1, n):
        pl.semaphore_signal(
            barrier, inc=1, device_id={"tensor": lax.rem(t + k, n)}, device_id_type=pl.DeviceIdType.MESH
        )
    for mask in masks:
        pl.semaphore_signal(barrier, inc=1, device_id={"dp": d ^ mask}, device_id_type=pl.DeviceIdType.MESH)
    pl.semaphore_wait(barrier, n - 1 + len(masks))


def attn_kernel(
    n_dp,
    n,
    one_hop,
    hidden_ref,
    cot_ref,
    gain_a_ref,
    gain_f_ref,
    wq_hbm,
    wk_hbm,
    wv_hbm,
    wo_hbm,
    cos_ref,
    sin_ref,
    bias_ref,
    x_out,
    cot_out,
    wo_out,
    q_ref,
    k_ref,
    v_ref,
    m_ref,
    lse_ref,
    mixed_ref,
    middle_ref,
    normed_ref,
    own_buf,
    x_buf,
    wq_ref,
    wk_ref,
    wv_ref,
    wo_ref,
    w_sem,
    x_sem,
    misc_sem,
    ag_send,
    ag_recv,
    cot_send,
    cot_recv,
    wz_send,
    wz_recv,
    wp_send,
    wp_recv,
    wc_send,
    wc_recv,
    m_send,
    m_recv,
):
    t, d = lax.axis_index("tensor"), lax.axis_index("dp")
    rows, width = hidden_ref.shape
    q_cols = wq_ref.shape[1]
    heads, kv_heads = q_cols // HD, wk_ref.shape[1] // HD
    rep = heads // kv_heads
    share = q_cols // n_dp
    half = q_cols // 2
    order = arrival_order(t, n)
    is_mid = (t > 0) & (t < n - 1)
    core, plane = lax.rem(d, 2), d // 2
    masks = list(range(2, n_dp, 2))

    load_w = [
        pltpu.make_async_copy(src, dst, w_sem.at[i])
        for i, (src, dst) in enumerate(((wq_hbm, wq_ref), (wk_hbm, wk_ref), (wv_hbm, wv_ref)))
    ]
    own_wo = pltpu.make_async_copy(wo_hbm, wo_ref.at[t], misc_sem.at[0])
    own_cot = pltpu.make_async_copy(cot_ref, cot_out.at[t], misc_sem.at[1])
    for copy in load_w:
        copy.start()
    own_wo.start()
    own_cot.start()

    def norm(values, gain_ref):
        inverse = lax.rsqrt(jnp.mean(values * values, axis=-1, keepdims=True) + NORM_EPS)
        return (values * inverse * gain_ref[...].astype(F32)).astype(BF)

    for r in range(0, rows, 64):
        part = slice(r, r + 64)
        own_buf[part, :] = norm(hidden_ref[part, :].astype(F32), gain_a_ref)
    group_barrier([1, *masks], n, d, t)

    def line_copy(buf, send_sem, recv_sem, s, to_right, src=None):
        return copy_to(
            buf.at[s] if src is None else src,
            buf.at[s],
            send_sem.at[0 if to_right else 1, s],
            recv_sem.at[s],
            tensor=t + 1 if to_right else t - 1,
        )

    gather_x = functools.partial(line_copy, x_buf, ag_send, ag_recv)
    gather_cot = functools.partial(line_copy, cot_out, cot_send, cot_recv)

    def first_hop(gather, src):
        pl.when(t < n - 1)(lambda: gather(t, True, src).start())
        pl.when(t > 0)(lambda: gather(t, False, src).start())

    def arrive(gather, i):
        s = order[i]
        gather(s, True).wait_recv()
        pl.when((s < t) & (t < n - 1))(lambda: gather(s, True).start())
        pl.when((s > t) & (t > 0))(lambda: gather(s, False).start())

    def keep_rows(i):
        return pltpu.make_async_copy(own_buf if i == 0 else x_buf.at[order[i]], x_out.at[order[i]], x_sem.at[i])

    my_rows = pl.ds(pl.multiple_of(core * half + plane * share, 16), share)
    my_half = pl.ds(pl.multiple_of(core * half, 16), half)

    def wo_line(k):
        return copy_to(
            wo_hbm.at[my_rows],
            wo_ref.at[t, my_rows],
            wz_send.at[k - 1],
            wz_recv.at[k - 1],
            tensor=lax.rem(t + k, n),
        )

    def wo_plane(k, j):
        s = lax.rem(t + n - k, n)
        return copy_to(
            wo_ref.at[s, my_rows],
            wo_ref.at[s, my_rows],
            wp_send.at[k - 1, j],
            wp_recv.at[k - 1, j],
            dp=d ^ masks[j],
        )

    def wo_core(k):
        s = lax.rem(t + n - k, n)
        return copy_to(
            wo_ref.at[s, my_half], wo_ref.at[s, my_half], wc_send.at[k - 1], wc_recv.at[k - 1], dp=d ^ 1
        )

    first_hop(gather_x, own_buf)
    for k in range(1, n):
        wo_line(k).start()
    keep_rows(0).start()

    for copy in load_w:
        copy.wait()
    for i in range(n):
        s = order[i]
        if i == 1:
            arrive(gather_x, 1)
            if n > 2:
                pl.when(is_mid)(lambda: arrive(gather_x, 2))
        elif i > 1:
            if i > 2:
                arrive(gather_x, i)
            else:
                pl.when(jnp.logical_not(is_mid))(lambda: arrive(gather_x, 2))
        if i:
            keep_rows(i).start()
        x = own_buf[...] if i == 0 else x_buf[s]
        here = pl.ds(pl.multiple_of(s * rows, rows), rows)
        cosine, sine = cos_ref[here, :], sin_ref[here, :]
        for w_ref, out_ref, count in ((wq_ref, q_ref, heads), (wk_ref, k_ref, kv_heads)):
            raw = mm(x, w_ref[...])
            for h in range(count):
                u = raw[:, head_cols(h)]
                out_ref[here, head_cols(h)] = (u * cosine + pltpu.roll(u, HD // 2, 1) * sine).astype(BF)
        v_ref[here, :] = mm(x, wv_ref[...]).astype(BF)
        if i == 1:
            for k in range(1, n):
                wo_line(k).wait_recv()
                for j in range(len(masks)):
                    wo_plane(k, j).start()
        if i == n - 1:
            first_hop(gather_cot, cot_ref)
            for k in range(1, n):
                for j in range(len(masks)):
                    wo_plane(k, j).wait_recv()
                wo_core(k).start()

    def heads_to(r):
        here = pl.ds(r * rows, rows)
        return copy_to(m_ref.at[here], mixed_ref.at[t], m_send.at[r], m_recv.at[t], tensor=r)

    causal = causal_tile(rep)
    for b in range(n * rows // BLK):
        attend_block(b, q_ref, k_ref, v_ref, bias_ref, m_ref, lse_ref, causal, rep)
        if (b + 1) * BLK % rows == 0:
            r = (b + 1) * BLK // rows - 1
            pl.when(t != r)(lambda: heads_to(r).start())

            @pl.when(t == r)
            def _():
                mixed_ref[r] = m_ref[r * rows : (r + 1) * rows, :]

    if n > 2 and not one_hop:

        @pl.when(is_mid)
        def _():
            arrive(gather_cot, 1)
            arrive(gather_cot, 2)

    own_wo.wait()
    for k in range(1, n):
        s = lax.rem(t + n - k, n)
        copy_to(m_ref.at[pl.ds(0, rows)], mixed_ref.at[s], m_send.at[0], m_recv.at[s], tensor=s).wait_recv()
        wo_core(k).wait_recv()
    keep_wo = pltpu.make_async_copy(wo_ref, wo_out, misc_sem.at[0])
    keep_wo.start()
    for r in range(0, rows, 128):
        part = slice(r, r + 128)
        total = hidden_ref[part, :].astype(F32)
        for s in range(n):
            total = total + mm(mixed_ref[s, part, :], wo_ref[s])
        middle_ref[part, :] = total
        normed_ref[part, :] = norm(total, gain_f_ref)

    if one_hop:
        pl.when(t > 0)(lambda: gather_cot(t - 1, True).wait_recv())
        pl.when(t < n - 1)(lambda: gather_cot(t + 1, False).wait_recv())
    else:
        for i in range(1, n):
            if i > 2:
                arrive(gather_cot, i)
            else:
                pl.when(jnp.logical_not(is_mid))(functools.partial(arrive, gather_cot, i))
    own_cot.wait()
    keep_wo.wait()
    for i in range(n):
        keep_rows(i).wait()
    for k in range(1, n):
        wo_line(k).wait_send()
        wo_core(k).wait_send()
        for j in range(len(masks)):
            wo_plane(k, j).wait_send()
    if one_hop:
        pl.when(t < n - 1)(lambda: gather_cot(t, True).wait_send())
        pl.when(t > 0)(lambda: gather_cot(t, False).wait_send())
    for s in range(n):
        pl.when(t != s)(lambda: heads_to(s).wait_send())
        for to_right in (True, False):
            goes_on = t < n - 1 if to_right else t > 0

            @pl.when(goes_on & (s <= t if to_right else s >= t))
            def _():
                gather_x(s, to_right).wait_send()
                if not one_hop:
                    gather_cot(s, to_right).wait_send()


def attn_call(n_dp, n, one_hop, hidden, cot, gain_a, gain_f, wq, wk, wv, wo, cosine, sine, bias):
    rows, width = hidden.shape
    q_cols, kv_cols = wq.shape[1], wk.shape[1]
    tokens = n * rows
    any_spec = pl.BlockSpec(memory_space=pl.ANY)
    vmem_spec = pl.BlockSpec(memory_space=pltpu.VMEM)
    dma = pltpu.SemaphoreType.DMA
    masks = n_dp // 2 - 1
    shape = jax.ShapeDtypeStruct
    return pl.pallas_call(
        functools.partial(attn_kernel, n_dp, n, one_hop),
        out_shape=[
            shape((n, rows, width), BF),
            shape((n, rows, width), BF),
            shape((n, q_cols, width), BF),
            shape((tokens, q_cols), BF),
            shape((tokens, kv_cols), BF),
            shape((tokens, kv_cols), BF),
            shape((tokens, q_cols), BF),
            shape((tokens, HD), F32),
            shape((n, rows, q_cols), BF),
            shape((rows, width), F32),
            shape((rows, width), BF),
        ],
        in_specs=[vmem_spec, any_spec, vmem_spec, vmem_spec] + [any_spec] * 4 + [vmem_spec] * 3,
        out_specs=[any_spec] * 3 + [vmem_spec] * 8,
        scratch_shapes=[
            pltpu.VMEM((rows, width), BF),
            pltpu.VMEM((n, rows, width), BF),
            pltpu.VMEM((width, q_cols), BF),
            pltpu.VMEM((width, kv_cols), BF),
            pltpu.VMEM((width, kv_cols), BF),
            pltpu.VMEM((n, q_cols, width), BF),
            dma((3,)),
            dma((n,)),
            dma((2,)),
            dma((2, n)),
            dma((n,)),
            dma((2, n)),
            dma((n,)),
            dma((n - 1,)),
            dma((n - 1,)),
            dma((n - 1, masks)),
            dma((n - 1, masks)),
            dma((n - 1,)),
            dma((n - 1,)),
            dma((n,)),
            dma((n,)),
        ],
        compiler_params=pltpu.CompilerParams(
            vmem_limit_bytes=VMEM_LIMIT, collective_id=2, has_side_effects=True
        ),
        cost_estimate=pl.CostEstimate(
            flops=2 * tokens * width * (q_cols + 2 * kv_cols), bytes_accessed=1 << 25, transcendentals=0
        ),
        name="attn",
    )(hidden, cot, gain_a, gain_f, wq, wk, wv, wo, cosine, sine, bias)


def arrival_order(t, n):
    near = jnp.minimum(t, n - 1 - t)
    order = [t]
    for i in range(1, n):
        both = t - (i + 1) // 2 if i % 2 else t + i // 2
        one_side = jnp.where(t > n - 1 - t, t - (i - near), t + (i - near))
        order.append(jnp.where(i <= 2 * near, both, one_side))
    return order


def attend_back_block(g, b, q_ref, k_ref, v_ref, o_ref, lse_ref, do_ref, turn_back, bias_ref, d_ref, dk_acc, dv_acc):
    heads, kv_heads = q_ref.shape[1] // HD, k_ref.shape[1] // HD
    rep = heads // kv_heads
    last = q_ref.shape[0] // BLK - 1
    causal = causal_tile(rep)
    rows = slice(b * BLK, (b + 1) * BLK)
    q = stack_heads(q_ref, rows, g * rep, rep)
    do = stack_heads(do_ref, rows, g * rep, rep)
    o = stack_heads(o_ref, rows, g * rep, rep)
    lse = [lse_ref[rows, h : h + 1] for h in range(g * rep, (g + 1) * rep)]
    lse = jnp.concatenate(lse, axis=0) if rep > 1 else lse[0]
    delta = jnp.sum(do.astype(F32) * o.astype(F32), axis=1, keepdims=True)
    k_d = k_ref[rows, head_cols(g)]
    p = jnp.where(causal, jnp.exp2(mm_bt(q, k_d) * SCALE2 - lse), 0.0)
    ds = (p * (mm_bt(do, v_ref[rows, head_cols(g)]) - delta)).astype(BF)
    dq = mm(ds, k_d)
    dk = mm_at(ds, q)
    dv = mm_at(p.astype(BF), do)
    if b < last:
        dk = dk + dk_acc[rows, head_cols(g)]
        dv = dv + dv_acc[rows, head_cols(g)]
    d_ref[rows, head_cols(heads + g)] = turn_back(dk * SCALE, rows)
    d_ref[rows, head_cols(heads + kv_heads + g)] = dv.astype(BF)
    if b:
        past = slice(0, b * BLK)
        k_p = k_ref[past, head_cols(g)]
        p = jnp.exp2(mm_bt(q, k_p) * SCALE2 + (bias_ref[b : b + 1, past] - lse))
        ds = (p * (mm_bt(do, v_ref[past, head_cols(g)]) - delta)).astype(BF)
        dq = dq + mm(ds, k_p)
        dk = mm_at(ds, q)
        dv = mm_at(p.astype(BF), do)
        if b < last:
            dk = dk + dk_acc[past, head_cols(g)]
            dv = dv + dv_acc[past, head_cols(g)]
        dk_acc[past, head_cols(g)] = dk
        dv_acc[past, head_cols(g)] = dv
    dq = dq * SCALE
    for i in range(rep):
        d_ref[rows, head_cols(g * rep + i)] = turn_back(dq[i * BLK : (i + 1) * BLK], rows)


def attn_bwd_kernel(q_ref, k_ref, v_ref, o_ref, lse_ref, do_ref, cos_ref, sin_ref, bias_ref, d_ref, dk_acc, dv_acc):
    def turn_back(grad, rows):
        return (grad * cos_ref[rows, :] - pltpu.roll(grad, HD // 2, 1) * sin_ref[rows, :]).astype(BF)

    for b in range(q_ref.shape[0] // BLK - 1, -1, -1):
        for g in range(k_ref.shape[1] // HD):
            attend_back_block(
                g, b, q_ref, k_ref, v_ref, o_ref, lse_ref, do_ref, turn_back, bias_ref, d_ref, dk_acc, dv_acc
            )


BACK_INS = ("fi", "mid", "cot", "hid", "q", "k", "v", "m", "lse", "cos", "sin", "mixed", "wq", "wk", "wv")
BACK_NAMES = (
    BACK_INS,
    ("gain_a", "gain_f", "bias", "x_h", "wo_h", "tot_h", "two_h"),
    ("input_grad", "project_grad", "out_grad", "gain_grad", "three_h"),
    tuple(name + "_b" for name in BACK_INS),
    ("wo", "bg", "mg", "do", "dqkv", "dk_acc", "dv_acc", "got", "one_o", "one_p", "two_o", "two_p"),
    ("three_o", "three_p", "s3", "give", "zr", "gain_st", "gain_dp", "gain_line"),
    ("in_sem", "wo_sem", "x_sem", "s3_sem", "mg_send", "mg_recv", "th_send", "th_recv", "one_send", "one_recv"),
    ("stw_send", "stw_recv", "sth_send", "sth_recv", "z_send", "z_recv", "rs_send", "rs_recv"),
    ("gd_send", "gd_recv", "gl_send", "gl_recv"),
)


def back_kernel(n, *refs):
    names = [name for group in BACK_NAMES for name in group]
    r = types.SimpleNamespace(**dict(zip(names, refs, strict=True)))
    t, d = lax.axis_index("tensor"), lax.axis_index("dp")
    rows, width = r.bg.shape
    q_cols, kv_cols = r.q_b.shape[1], r.k_b.shape[1]
    all_cols = q_cols + 2 * kv_cols
    tokens = n * rows
    core, x, y = lax.rem(d, 2), lax.rem(d // 2, 2), d // 4
    chunk = width // 8
    parts = r.rs_send.shape[2]
    part_rows = rows // parts
    order = arrival_order(t, n)
    is_mid = (t > 0) & (t < n - 1)
    pairs_o = [(2 * y + x, 2 * y + 1 - x, 2), (2 * (1 - y) + x, 2 * (1 - y) + 1 - x, 2)]
    pairs_o += [(2 * y + x, 2 * (1 - y) + x, 4), (2 * y + 1 - x, 2 * (1 - y) + 1 - x, 4)]

    loads = {
        name: pltpu.make_async_copy(getattr(r, name), getattr(r, name + "_b"), r.in_sem.at[i])
        for i, name in enumerate(BACK_INS)
    }
    load_wo = [pltpu.make_async_copy(r.wo_h.at[s], r.wo.at[s], r.wo_sem.at[s]) for s in range(n)]
    load_x = [pltpu.make_async_copy(r.x_h.at[s], r.wo.at[s, pl.ds(0, rows)], r.x_sem.at[s]) for s in range(n)]
    half = r.s3.shape[3]
    load_s3 = []
    for w in range(3):
        for k in range(2):
            load_s3.append(pltpu.make_async_copy(r.tot_h.at[w, 2 * k + 1], r.s3.at[w, k], r.s3_sem.at[0, w, k]))
            landing = r.wo.at[w, pl.ds(rows, rows), pl.ds(k * half, half)]
            load_s3.append(pltpu.make_async_copy(r.two_h.at[w, 2 * k + 1], landing, r.s3_sem.at[1, w, k]))
    for name in ("fi", "mid", "cot"):
        loads[name].start()
    for copy in load_wo:
        copy.start()
    for name in BACK_INS[3:]:
        loads[name].start()
    for copy in load_s3[::2]:
        copy.start()
    group_barrier(range(1, 8), n, d, t)

    for name in ("fi", "mid", "cot"):
        loads[name].wait()

    def norm_back_part(grad, values, gain_ref):
        inverse = lax.rsqrt(jnp.mean(values * values, axis=-1, keepdims=True) + NORM_EPS)
        scaled = values * inverse
        weighted = grad * gain_ref[...].astype(F32)
        back = inverse * (weighted - scaled * jnp.mean(weighted * scaled, axis=-1, keepdims=True))
        return back, grad * scaled

    def gain_along_dp(mask):
        return copy_to(
            r.gain_st.at[d ^ mask, pl.ds(0, 8)],
            r.gain_dp.at[mask - 1],
            r.gd_send.at[mask - 1],
            r.gd_recv.at[mask - 1],
            dp=d ^ mask,
        )

    gain_sum = jnp.zeros((8, width), F32)
    for first in range(0, rows, 64):
        part = slice(first, first + 64)
        back, gain_part = norm_back_part(r.fi_b[part, :], r.mid_b[part, :], r.gain_f)
        gain_sum = gain_sum + jnp.sum(gain_part.reshape(8, 8, width), axis=0)
        total = r.cot_b[part, :].astype(F32) + back
        r.fi_b[part, :] = total
        r.bg[part, :] = total.astype(BF)
    for c in range(8):
        r.gain_st[c, 0:8, :] = gain_sum[:, c * chunk : (c + 1) * chunk]
    for mask in range(1, 8):
        gain_along_dp(mask).start()

    def rows_of(s):
        return pl.ds(pl.multiple_of(s * rows, rows), rows)

    def heads_back(k):
        s = lax.rem(t + k, n)
        return copy_to(r.mg.at[s], r.do.at[rows_of(t)], r.mg_send.at[k - 1], r.mg_recv.at[k - 1], tensor=s)

    for copy in load_wo:
        copy.wait()
    for k in range(1, n):
        s = lax.rem(t + k, n)
        r.mg[s] = mm_bt(r.bg[...], r.wo[s]).astype(BF)
        heads_back(k).start()
    r.do[rows_of(t), :] = mm_bt(r.bg[...], r.wo[t]).astype(BF)

    for copy in load_s3[1::2] + load_x:
        copy.start()

    def ffn_three(w, k):
        return copy_to(r.s3.at[w, k], r.three_h.at[w, k], r.th_send.at[w, k], r.th_recv.at[w, k], dp=d ^ (4, 2)[k])

    for w in range(3):
        for k in range(2):
            for copy in load_s3[4 * w + 2 * k : 4 * w + 2 * k + 2]:
                copy.wait()
            other = r.wo[w, rows : 2 * rows, k * half : (k + 1) * half]
            r.s3[w, k] = (r.s3[w, k].astype(F32) + other.astype(F32)).astype(BF)
            ffn_three(w, k).start()

    ones, twos, threes = (r.one_o, r.one_p), (r.two_o, r.two_p), (r.three_o, r.three_p)

    def stage_one(i, j):
        cols = pl.ds(0, ones[i].shape[2])
        src = r.give.at[lax.rem(j, 2), :, cols]
        return copy_to(src, ones[i].at[j], r.one_send.at[i, j], r.one_recv.at[i, j], dp=d ^ 1)

    def halves(i, k):
        size = ones[i].shape[2] // 2
        return pl.ds((k // 2) * size, size)

    def stage_two(i, k):
        src = ones[i].at[pairs_o[k][1]].at[:, halves(i, k)]
        return copy_to(src, twos[i].at[k], r.stw_send.at[i, k], r.stw_recv.at[i, k], dp=d ^ pairs_o[k][2])

    def stage_three(i, k):
        j = (2 * (1 - y) + x, 2 * y + 1 - x)[k]
        src = ones[i].at[j].at[:, halves(i, 2 * k)]
        return copy_to(src, threes[i].at[k], r.sth_send.at[i, k], r.sth_recv.at[i, k], dp=d ^ (4, 2)[k])

    def start_three(i):
        for k in range(2):
            stage_two(i, 2 * k + 1).wait_recv()
            j = (2 * (1 - y) + x, 2 * y + 1 - x)[k]
            piece = ones[i].at[j].at[:, halves(i, 2 * k)]
            piece[...] = (piece[...].astype(F32) + twos[i][2 * k + 1].astype(F32)).astype(BF)
            stage_three(i, k).start()

    def final_half(i, k):
        stage_two(i, 2 * k).wait_recv()
        stage_three(i, k).wait_recv()
        total = ones[i].at[2 * y + x].at[:, halves(i, 2 * k)][...].astype(F32)
        return total + twos[i][2 * k].astype(F32) + threes[i][k].astype(F32)

    def dp_start(i, terms):
        def give(j, carry):
            @pl.when(j >= 2)
            def _():
                stage_one(i, j - 2).wait_send()

            for cols, value in terms(2 * j + 1 - core):
                r.give[lax.rem(j, 2), :, cols] = value.astype(BF)
            stage_one(i, j).start()
            return carry

        def keep(j, carry):
            stage_one(i, j).wait_recv()
            for cols, value in terms(2 * j + core):
                piece = ones[i].at[j].at[:, cols]
                piece[...] = (piece[...].astype(F32) + value).astype(BF)
            return carry

        lax.fori_loop(0, 4, give, 0)
        lax.fori_loop(0, 4, keep, 0)
        for j in (2, 3):
            stage_one(i, j).wait_send()
        for k in (1, 3, 0, 2):
            stage_two(i, k).start()

    loads["mixed"].wait()

    def out_terms(c):
        grads = r.bg[:, pl.ds(pl.multiple_of(c * chunk, chunk), chunk)]
        for s in range(n):
            yield slice(s * q_cols, (s + 1) * q_cols), mm_at(grads, r.mixed_b[s])

    dp_start(0, out_terms)

    for name in BACK_INS[3:]:
        if name != "mixed":
            loads[name].wait()
    for k in range(1, n):
        heads_back(k).wait_recv()

    def turn_back(grad, part):
        return (grad * r.cos_b[part, :] - pltpu.roll(grad, HD // 2, 1) * r.sin_b[part, :]).astype(BF)

    for b in range(tokens // BLK - 1, -1, -1):
        for g in range(kv_cols // HD):
            attend_back_block(
                g,
                b,
                r.q_b,
                r.k_b,
                r.v_b,
                r.m_b,
                r.lse_b,
                r.do,
                turn_back,
                r.bias,
                r.dqkv,
                r.dk_acc,
                r.dv_acc,
            )

    def scatter(s, c, to_right):
        k, slot = (0, s - 1) if to_right else (1, n - 2 - s)
        piece = pl.ds(c * part_rows, part_rows)
        return copy_to(
            r.wo.at[s, pl.ds(rows + c * part_rows, part_rows)],
            r.got.at[k, slot, piece],
            r.rs_send.at[k, slot, c],
            r.rs_recv.at[k, slot, c],
            tensor=t + 1 if to_right else t - 1,
        )

    for i in range(n - 1, -1, -1):
        s = order[i]
        here = rows_of(s)
        for first in range(0, width, 512):
            cols = slice(first, first + 512)
            term = mm_bt(r.dqkv[here, :q_cols], r.wq_b[cols, :])
            term = term + mm_bt(r.dqkv[here, q_cols : q_cols + kv_cols], r.wk_b[cols, :])
            term = term + mm_bt(r.dqkv[here, q_cols + kv_cols :], r.wv_b[cols, :])
            if i:
                r.wo[s, rows : 2 * rows, cols] = term.astype(BF)
            else:
                r.mid_b[:, cols] = term
        if i == n - 1:
            for c in range(parts):
                pl.when(t == 0)(lambda: scatter(n - 1, c, True).start())
                pl.when(t == n - 1)(lambda: scatter(0, c, False).start())

    def next_sends(i):
        for c in range(parts):

            @pl.when(t == 0)
            def _():
                scatter(i + 1, c, True).wait_send()
                scatter(i, c, True).start()

            @pl.when(t == n - 1)
            def _():
                scatter(n - 2 - i, c, False).wait_send()
                scatter(n - 1 - i, c, False).start()

    from_left = t * 2 < n - 1

    def pass_on(index, near):
        for c in range(parts):
            piece = pl.ds(c * part_rows, part_rows)
            for to_right in (True, False):
                s = index if to_right else n - 1 - index
                way = 0 if to_right else 1
                has_source = t > 0 if to_right else t < n - 1
                now = from_left == (to_right == near)

                @pl.when(has_source & now & (s > t if to_right else s < t))
                def _():
                    scatter(s, c, to_right).wait_recv()
                    term = r.wo.at[s, pl.ds(rows + c * part_rows, part_rows)]
                    term[...] = (term[...].astype(F32) + r.got[way, index - 1, piece].astype(F32)).astype(BF)
                    scatter(s, c, to_right).start()

    def take_own():
        for to_right in (True, False):
            way = 0 if to_right else 1
            has_source = t > 0 if to_right else t < n - 1
            for index in range(1, n):
                s = index if to_right else n - 1 - index

                @pl.when(has_source & (s == t))
                def _():
                    for c in range(parts):
                        scatter(s, c, to_right).wait_recv()
                    r.mid_b[...] += r.got[way, index - 1].astype(F32)

    for copy in load_x:
        copy.wait()

    def project_terms(c):
        cols = pl.ds(pl.multiple_of(c * chunk, chunk), chunk)
        normed = r.wo[:, 0:rows, cols].reshape(tokens, chunk)
        for first in range(0, all_cols, 512):
            part = slice(first, first + 512)
            yield part, mm_at(normed, r.dqkv[:, part])

    dp_start(1, project_terms)
    start_three(0)
    next_sends(2)
    pass_on(3, True)
    start_three(1)
    next_sends(1)
    pass_on(3, False)
    pass_on(2, True)
    for k in range(1, n):
        heads_back(k).wait_send()

    def out_piece(k):
        s = lax.rem(t + k, n)
        return copy_to(r.mg.at[s], r.zr.at[k - 1], r.z_send.at[k - 1], r.z_recv.at[k - 1], tensor=s)

    per_half = n // 2
    for k in range(2):
        total = final_half(0, k)
        for i in range(per_half):
            s = k * per_half + i
            value = total[:, i * q_cols : (i + 1) * q_cols]
            r.mg[s] = value.astype(BF)

            @pl.when(s == t)
            def _():
                r.out_grad[...] = value

    for k in range(1, n):
        out_piece(k).start()
    mine = pl.ds(pl.multiple_of(d * chunk, chunk), chunk)
    size = all_cols // 2
    gain_terms = jnp.zeros((8, chunk), F32)
    for k in range(2):
        value = final_half(1, k)
        r.project_grad[:, k * size : (k + 1) * size] = value
        weight = r.wq_b[mine, :] if k == 0 else jnp.concatenate([r.wk_b[mine, :], r.wv_b[mine, :]], axis=1)
        gain_terms = gain_terms + lax.dot_general(
            jnp.ones((8, size), F32),
            value * weight.astype(F32),
            (((1,), (1,)), ((), ())),
            precision=lax.Precision.HIGHEST,
            preferred_element_type=F32,
        )
    r.gain_st[8, 0:8, :] = gain_terms
    total = r.gain_st[d, 0:8]
    for mask in range(1, 8):
        gain_along_dp(mask).wait_recv()
        total = total + r.gain_dp[mask - 1]
    r.gain_st[8, 8:16, :] = total

    def gain_along_line(k):
        s = lax.rem(t + k, n)
        return copy_to(r.gain_st.at[8], r.gain_line.at[k - 1], r.gl_send.at[k - 1], r.gl_recv.at[k - 1], tensor=s)

    for k in range(1, n):
        gain_along_line(k).start()
    take_own()
    for first in range(0, rows, 64):
        part = slice(first, first + 64)
        back, unused = norm_back_part(r.mid_b[part, :], r.hid_b[part, :].astype(F32), r.gain_a)
        r.input_grad[part, :] = (r.fi_b[part, :] + back).astype(BF)
    for k in range(1, n):
        out_piece(k).wait_recv()
        r.out_grad[...] += r.zr[k - 1].astype(F32)
    total = r.gain_st[8]
    for k in range(1, n):
        gain_along_line(k).wait_recv()
        total = total + r.gain_line[k - 1]
    r.gain_grad[0:1, :] = total[0:1] / r.gain_a[:, mine].astype(F32)
    r.gain_grad[1:2, :] = jnp.sum(total[8:16], axis=0, keepdims=True)
    for k in range(1, n):
        gain_along_line(k).wait_send()
    for mask in range(1, 8):
        gain_along_dp(mask).wait_send()

    for k in range(1, n):
        out_piece(k).wait_send()
    for w in range(3):
        for k in range(2):
            ffn_three(w, k).wait()
    for i in range(2):
        for k in range(4):
            stage_two(i, k).wait_send()
        for k in range(2):
            stage_three(i, k).wait_send()
    for s in range(n):
        for to_right in (True, False):
            goes_on = t < n - 1 if to_right else t > 0

            @pl.when(goes_on & (s > t if to_right else s < t) & (is_mid | (s == (t + 1 if to_right else t - 1))))
            def _():
                for c in range(parts):
                    scatter(s, c, to_right).wait_send()


def back_call(n, arrays, gain_a, gain_f, bias, x_all, w_out_all, totals, twos):
    rows, width = arrays["hid"].shape
    q_cols, kv_cols = arrays["q"].shape[1], arrays["k"].shape[1]
    all_cols = q_cols + 2 * kv_cols
    tokens = n * rows
    chunk = width // 8
    parts = rows // 64
    any_spec = pl.BlockSpec(memory_space=pl.ANY)
    vmem_spec = pl.BlockSpec(memory_space=pltpu.VMEM)
    dma = pltpu.SemaphoreType.DMA
    shape = jax.ShapeDtypeStruct
    return pl.pallas_call(
        functools.partial(back_kernel, n),
        out_shape=[
            shape((rows, width), BF),
            shape((chunk, all_cols), F32),
            shape((chunk, q_cols), F32),
            shape((8, chunk), F32),
            shape((3, 2, chunk, width // 2), BF),
        ],
        in_specs=[any_spec] * len(BACK_INS) + [vmem_spec] * 3 + [any_spec] * 4,
        out_specs=[vmem_spec] * 4 + [any_spec],
        scratch_shapes=[pltpu.VMEM(arrays[name].shape, arrays[name].dtype) for name in BACK_INS]
        + [
            pltpu.VMEM((n, q_cols, width), BF),
            pltpu.VMEM((rows, width), BF),
            pltpu.VMEM((n, rows, q_cols), BF),
            pltpu.VMEM((tokens, q_cols), BF),
            pltpu.VMEM((tokens, all_cols), BF),
            pltpu.VMEM((tokens, kv_cols), F32),
            pltpu.VMEM((tokens, kv_cols), F32),
            pltpu.VMEM((2, n - 1, rows, width), BF),
            pltpu.VMEM((4, chunk, n * q_cols), BF),
            pltpu.VMEM((4, chunk, all_cols), BF),
            pltpu.VMEM((4, chunk, n * q_cols // 2), BF),
            pltpu.VMEM((4, chunk, all_cols // 2), BF),
            pltpu.VMEM((2, chunk, n * q_cols // 2), BF),
            pltpu.VMEM((2, chunk, all_cols // 2), BF),
            pltpu.VMEM((3, 2, chunk, width // 2), BF),
            pltpu.VMEM((2, chunk, n * q_cols), BF),
            pltpu.VMEM((n - 1, chunk, q_cols), BF),
            pltpu.VMEM((9, 16, chunk), F32),
            pltpu.VMEM((7, 8, chunk), F32),
            pltpu.VMEM((n - 1, 16, chunk), F32),
            dma((len(BACK_INS),)),
            dma((n,)),
            dma((n,)),
            dma((2, 3, 2)),
            dma((n - 1,)),
            dma((n - 1,)),
            dma((3, 2)),
            dma((3, 2)),
            dma((2, 4)),
            dma((2, 4)),
            dma((2, 4)),
            dma((2, 4)),
            dma((2, 2)),
            dma((2, 2)),
            dma((n - 1,)),
            dma((n - 1,)),
            dma((2, n - 1, parts)),
            dma((2, n - 1, parts)),
            dma((7,)),
            dma((7,)),
            dma((n - 1,)),
            dma((n - 1,)),
        ],
        compiler_params=pltpu.CompilerParams(
            vmem_limit_bytes=63 * 1024 * 1024, collective_id=3, has_side_effects=True
        ),
        cost_estimate=pl.CostEstimate(flops=1 << 36, bytes_accessed=1 << 26, transcendentals=0),
        name="back",
    )(*[arrays[name] for name in BACK_INS], gain_a, gain_f, bias, x_all, w_out_all, totals, twos)


def ffn_kernel(
    n,
    own_ref,
    cot_ref,
    wg_hbm,
    wu_hbm,
    wd_hbm,
    h_out,
    gg_out,
    ug_out,
    n_out,
    fb_out,
    fi_out,
    wg_ref,
    wu_ref,
    wd_ref,
    n_buf,
    c_buf,
    st_buf,
    fi_part,
    got,
    fb_acc,
    fi_acc,
    w_sem,
    c_sem,
    st_sem,
    n_sem,
    ag_send,
    ag_recv,
    rs_send,
    rs_recv,
):
    t, d = lax.axis_index("tensor"), lax.axis_index("dp")
    rows, width = own_ref.shape
    units = wg_ref.shape[1]
    tile = min(512, units)
    tiles = units // tile
    parts = rs_send.shape[2]
    part_rows = rows // parts
    order = arrival_order(t, n)
    is_mid = (t > 0) & (t < n - 1)

    def load_weights(j):
        cols = pl.ds(j * tile, tile)
        return [
            pltpu.make_async_copy(wg_hbm.at[:, cols], wg_ref.at[:, cols], w_sem.at[0, j]),
            pltpu.make_async_copy(wu_hbm.at[:, cols], wu_ref.at[:, cols], w_sem.at[1, j]),
            pltpu.make_async_copy(wd_hbm.at[cols, :], wd_ref.at[cols, :], w_sem.at[2, j]),
        ]

    def load_cot(i):
        return pltpu.make_async_copy(cot_ref.at[order[i]], c_buf.at[i % 2], c_sem.at[i % 2])

    def gather(s, to_right, src=None):
        return copy_to(
            n_buf.at[s] if src is None else src,
            n_buf.at[s],
            ag_send.at[0 if to_right else 1, s],
            ag_recv.at[s],
            tensor=t + 1 if to_right else t - 1,
        )

    def keep_rows(i):
        return pltpu.make_async_copy(own_ref if i == 0 else n_buf.at[order[i]], n_out.at[order[i]], n_sem.at[i])

    def scatter(s, c, to_right):
        k, slot = (0, s - 1) if to_right else (1, n - 2 - s)
        piece = pl.ds(c * part_rows, part_rows)
        return copy_to(
            fi_part.at[s, piece],
            got.at[k, slot, piece],
            rs_send.at[k, slot, c],
            rs_recv.at[k, slot, c],
            tensor=t + 1 if to_right else t - 1,
        )

    for copy in load_weights(0):
        copy.start()
    load_cot(0).start()
    group_barrier([], n, d, t)
    pl.when(t < n - 1)(lambda: gather(t, True, own_ref).start())
    pl.when(t > 0)(lambda: gather(t, False, own_ref).start())
    for j in range(1, tiles):
        for copy in load_weights(j):
            copy.start()
    keep_rows(0).start()

    def arrive(i):
        s = order[i]
        gather(s, True).wait_recv()
        pl.when((s < t) & (t < n - 1))(lambda: gather(s, True).start())
        pl.when((s > t) & (t > 0))(lambda: gather(s, False).start())
        keep_rows(i).start()

    def stage_out(i):
        return [
            pltpu.make_async_copy(
                st_buf.at[i % 2, k, :, pl.ds(0, out.shape[2])], out.at[order[i]], st_sem.at[k, i % 2]
            )
            for k, out in enumerate((h_out, gg_out, ug_out, fb_out))
        ]

    for i in range(n):
        s = order[i]
        slot = i % 2
        if i == 1:
            arrive(1)
            if n > 2:
                pl.when(is_mid)(functools.partial(arrive, 2))
        elif i > 1:
            pl.when(jnp.logical_not(is_mid))(functools.partial(arrive, i))
        if i + 1 < n:
            load_cot(i + 1).start()
        load_cot(i).wait()
        if i >= 2:
            for copy in stage_out(i - 2):
                copy.wait()
        x_ref = own_ref if i == 0 else n_buf.at[s]
        fb_acc[...] = jnp.zeros_like(fb_acc)
        fi_acc[...] = jnp.zeros_like(fi_acc)

        def one_tile(j, carry):
            if i == 0:
                for copy in load_weights(j):
                    copy.wait()
            if 2 <= i < n - 1:
                pl.when(is_mid & (j == tiles // 2))(functools.partial(arrive, i + 1))
            cols = pl.ds(pl.multiple_of(j * tile, tile), tile)
            x = x_ref[...]
            wg, wu, wd = wg_ref[:, cols], wu_ref[:, cols], wd_ref[cols, :]
            gate = mm(x, wg)
            up = mm(x, wu)
            act_grad = mm_bt(c_buf[slot], wd)
            sig = jax.nn.sigmoid(gate)
            silu = gate * sig
            h = (silu * up).astype(BF)
            gg = (act_grad * up * (sig * (1.0 + gate * (1.0 - sig)))).astype(BF)
            ug = (act_grad * silu).astype(BF)
            for k, value in enumerate((h, gg, ug)):
                st_buf[slot, k, :, cols] = value
            for k in range(0, width, 512):
                piece = slice(k, k + 512)
                fb_acc[:, piece] += mm(h, wd_ref[cols, piece])
                fi_acc[:, piece] += mm_bt(gg, wg_ref[piece, cols]) + mm_bt(ug, wu_ref[piece, cols])
            return carry

        lax.fori_loop(0, tiles, one_tile, 0)
        st_buf[slot, 3, :, :width] = fb_acc[...].astype(BF)
        for copy in stage_out(i):
            copy.start()
        if i == 0:
            fi_out[...] = fi_acc[...]
        else:
            fi_part[s] = fi_acc[...].astype(BF)

            @pl.when(t == 0)
            def _():
                for c in range(parts):
                    scatter(i, c, True).start()

            @pl.when(t == n - 1)
            def _():
                for c in range(parts):
                    scatter(n - 1 - i, c, False).start()

    def pass_on(index, c):
        piece = pl.ds(c * part_rows, part_rows)
        for to_right in (True, False):
            s = index if to_right else n - 1 - index
            k = 0 if to_right else 1
            has_source = t > 0 if to_right else t < n - 1
            beyond = s > t if to_right else s < t

            @pl.when(has_source & beyond)
            def _():
                scatter(s, c, to_right).wait_recv()
                total = fi_part[s, piece].astype(F32) + got[k, index - 1, piece].astype(F32)
                fi_part[s, piece] = total.astype(BF)
                scatter(s, c, to_right).start()

            @pl.when(has_source & (s == t))
            def _():
                scatter(s, c, to_right).wait_recv()
                fi_out[piece] += got[k, index - 1, piece].astype(F32)

    for i in range(max(0, n - 2), n):
        for copy in stage_out(i):
            copy.wait()
    for index in range(1, n):
        for c in range(parts):
            pass_on(index, c)
    for i in range(n):
        keep_rows(i).wait()
    for s in range(n):
        for to_right in (True, False):
            goes_on = t < n - 1 if to_right else t > 0

            @pl.when(goes_on & (s <= t if to_right else s >= t))
            def _():
                gather(s, to_right).wait_send()

            @pl.when(goes_on & (s > t if to_right else s < t))
            def _():
                for c in range(parts):
                    scatter(s, c, to_right).wait_send()


def ffn_call(n, own_rows, cot_all, w_gate, w_up, w_down):
    rows, width = own_rows.shape
    units = w_gate.shape[1]
    tile = min(512, units)
    tiles = units // tile
    parts = max(1, rows // 64)
    tall = jax.ShapeDtypeStruct((n, rows, units), BF)
    wide = jax.ShapeDtypeStruct((n, rows, width), BF)
    any_spec = pl.BlockSpec(memory_space=pl.ANY)
    vmem_spec = pl.BlockSpec(memory_space=pltpu.VMEM)
    dma = pltpu.SemaphoreType.DMA
    return pl.pallas_call(
        functools.partial(ffn_kernel, n),
        out_shape=[tall, tall, tall, wide, wide, jax.ShapeDtypeStruct((rows, width), F32)],
        in_specs=[vmem_spec] + [any_spec] * 4,
        out_specs=[any_spec] * 5 + [vmem_spec],
        scratch_shapes=[
            pltpu.VMEM((width, units), BF),
            pltpu.VMEM((width, units), BF),
            pltpu.VMEM((units, width), BF),
            pltpu.VMEM((n, rows, width), BF),
            pltpu.VMEM((2, rows, width), BF),
            pltpu.VMEM((2, 4, rows, max(units, width)), BF),
            pltpu.VMEM((n, rows, width), BF),
            pltpu.VMEM((2, n - 1, rows, width), BF),
            pltpu.VMEM((rows, width), F32),
            pltpu.VMEM((rows, width), F32),
            dma((3, tiles)),
            dma((2,)),
            dma((4, 2)),
            dma((n,)),
            dma((2, n)),
            dma((n,)),
            dma((2, n - 1, parts)),
            dma((2, n - 1, parts)),
        ],
        compiler_params=pltpu.CompilerParams(
            vmem_limit_bytes=63 * 1024 * 1024, collective_id=4, has_side_effects=True
        ),
        cost_estimate=pl.CostEstimate(
            flops=12 * n * rows * width * units, bytes_accessed=6 * width * units, transcendentals=0
        ),
        name="ffn_plain",
    )(own_rows, cot_all, w_gate, w_up, w_down)


MID_NAMES = (
    ("own", "cot_in", "wg_h", "wu_h", "wd_h"),
    ("cot", "h_out", "tot", "two", "fi_out", "fb_out"),
    ("wg", "wu", "wd", "n_buf", "gu", "h_st", "c_buf", "part", "land", "acc"),
    ("w_sem", "own_sem", "c_sem", "h_sem", "re_sem", "tot_sem", "out_sem", "ready"),
    ("ag_send", "ag_recv", "ct_send", "ct_recv", "rs_send", "rs_recv"),
    ("one_send", "one_recv", "two_send", "two_recv"),
)


def middle_kernel(n, *refs):
    names = [name for group in MID_NAMES for name in group]
    r = types.SimpleNamespace(**dict(zip(names, refs, strict=True)))
    t, d = lax.axis_index("tensor"), lax.axis_index("dp")
    rows, width = r.own.shape
    units = r.wg.shape[1]
    tokens = n * rows
    tile = 512
    tiles = units // tile
    parts = r.rs_send.shape[3]
    part_rows = rows // parts
    order = arrival_order(t, n)
    is_mid = (t > 0) & (t < n - 1)
    is_end = jnp.logical_not(is_mid)
    core, x, y = lax.rem(d, 2), lax.rem(d // 2, 2), d // 4
    chunk = width // 8
    halves = units // 2

    def load_weights(j):
        cols = pl.ds(j * tile, tile)
        return [
            pltpu.make_async_copy(r.wg_h.at[:, cols], r.wg.at[:, cols], r.w_sem.at[0, j]),
            pltpu.make_async_copy(r.wu_h.at[:, cols], r.wu.at[:, cols], r.w_sem.at[1, j]),
            pltpu.make_async_copy(r.wd_h.at[cols, :], r.wd.at[cols, :], r.w_sem.at[2, j]),
        ]

    def line(buf, send_sem, recv_sem, s, to_right, src=None):
        return copy_to(
            buf.at[s] if src is None else src,
            buf.at[s],
            send_sem.at[0 if to_right else 1, s],
            recv_sem.at[s],
            tensor=t + 1 if to_right else t - 1,
        )

    gather = functools.partial(line, r.n_buf, r.ag_send, r.ag_recv)
    gather_cot = functools.partial(line, r.cot, r.ct_send, r.ct_recv)
    own_rows = pltpu.make_async_copy(r.own, r.n_buf.at[t], r.own_sem.at[0])

    def load_cot(i):
        return pltpu.make_async_copy(r.cot.at[order[i]], r.c_buf.at[i % 2], r.c_sem.at[i % 2])

    def keep_h(i):
        return pltpu.make_async_copy(r.h_st, r.h_out.at[order[i]], r.h_sem.at[0])

    def scatter(q, s, c, to_right):
        k, index = (0, s - 1) if to_right else (1, n - 2 - s)
        piece = pl.ds(c * part_rows, part_rows)
        to = t + 1 if to_right else t - 1
        slot = s if to_right else jnp.where(to == s, n, s)
        return copy_to(
            r.part.at[q, s, piece],
            r.land.at[q, slot, piece],
            r.rs_send.at[q, k, index, c],
            r.rs_recv.at[q, k, index, c],
            tensor=to,
        )

    own_rows.start()
    for copy in load_weights(0):
        copy.start()
    load_cot(0).start()
    group_barrier([1, 2, 4], n, d, t)
    own_rows.wait()
    pl.when(t < n - 1)(lambda: gather(t, True).start())
    pl.when(t > 0)(lambda: gather(t, False).start())
    for j in range(1, tiles):
        for copy in load_weights(j):
            copy.start()

    def arrive(which, i):
        s = order[i]
        which(s, True).wait_recv()
        pl.when((s < t) & (t < n - 1))(lambda: which(s, True).start())
        pl.when((s > t) & (t > 0))(lambda: which(s, False).start())

    def end_sends(q, i, chunks):
        @pl.when(t == 0)
        def _():
            for c in chunks:
                scatter(q, i, c, True).start()

        @pl.when(t == n - 1)
        def _():
            for c in chunks:
                scatter(q, n - 1 - i, c, False).start()

    def forward(i):
        s = order[i]
        if i:
            keep_h(i - 1).wait()
        r.acc[...] = jnp.zeros_like(r.acc)

        def one_tile(j, carry):
            if i == 0:
                for copy in load_weights(j):
                    copy.wait()
            if 2 <= i < n - 1:
                pl.when(is_mid & (j == tiles // 2))(functools.partial(arrive, gather, i + 1))
            cols = pl.ds(pl.multiple_of(j * tile, tile), tile)
            rows_in = r.n_buf[s]
            gate = mm(rows_in, r.wg[:, cols])
            up = mm(rows_in, r.wu[:, cols])
            sig = jax.nn.sigmoid(gate)
            silu = gate * sig
            h = (silu * up).astype(BF)
            r.h_st[:, cols] = h
            r.gu[0, s, :, cols] = (up * (sig * (1.0 + gate * (1.0 - sig)))).astype(BF)
            r.gu[1, s, :, cols] = silu.astype(BF)
            for k in range(0, width, 512):
                piece = slice(k, k + 512)
                r.acc[:, piece] += mm(h, r.wd[cols, piece])
            return carry

        lax.fori_loop(0, tiles, one_tile, 0)
        keep_h(i).start()
        r.part[0, s] = r.acc[...].astype(BF)
        if i:
            end_sends(0, i, range(parts))

    def backward(i, chunks):
        s = order[i]
        r.acc[...] = jnp.zeros_like(r.acc)
        load_cot(i).wait()

        def one_tile(j, carry):
            cols = pl.ds(pl.multiple_of(j * tile, tile), tile)
            act_grad = mm_bt(r.c_buf[i % 2], r.wd[cols, :])
            gg = (act_grad * r.gu[0, s, :, cols].astype(F32)).astype(BF)
            ug = (act_grad * r.gu[1, s, :, cols].astype(F32)).astype(BF)
            r.gu[0, s, :, cols] = gg
            r.gu[1, s, :, cols] = ug
            for k in range(0, width, 512):
                piece = slice(k, k + 512)
                r.acc[:, piece] += mm_bt(gg, r.wg[piece, cols]) + mm_bt(ug, r.wu[piece, cols])
            return carry

        lax.fori_loop(0, tiles, one_tile, 0)
        r.part[1, s] = r.acc[...].astype(BF)
        if i:
            end_sends(1, i, chunks)

    from_left = t * 2 < n - 1

    def pass_on(q, index, near):
        for c in range(parts):
            piece = pl.ds(c * part_rows, part_rows)
            for to_right in (True, False):
                s = index if to_right else n - 1 - index
                has_source = t > 0 if to_right else t < n - 1
                now = from_left == (to_right == near)

                @pl.when(has_source & now & (s > t if to_right else s < t))
                def _():
                    scatter(q, s, c, to_right).wait_recv()
                    total = r.part[q, s, piece].astype(F32) + r.land[q, s, piece].astype(F32)
                    r.part[q, s, piece] = total.astype(BF)
                    scatter(q, s, c, to_right).start()

    everything = range(parts)
    forward(0)
    load_cot(1).start()
    backward(0, everything)
    arrive(gather, 1)
    pl.when(is_mid)(functools.partial(arrive, gather, 2))
    pl.when(is_mid)(lambda: load_cot(2).start())
    forward(1)
    backward(1, everything)
    pl.when(is_end)(functools.partial(arrive, gather, 2))
    forward(2)
    pl.when(is_mid)(functools.partial(backward, 2, everything))
    pl.when(is_end)(functools.partial(arrive, gather, 3))
    forward(3)

    @pl.when(is_mid)
    def _():
        gather_cot(t - 1, True).start()
        gather_cot(t + 1, False).start()

    @pl.when(is_end)
    def _():
        arrive(gather_cot, 2)
        load_cot(2).start()
        backward(2, everything)

    arrive(gather_cot, 3)
    load_cot(3).start()
    backward(3, (0, 1))
    keep_h(3).wait()

    first, second = pl.ds(0, tokens), pl.ds(tokens, tokens)
    reload = []
    for k, (src, dst, base) in enumerate(((r.h_out, r.wg, 0), (r.cot, r.wu, tokens))):
        for s in range(n):
            place = dst.at[pl.ds(base + s * rows, rows)]
            reload.append(pltpu.make_async_copy(src.at[s], place, r.re_sem.at[k, s]))
    for copy in reload:
        copy.start()
    pl.semaphore_signal(r.ready, inc=1, device_id={"dp": d ^ 1}, device_id_type=pl.DeviceIdType.MESH)
    pl.semaphore_wait(r.ready, 1)

    def block(w, j):
        if w == 2:
            return r.wg.at[pl.ds(tokens + j * chunk, chunk)]
        return r.wd.at[pl.ds((w * 4 + j) * chunk, chunk)]

    def lhs(w, j, who):
        cols = pl.ds(pl.multiple_of((2 * j + who) * chunk, chunk), chunk)
        if w == 0:
            return r.wu[second, cols]
        return r.n_buf[:, :, cols].reshape(tokens, chunk)

    def rhs(w, part):
        if w == 0:
            return r.wg[first, part]
        return r.gu[w - 1, :, :, part].reshape(tokens, part.stop - part.start)

    def stage_one(w, j):
        return copy_to(r.c_buf.at[lax.rem(j, 2)], block(w, j), r.one_send.at[w, j], r.one_recv.at[w, j], dp=d ^ 1)

    def stage_two(w, k):
        j = (2 * y + 1 - x, 2 * (1 - y) + 1 - x, 2 * (1 - y) + x, 2 * (1 - y) + 1 - x)[k]
        cols = pl.ds((k // 2) * halves, halves)
        return copy_to(
            block(w, j).at[:, cols], r.two.at[w, k], r.two_send.at[w, k], r.two_recv.at[w, k], dp=d ^ (2, 2, 4, 4)[k]
        )

    def keep_total(w, k):
        j = (2 * y + x, 2 * (1 - y) + x, 2 * y + x, 2 * y + 1 - x)[k]
        cols = pl.ds((k // 2) * halves, halves)
        return pltpu.make_async_copy(block(w, j).at[:, cols], r.tot.at[w, k], r.tot_sem.at[w, k])

    for w in range(3):
        if w == 0:
            for copy in reload:
                copy.wait()

        def give(j, carry):
            @pl.when(j >= 2)
            def _():
                stage_one(w, j - 2).wait_send()

            grads = lhs(w, j, 1 - core)
            for k in range(0, units, 512):
                part = slice(k, k + 512)
                r.c_buf[lax.rem(j, 2), :, part] = mm_at(grads, rhs(w, part)).astype(BF)
            stage_one(w, j).start()
            return carry

        def keep(j, carry):
            stage_one(w, j).wait_recv()
            grads = lhs(w, j, core)
            for k in range(0, units, 512):
                part = slice(k, k + 512)
                piece = block(w, j).at[:, part]
                piece[...] = (piece[...].astype(F32) + mm_at(grads, rhs(w, part))).astype(BF)
            return carry

        lax.fori_loop(0, 4, give, 0)
        if w == 0:
            end_sends(1, 3, (2,))
        lax.fori_loop(0, 4, keep, 0)
        if w == 0:
            end_sends(1, 3, (3,))
        for j in (2, 3):
            stage_one(w, j).wait_send()
        for k in range(4):
            stage_two(w, k).start()
            keep_total(w, k).start()
        if w == 0:
            pass_on(0, 2, True)
    pass_on(0, 3, True)
    pass_on(0, 3, False)
    pass_on(1, 2, True)
    pass_on(1, 3, True)
    pass_on(1, 3, False)

    def total_of(q):
        r.acc[...] = r.part[q, t].astype(F32)
        for to_right in (True, False):
            has_source = t > 0 if to_right else t < n - 1

            @pl.when(has_source)
            def _():
                for s in range(n):

                    @pl.when(s == t)
                    def _():
                        for c in range(parts):
                            scatter(q, s, c, to_right).wait_recv()

                slot = t if to_right else n
                r.acc[...] += r.land[q, slot].astype(F32)

    for q, out in ((0, r.fb_out), (1, r.fi_out)):
        total_of(q)
        copy = pltpu.make_async_copy(r.acc, out, r.out_sem.at[q])
        copy.start()
        copy.wait()

    for w in range(3):
        for k in range(4):
            keep_total(w, k).wait()
            stage_two(w, k).wait()
    for s in range(n):
        for to_right in (True, False):
            goes_on = t < n - 1 if to_right else t > 0

            @pl.when(goes_on & (s <= t if to_right else s >= t))
            def _():
                gather(s, to_right).wait_send()

            @pl.when(goes_on & (s < t if to_right else s > t))
            def _():
                gather_cot(s, to_right).wait_send()

            @pl.when(goes_on & (s > t if to_right else s < t))
            def _():
                for q in range(2):
                    for c in range(parts):
                        scatter(q, s, c, to_right).wait_send()


def middle_call(n, own_rows, cot_part, w_gate, w_up, w_down):
    rows, width = own_rows.shape
    units = w_gate.shape[1]
    parts = rows // 64
    shape = jax.ShapeDtypeStruct
    wide = shape((n, rows, width), BF)
    pieces = shape((3, 4, width // 8, units // 2), BF)
    any_spec = pl.BlockSpec(memory_space=pl.ANY)
    dma = pltpu.SemaphoreType.DMA
    return pl.pallas_call(
        functools.partial(middle_kernel, n),
        out_shape=[wide, shape((n, rows, units), BF), pieces, pieces] + [shape((rows, width), F32)] * 2,
        in_specs=[any_spec] * 5,
        out_specs=[any_spec] * 6,
        input_output_aliases={1: 0},
        scratch_shapes=[
            pltpu.VMEM((width, units), BF),
            pltpu.VMEM((width, units), BF),
            pltpu.VMEM((units, width), BF),
            pltpu.VMEM((n, rows, width), BF),
            pltpu.VMEM((2, n, rows, units), BF),
            pltpu.VMEM((rows, units), BF),
            pltpu.VMEM((2, rows, width), BF),
            pltpu.VMEM((2, n, rows, width), BF),
            pltpu.VMEM((2, n + 1, rows, width), BF),
            pltpu.VMEM((rows, width), F32),
            dma((3, units // 512)),
            dma((1,)),
            dma((2,)),
            dma((1,)),
            dma((2, n)),
            dma((3, 4)),
            dma((2,)),
            pltpu.SemaphoreType.REGULAR,
            dma((2, n)),
            dma((n,)),
            dma((2, n)),
            dma((n,)),
            dma((2, 2, n - 1, parts)),
            dma((2, 2, n - 1, parts)),
            dma((3, 4)),
            dma((3, 4)),
            dma((3, 4)),
            dma((3, 4)),
        ],
        compiler_params=pltpu.CompilerParams(
            vmem_limit_bytes=64 * 1024 * 1024 - 65536, collective_id=1, has_side_effects=True
        ),
        cost_estimate=pl.CostEstimate(
            flops=18 * n * rows * width * units, bytes_accessed=6 * width * units, transcendentals=0
        ),
        name="middle",
    )(own_rows, cot_part, w_gate, w_up, w_down)


def full_call(kernel, out_shapes, args, scratch=(), flops=0, name=None):
    spec = pl.BlockSpec(memory_space=pltpu.VMEM)
    return pl.pallas_call(
        kernel,
        out_shape=out_shapes,
        in_specs=[spec] * len(args),
        out_specs=[spec] * len(out_shapes),
        scratch_shapes=list(scratch),
        compiler_params=pltpu.CompilerParams(vmem_limit_bytes=VMEM_LIMIT),
        cost_estimate=pl.CostEstimate(flops=flops, bytes_accessed=flops // 400, transcendentals=0),
        name=name,
    )(*args)


def normalize(rows_wide, gain_wide):
    inverse = lax.rsqrt(jnp.mean(rows_wide * rows_wide, axis=-1, keepdims=True) + NORM_EPS)
    scaled_rows = rows_wide * inverse
    return scaled_rows, inverse, (scaled_rows * gain_wide).astype(BF)


def norm_back(normed_grad, scaled_rows, inverse, gain_wide):
    weighted = normed_grad * gain_wide
    return inverse * (weighted - scaled_rows * jnp.mean(weighted * scaled_rows, axis=-1, keepdims=True))


def pairs(n, bit):
    return [(i, i ^ bit) for i in range(n)]


def pick(array, index, axis):
    return lax.dynamic_index_in_dim(array, index, axis, keepdims=False)


def dp_scatter(give, keep, n_dp):
    me = lax.axis_index("dp")
    total = keep + lax.ppermute(give, "dp", pairs(n_dp, 1))
    if n_dp != 8:
        bit = 2
        while total.shape[0] > 1:
            parts = total.reshape(-1, 2, *total.shape[1:])
            mine = (me // bit) % 2
            total = pick(parts, mine, 1) + lax.ppermute(pick(parts, 1 - mine, 1), "dp", pairs(n_dp, bit))
            bit *= 2
        return total[0].astype(F32)
    x, y = (me // 2) % 2, me // 4
    cols = total.shape[-1] // 2
    parts = total.reshape(2, 2, *total.shape[1:])
    a, b = parts[..., :cols], parts[..., cols:]
    got_a = lax.ppermute(pick(a, 1 - x, 1), "dp", pairs(n_dp, 2))
    got_b = lax.ppermute(pick(b, 1 - y, 0), "dp", pairs(n_dp, 4))
    a = pick(a, x, 1) + got_a
    b = pick(b, y, 0) + got_b
    got_a = lax.ppermute(pick(a, 1 - y, 0), "dp", pairs(n_dp, 4))
    got_b = lax.ppermute(pick(b, 1 - x, 0), "dp", pairs(n_dp, 2))
    a = pick(a, y, 0).astype(F32) + got_a.astype(F32)
    b = pick(b, x, 0).astype(F32) + got_b.astype(F32)
    return jnp.concatenate([a, b], axis=-1)


def core_split(rows, n_dp):
    tokens, width = rows.shape
    core = lax.axis_index("dp") % 2
    parts = rows.reshape(tokens, n_dp // 2, 2, width // n_dp)
    return [pick(parts, c, 2).reshape(tokens, width // 2) for c in (1 - core, core)]


def grad_scatter(split_rows, cols, n_dp):
    give, keep = [
        mm_at(part, cols).astype(BF).reshape(n_dp // 2, 2 * part.shape[1] // n_dp, cols.shape[1])
        for part in split_rows
    ]
    return dp_scatter(give, keep, n_dp)


def after(value, *others):
    return lax.optimization_barrier((value, *others))[0]


def shards(n_dp, n_t, hidden_in, gain_attn, w_query, w_key, w_value, w_out, gain_ffn, w_gate, w_up, w_down, segments, parents, cotangent):
    tokens = segments.shape[0]
    own, width = hidden_in.shape
    q_cols, kv_cols, units = w_query.shape[1], w_key.shape[1], w_gate.shape[1]
    heads = q_cols // HD
    me_t = lax.axis_index("tensor")
    me_dp = lax.axis_index("dp")
    gain_attn_wide = gain_attn.astype(F32)
    gain_ffn_wide = gain_ffn.astype(F32)

    def ring(value, shift):
        return lax.ppermute(value, "tensor", [(i, (i + shift) % n_t) for i in range(n_t)])

    ancestry, depth = tree_tables(segments, parents)
    cosine, sine = rope_tables(depth)
    bias = jnp.where(jnp.repeat(ancestry, BLK, axis=1) > 0.5, 0.0, NEG)
    fused = n_dp == 8 and n_t == 4 and units == width and q_cols == 2 * own and tokens * 2 == width
    x_all, cot_all, w_out_all, queries, keys, values, mixed, lse, mixed_own, middle, normed_ffn = attn_call(
        n_dp, n_t, fused, hidden_in, cotangent, gain_attn[None], gain_ffn[None], w_query, w_key, w_value, w_out, cosine, sine, bias
    )
    x_all = x_all.reshape(tokens, width)
    w_out_all = w_out_all.reshape(n_t * q_cols, width)
    rows_wide = hidden_in.astype(F32)
    if fused:
        unused_cot, unused_h, totals, twos, ffn_in_grad, fb_sum = middle_call(
            n_t, normed_ffn, cot_all, w_gate, w_up, w_down
        )
        output = (middle + fb_sum).astype(BF)
        arrays = dict(
            fi=ffn_in_grad,
            mid=middle,
            cot=cotangent,
            hid=hidden_in,
            q=queries,
            k=keys,
            v=values,
            m=mixed,
            lse=lse,
            cos=cosine,
            sin=sine,
            mixed=mixed_own,
            wq=w_query,
            wk=w_key,
            wv=w_value,
        )
        input_grad, project_wgrad, w_out_grad, gain_grads, threes = back_call(
            n_t,
            arrays,
            gain_attn[None],
            gain_ffn[None],
            bias,
            x_all.reshape(n_t, own, width),
            w_out_all.reshape(n_t, q_cols, width),
            totals,
            twos,
        )
        w_out_grad = w_out_grad.T
        final = [totals[:, k].astype(F32) + twos[:, k].astype(F32) + threes[:, k // 2].astype(F32) for k in (0, 2)]
        w_down_grad, w_gate_grad, w_up_grad = [jnp.concatenate([f[w] for f in final], axis=1) for w in range(3)]
        w_down_grad = w_down_grad.T
        w_query_grad = project_wgrad[:, :q_cols]
        w_key_grad = project_wgrad[:, q_cols : q_cols + kv_cols]
        w_value_grad = project_wgrad[:, q_cols + kv_cols :]
        gain_attn_grad, gain_ffn_grad = gain_grads[0], gain_grads[1]
    else:
        w_project = jnp.concatenate([w_query, w_key, w_value], axis=1)
        h_all, gg_all, ug_all, n_all, fb_part, ffn_in_grad = ffn_call(n_t, normed_ffn, cot_all, w_gate, w_up, w_down)
        fb_sum = lax.psum_scatter(fb_part.reshape(tokens, width), "tensor", scatter_dimension=0, tiled=True)
        output = (middle + fb_sum.astype(F32)).astype(BF)
        h_all, gg_all, ug_all = [a.reshape(tokens, units) for a in (h_all, gg_all, ug_all)]
        cot_split = core_split(cot_all.reshape(tokens, width), n_dp)
        normed_split = core_split(n_all.reshape(tokens, width), n_dp)
        w_down_grad = grad_scatter(cot_split, h_all, n_dp).T
        w_gate_grad = grad_scatter(normed_split, gg_all, n_dp)
        w_up_grad = grad_scatter(normed_split, ug_all, n_dp)

        scaled_attn, inverse_attn, _ = normalize(rows_wide, gain_attn_wide)
        scaled_ffn, inverse_ffn, _ = normalize(middle, gain_ffn_wide)
        middle_grad = cotangent.astype(F32) + norm_back(ffn_in_grad, scaled_ffn, inverse_ffn, gain_ffn_wide)
        branch_grad = middle_grad.astype(BF)
        mixed_grads = mm_bt(branch_grad, w_out_all).astype(BF).reshape(own, n_t, q_cols)
        mixed_grads = [pick(mixed_grads, (me_t + n_t - d) % n_t, 1) for d in range(n_t)]
        mixed_grads = [mixed_grads[0]] + [ring(mixed_grads[d], n_t - d) for d in range(1, n_t)]
        mixed_grad = jnp.roll(jnp.concatenate(mixed_grads, axis=0), me_t * own, axis=0)

        (project_grad,) = full_call(
            attn_bwd_kernel,
            [jax.ShapeDtypeStruct((tokens, q_cols + 2 * kv_cols), BF)],
            (queries, keys, values, mixed, lse, mixed_grad, cosine, sine, bias),
            scratch=[pltpu.VMEM((tokens, kv_cols), F32)] * 2,
            flops=10 * heads * tokens * tokens * HD,
            name="attn_bwd",
        )
        dq, dk, dv = (
            project_grad[:, :q_cols],
            project_grad[:, q_cols : q_cols + kv_cols],
            project_grad[:, q_cols + kv_cols :],
        )
        attn_in_part = mm_bt(project_grad, w_project).astype(BF)
        attn_in_grad = lax.psum_scatter(attn_in_part, "tensor", scatter_dimension=0, tiled=True).astype(F32)

        mixed_wide = jnp.moveaxis(mixed_own, 0, 1).reshape(own, n_t * q_cols)
        out_grad = grad_scatter(core_split(branch_grad, n_dp), mixed_wide, n_dp)
        out_parts = out_grad.reshape(-1, n_t, q_cols)
        w_out_grad = pick(out_parts, me_t, 1)
        for d in range(1, n_t):
            piece = pick(out_parts, (me_t + d) % n_t, 1).astype(BF)
            w_out_grad = w_out_grad + ring(piece, d).astype(F32)
        w_out_grad = w_out_grad.T

        project_wgrad = grad_scatter(core_split(x_all, n_dp), project_grad, n_dp)
        w_query_grad = project_wgrad[:, :q_cols]
        w_key_grad = project_wgrad[:, q_cols : q_cols + kv_cols]
        w_value_grad = project_wgrad[:, q_cols + kv_cols :]

        input_grad = (middle_grad + norm_back(attn_in_grad, scaled_attn, inverse_attn, gain_attn_wide)).astype(BF)

        def own_rows(array):
            return lax.dynamic_slice_in_dim(array, me_dp * (width // n_dp), width // n_dp, 0).astype(F32)

        gain_sums = jnp.stack(
            [
                jnp.sum(own_rows(w_project) * project_wgrad, axis=1),
                jnp.sum(own_rows(w_gate) * w_gate_grad, axis=1) + jnp.sum(own_rows(w_up) * w_up_grad, axis=1),
            ]
        )
        bit = 1
        while bit < n_t:
            gain_sums = gain_sums + lax.ppermute(gain_sums, "tensor", pairs(n_t, bit))
            bit *= 2
        gain_attn_grad = gain_sums[0] / own_rows(gain_attn)
        gain_ffn_grad = gain_sums[1] / own_rows(gain_ffn)

    return (
        output,
        input_grad,
        gain_attn_grad,
        w_query_grad,
        w_key_grad,
        w_value_grad,
        w_out_grad,
        gain_ffn_grad,
        w_gate_grad,
        w_up_grad,
        w_down_grad,
    )


def solution(mesh):
    return jax.shard_map(
        functools.partial(shards, mesh.shape["dp"], mesh.shape["tensor"]),
        mesh=mesh,
        in_specs=(
            P(("dp", "tensor"), None),
            P(),
            P(None, "tensor"),
            P(None, "tensor"),
            P(None, "tensor"),
            P("tensor", None),
            P(),
            P(None, "tensor"),
            P(None, "tensor"),
            P("tensor", None),
            P("dp"),
            P("dp"),
            P(("dp", "tensor"), None),
        ),
        out_specs=(
            P(("dp", "tensor"), None),
            P(("dp", "tensor"), None),
            P("dp"),
            P("dp", "tensor"),
            P("dp", "tensor"),
            P("dp", "tensor"),
            P("tensor", "dp"),
            P("dp"),
            P("dp", "tensor"),
            P("dp", "tensor"),
            P("tensor", "dp"),
        ),
        check_vma=False,
    )
```

time: 812 us -> 541 us (0.67)
  Pallas kernels: 211 us -> 499 us
  waiting for transfers between devices: 238 us -> 0 us
  local copies, waits for them, and re-layouts: 145 us -> 17.5 us
  matrix products: 76.7 us -> 0 us
  starting transfers between devices: 49.2 us -> 0 us
  other arithmetic: 64.3 us -> 16.5 us
  between operations: 15.3 us -> 0.92 us
    pallas_call x3, Pallas kernels: 211 us -> 499 us  [the longest x1 226 us: middle_call(): pl.pallas_call(functools.partial(middle_kernel, n), out_shape=[wide, shap...]
    ppermute x39 -> x0, waiting for transfers between devices: 126 us -> none  [the longest x12 47.4 us: ring(): lax.ppermute(value, 'tensor', [(i, (i + shift) % n_t) for i in range(n_t)])]
    all_gather x3 -> x0, waiting for transfers between devices: 112 us -> none  [the longest x1 50.3 us: shards(): x_all = lax.all_gather(normed_attn, 'tensor', axis=0, tiled=True)]
    dot_general x19 -> x0, matrix products: 76.7 us -> none  [the longest x10 51.7 us: mm_at(): lax.dot_general(a, b, (((0,), (0,)), ((), ())), preferred_element_type=F32)]
    unnamed x144 -> x15, local copies, waits for them, and re-layouts: 63.6 us -> 4.98 us
    ppermute x39 -> x0, starting transfers between devices: 49 us -> none  [the longest x12 19.3 us: ring(): lax.ppermute(value, 'tensor', [(i, (i + shift) % n_t) for i in range(n_t)])]
    dynamic_slice x14 -> x0, local copies, waits for them, and re-layouts: 40.6 us -> none  [the longest x12 37.3 us: pick(): return lax.dynamic_index_in_dim(array, index, axis, keepdims=False)]
    add x28 -> x1, other arithmetic: 29.7 us -> 3.83 us  [shards(): totals[:, k].astype(F32) + twos[:, k].astype(F32)]
  transfers between devices with their start and end apart: 44 -> 0, of which waited for: 17 -> 0; matrix products, arithmetic and copies ran while one was open for 30% -> 0% of each run, Pallas kernels for 2% -> 0%
where the time goes in v2:
time: 541 us; the launch traced here: 534 us
  Pallas kernels  499 us (92%)
  local copies, waits for them, and re-layouts  17.5 us (3%)
  other arithmetic  16.5 us (3%)
    pallas_call x1, Pallas kernels, middle_call(): pl.pallas_call(functools.partial(middle_kernel, n), out_shape=[wide, shap...  226 us
    pallas_call x1, Pallas kernels, attn_call(): pl.pallas_call(functools.partial(attn_kernel, n_dp, n, one_hop), out_shap...  146 us
    pallas_call x1, Pallas kernels, back_call(): pl.pallas_call(functools.partial(back_kernel, n), out_shape=[shape((rows,...  127 us

profile of v2, /device:TPU:0, one launch (start us, length us, event | category | flops | bytes accessed | tf_op | source)
XLA Modules:
  0.0 533.7 jit_solution(13673614964474961572)
XLA Ops:
  0.6 0.8 slice_reduce_fusion
  1.4 0.2 select_reduce_fusion
  1.6 0.7 add.40
  2.3 0.1 fusion.5
  2.4 0.1 and_reduce_fusion.2
  2.5 0.1 and_reduce_fusion.1
  2.6 0.1 and_reduce_fusion
  2.7 0.1 fusion.7
  2.8 0.1 copy.31
  2.9 0.1 fusion.2
  2.9 1.3 broadcast_in_dim.24.gain_a_ref.refs_15_
  4.2 1.3 broadcast_in_dim.27.gain_f_ref.refs_16_
  5.5 0.7 broadcast_bitcast_fusion.bias_ref.refs_17_
  6.2 1.9 fusion
  8.1 1.3 pad_maximum_fusion.2
  9.4 145.5 %attn.1 = (bf16[4,256,2048]{2,1,0:T(8,128)(2,1)}, bf16[4,256,2048]{2,1,0:T(8,128)(2,1)}, bf16[4,512,2048]{2,1,0:T(8,128)(2,1)}, bf16[1024,512]{1,0:T(8,128)(2,1)...) custom-call(bf16[256,2048]{1,0:T(8,128)(2,1)} %refs_3_.3, ...), custom_call_target="tpu_custom_call" | custom-call | flops 4294967296 | bytes 33554432 | tf_op jit(solution)/shard_map/attn/pallas_call | solution.py:379
  155.0 225.9 %middle.1 = (bf16[4,256,2048]{2,1,0:T(8,128)(2,1)}, bf16[4,256,2048]{2,1,0:T(8,128)(2,1)}, bf16[3,4,256,1024]{3,2,1,0:T(8,128)(2,1)}, bf16[3,4,256,1024]{3,2,1,0...) custom-call(bf16[256,2048]{1,0:T(8,128)(2,1)} %get-tuple-element.32.refs_0_, ...), custom_call_target="tpu_custom_call", output_to_operand_aliasing={{0}: (1, {})} | custom-call | flops 77309411328 | bytes 25165824 | tf_op jit(solution)/shard_map/middle/pallas_call | solution.py:1548
  380.9 127.3 %back.1 = (bf16[256,2048]{1,0:T(8,128)(2,1)}, f32[256,1024]{1,0:T(8,128)}, f32[256,512]{1,0:T(8,128)}, f32[8,256]{1,0:T(8,128)}, bf16[3,2,256,1024]{3,2,1,0:T(8,128)(2,1)}) custom-call(f32[256,2048]{1,0:T(8,128)} %get-tuple-element.35.refs_0_, f32[256,2048]{1,0:T(8,128)} %get-tuple-element.31.refs_1_, bf16[256,2048]{1,0:T(8,128)(2,1)} %refs_2_.3, ...), custom_call_target="tpu_custom_call" | custom-call | flops 68719476736 | bytes 67108864 | tf_op jit(solution)/shard_map/back/pallas_call | solution.py:889
  508.2 0.0 copy-start.4
  508.2 3.6 add_convert_fusion
  511.8 0.0 copy-done.4
  511.8 3.8 convert_add_fusion.1
  515.6 1.8 slice_bitcast_fusion.1
  517.4 1.3 fusion.9
  518.8 2.0 copy.32
  520.8 1.9 slice.62
  522.7 1.9 fusion.8
  524.5 0.0 copy-start.2
  524.5 1.5 slice_bitcast_fusion
  526.1 0.0 copy-done.2
  526.1 0.1 maximum_bitcast_fusion
  526.2 0.0 copy-start.1
  526.2 1.8 copy.33
  528.0 0.0 copy-done.1
  528.0 0.0 copy-start
  528.0 0.0 copy-start.3
  528.0 2.9 pad_maximum_fusion.1
  530.9 0.0 copy-done
  530.9 0.0 copy-done.3
  530.9 0.0 copy-start.5
  530.9 1.5 pad_maximum_fusion
  532.4 0.1 copy-done.5
  532.5 1.0 copy.36
  (2 shorter events, 0.0 us)
Async XLA Ops:
  508.2 3.6 copy-start.4
  524.5 1.5 copy-start.2
  526.2 1.8 copy-start.1
  528.0 2.9 copy-start
  528.0 2.9 copy-start.3
  530.9 1.6 copy-start.5

commit v3 on v2

--- a/solution.py
+++ b/solution.py
@@ -491,14 +491,14 @@
 BACK_INS = ("fi", "mid", "cot", "hid", "q", "k", "v", "m", "lse", "cos", "sin", "mixed", "wq", "wk", "wv")
 BACK_NAMES = (
     BACK_INS,
-    ("gain_a", "gain_f", "bias", "x_h", "wo_h", "tot_h", "two_h"),
-    ("input_grad", "project_grad", "out_grad", "gain_grad", "three_h"),
+    ("gain_a", "gain_f", "bias", "x_h", "wo_h", "tot_h", "two_h", "late_h"),
+    ("input_grad", "project_grad", "out_grad", "gain_grad", "three_h", "late_two"),
     tuple(name + "_b" for name in BACK_INS),
     ("wo", "bg", "mg", "do", "dqkv", "dk_acc", "dv_acc", "got", "one_o", "one_p", "two_o", "two_p"),
     ("three_o", "three_p", "s3", "give", "zr", "gain_st", "gain_dp", "gain_line"),
     ("in_sem", "wo_sem", "x_sem", "s3_sem", "mg_send", "mg_recv", "th_send", "th_recv", "one_send", "one_recv"),
     ("stw_send", "stw_recv", "sth_send", "sth_recv", "z_send", "z_recv", "rs_send", "rs_recv"),
-    ("gd_send", "gd_recv", "gl_send", "gl_recv"),
+    ("gd_send", "gd_recv", "gl_send", "gl_recv", "lt_send", "lt_recv"),
 )
 
 
@@ -531,7 +531,13 @@
         for k in range(2):
             load_s3.append(pltpu.make_async_copy(r.tot_h.at[w, 2 * k + 1], r.s3.at[w, k], r.s3_sem.at[0, w, k]))
             landing = r.wo.at[w, pl.ds(rows, rows), pl.ds(k * half, half)]
-            load_s3.append(pltpu.make_async_copy(r.two_h.at[w, 2 * k + 1], landing, r.s3_sem.at[1, w, k]))
+            other = r.two_h.at[w, 2 * k + 1] if w < 2 else r.late_two.at[2 * k + 1]
+            load_s3.append(pltpu.make_async_copy(other, landing, r.s3_sem.at[1, w, k]))
+
+    def late_stage(k):
+        src, dst = r.late_h.at[k], r.late_two.at[k]
+        return copy_to(src, dst, r.lt_send.at[k], r.lt_recv.at[k], dp=d ^ (2, 2, 4, 4)[k])
+
     for name in ("fi", "mid", "cot"):
         loads[name].start()
     for copy in load_wo:
@@ -541,6 +547,8 @@
     for copy in load_s3[::2]:
         copy.start()
     group_barrier(range(1, 8), n, d, t)
+    for k in (1, 3, 0, 2):
+        late_stage(k).start()
 
     for name in ("fi", "mid", "cot"):
         loads[name].wait()
@@ -589,19 +597,22 @@
         heads_back(k).start()
     r.do[rows_of(t), :] = mm_bt(r.bg[...], r.wo[t]).astype(BF)
 
-    for copy in load_s3[1::2] + load_x:
+    for copy in load_s3[1:8:2] + load_x:
         copy.start()
 
     def ffn_three(w, k):
         return copy_to(r.s3.at[w, k], r.three_h.at[w, k], r.th_send.at[w, k], r.th_recv.at[w, k], dp=d ^ (4, 2)[k])
 
-    for w in range(3):
+    def start_ffn_three(w):
         for k in range(2):
             for copy in load_s3[4 * w + 2 * k : 4 * w + 2 * k + 2]:
                 copy.wait()
             other = r.wo[w, rows : 2 * rows, k * half : (k + 1) * half]
             r.s3[w, k] = (r.s3[w, k].astype(F32) + other.astype(F32)).astype(BF)
             ffn_three(w, k).start()
+
+    start_ffn_three(0)
+    start_ffn_three(1)
 
     ones, twos, threes = (r.one_o, r.one_p), (r.two_o, r.two_p), (r.three_o, r.three_p)
 
@@ -674,8 +685,12 @@
     for name in BACK_INS[3:]:
         if name != "mixed":
             loads[name].wait()
+    for k in range(2):
+        late_stage(2 * k + 1).wait_recv()
+        load_s3[9 + 2 * k].start()
     for k in range(1, n):
         heads_back(k).wait_recv()
+    start_ffn_three(2)
 
     def turn_back(grad, part):
         return (grad * r.cos_b[part, :] - pltpu.roll(grad, HD // 2, 1) * r.sin_b[part, :]).astype(BF)
@@ -857,6 +872,10 @@
 
     for k in range(1, n):
         out_piece(k).wait_send()
+    for k in range(4):
+        late_stage(k).wait_send()
+    for k in (0, 2):
+        late_stage(k).wait_recv()
     for w in range(3):
         for k in range(2):
             ffn_three(w, k).wait()
@@ -875,7 +894,7 @@
                     scatter(s, c, to_right).wait_send()
 
 
-def back_call(n, arrays, gain_a, gain_f, bias, x_all, w_out_all, totals, twos):
+def back_call(n, arrays, gain_a, gain_f, bias, x_all, w_out_all, totals, twos, late):
     rows, width = arrays["hid"].shape
     q_cols, kv_cols = arrays["q"].shape[1], arrays["k"].shape[1]
     all_cols = q_cols + 2 * kv_cols
@@ -894,9 +913,10 @@
             shape((chunk, q_cols), F32),
             shape((8, chunk), F32),
             shape((3, 2, chunk, width // 2), BF),
+            shape((4, chunk, width // 2), BF),
         ],
-        in_specs=[any_spec] * len(BACK_INS) + [vmem_spec] * 3 + [any_spec] * 4,
-        out_specs=[vmem_spec] * 4 + [any_spec],
+        in_specs=[any_spec] * len(BACK_INS) + [vmem_spec] * 3 + [any_spec] * 5,
+        out_specs=[vmem_spec] * 4 + [any_spec] * 2,
         scratch_shapes=[pltpu.VMEM(arrays[name].shape, arrays[name].dtype) for name in BACK_INS]
         + [
             pltpu.VMEM((n, q_cols, width), BF),
@@ -941,13 +961,86 @@
             dma((7,)),
             dma((n - 1,)),
             dma((n - 1,)),
+            dma((4,)),
+            dma((4,)),
         ],
         compiler_params=pltpu.CompilerParams(
             vmem_limit_bytes=63 * 1024 * 1024, collective_id=3, has_side_effects=True
         ),
         cost_estimate=pl.CostEstimate(flops=1 << 36, bytes_accessed=1 << 26, transcendentals=0),
         name="back",
-    )(*[arrays[name] for name in BACK_INS], gain_a, gain_f, bias, x_all, w_out_all, totals, twos)
+    )(*[arrays[name] for name in BACK_INS], gain_a, gain_f, bias, x_all, w_out_all, totals, twos, late)
+
+
+def finish_kernel(tot, two, late, three, proj, out, ig, oo, gate, up, down, wq, wk, wv, wo, ig_out, oo_out):
+    def total(w):
+        other = two[w, 0] if w < 2 else late[0]
+        return tot[w, 0].astype(F32) + other.astype(F32) + three[w, 0].astype(F32)
+
+    down[...] = total(0).T
+    gate[...] = total(1)
+    up[...] = total(2)
+    wo[...] = out[...].T
+    ig_out[...] = ig[...]
+    oo_out[...] = oo[...]
+
+    @pl.when(pl.program_id(0) == 0)
+    def _():
+        wq[...] = proj[...]
+
+    @pl.when(pl.program_id(0) == 1)
+    def _():
+        wk[...] = proj[:, : wk.shape[1]]
+        wv[...] = proj[:, wk.shape[1] :]
+
+
+def finish_call(totals, twos, late, threes, project_grad, out_grad, input_grad, output):
+    chunk, half = totals.shape[2:]
+    rows, width = input_grad.shape
+    all_cols, q_cols = project_grad.shape[1], out_grad.shape[1]
+    kv_cols = (all_cols - q_cols) // 2
+    shape, spec = jax.ShapeDtypeStruct, pl.BlockSpec
+    side = lambda k: (0, k)
+    below = lambda k: (k, 0)
+    fixed = lambda k: (0, 0)
+    return pl.pallas_call(
+        finish_kernel,
+        grid=(2,),
+        in_specs=[
+            spec((3, 1, chunk, half), lambda k: (0, 2 * k, 0, 0)),
+            spec((2, 1, chunk, half), lambda k: (0, 2 * k, 0, 0)),
+            spec((1, chunk, half), lambda k: (2 * k, 0, 0)),
+            spec((3, 1, chunk, half), lambda k: (0, k, 0, 0)),
+            spec((chunk, all_cols // 2), side),
+            spec((chunk, q_cols // 2), side),
+            spec((rows, width // 2), side),
+            spec((rows, width // 2), side),
+        ],
+        out_specs=[
+            spec((chunk, half), side),
+            spec((chunk, half), side),
+            spec((half, chunk), below),
+            spec((chunk, q_cols), fixed),
+            spec((chunk, kv_cols), fixed),
+            spec((chunk, kv_cols), fixed),
+            spec((q_cols // 2, chunk), below),
+            spec((rows, width // 2), side),
+            spec((rows, width // 2), side),
+        ],
+        out_shape=[
+            shape((chunk, 2 * half), F32),
+            shape((chunk, 2 * half), F32),
+            shape((2 * half, chunk), F32),
+            shape((chunk, q_cols), F32),
+            shape((chunk, kv_cols), F32),
+            shape((chunk, kv_cols), F32),
+            shape((q_cols, chunk), F32),
+            shape((rows, width), BF),
+            shape((rows, width), BF),
+        ],
+        compiler_params=pltpu.CompilerParams(vmem_limit_bytes=VMEM_LIMIT),
+        name="finish",
+    )(totals, twos, late, threes, project_grad, out_grad, input_grad, output)
 
 
 def ffn_kernel(
@@ -1204,12 +1297,12 @@
 
 
 MID_NAMES = (
-    ("own", "cot_in", "wg_h", "wu_h", "wd_h"),
-    ("cot", "h_out", "tot", "two", "fi_out", "fb_out"),
+    ("own", "cot_in", "wg_h", "wu_h", "wd_h", "middle_h"),
+    ("cot", "h_out", "tot", "two", "late", "fi_out", "output"),
     ("wg", "wu", "wd", "n_buf", "gu", "h_st", "c_buf", "part", "land", "acc"),
     ("w_sem", "own_sem", "c_sem", "h_sem", "re_sem", "tot_sem", "out_sem", "ready"),
     ("ag_send", "ag_recv", "ct_send", "ct_recv", "rs_send", "rs_recv"),
-    ("one_send", "one_recv", "two_send", "two_recv"),
+    ("one_send", "one_recv", "two_send", "two_recv", "late_sem"),
 )
 
 
@@ -1383,14 +1476,14 @@
     backward(1, everything)
     pl.when(is_end)(functools.partial(arrive, gather, 2))
     forward(2)
-    pl.when(is_mid)(functools.partial(backward, 2, everything))
-    pl.when(is_end)(functools.partial(arrive, gather, 3))
-    forward(3)
-
     @pl.when(is_mid)
     def _():
         gather_cot(t - 1, True).start()
         gather_cot(t + 1, False).start()
+
+    pl.when(is_mid)(functools.partial(backward, 2, everything))
+    pl.when(is_end)(functools.partial(arrive, gather, 3))
+    forward(3)
 
     @pl.when(is_end)
     def _():
@@ -1440,6 +1533,11 @@
             block(w, j).at[:, cols], r.two.at[w, k], r.two_send.at[w, k], r.two_recv.at[w, k], dp=d ^ (2, 2, 4, 4)[k]
         )
 
+    def keep_late(k):
+        j = (2 * y + 1 - x, 2 * (1 - y) + 1 - x, 2 * (1 - y) + x, 2 * (1 - y) + 1 - x)[k]
+        cols = pl.ds((k // 2) * halves, halves)
+        return pltpu.make_async_copy(block(2, j).at[:, cols], r.late.at[k], r.late_sem.at[k])
+
     def keep_total(w, k):
         j = (2 * y + x, 2 * (1 - y) + x, 2 * y + x, 2 * y + 1 - x)[k]
         cols = pl.ds((k // 2) * halves, halves)
@@ -1480,7 +1578,10 @@
         for j in (2, 3):
             stage_one(w, j).wait_send()
         for k in range(4):
-            stage_two(w, k).start()
+            if w < 2:
+                stage_two(w, k).start()
+            else:
+                keep_late(k).start()
             keep_total(w, k).start()
         if w == 0:
             pass_on(0, 2, True)
@@ -1491,7 +1592,7 @@
     pass_on(1, 3, False)
 
     def total_of(q):
-        r.acc[...] = r.part[q, t].astype(F32)
+        r.acc[...] += r.part[q, t].astype(F32)
         for to_right in (True, False):
             has_source = t > 0 if to_right else t < n - 1
 
@@ -1507,16 +1608,27 @@
                 slot = t if to_right else n
                 r.acc[...] += r.land[q, slot].astype(F32)
 
-    for q, out in ((0, r.fb_out), (1, r.fi_out)):
-        total_of(q)
-        copy = pltpu.make_async_copy(r.acc, out, r.out_sem.at[q])
-        copy.start()
-        copy.wait()
+    add_middle = pltpu.make_async_copy(r.middle_h, r.acc, r.out_sem.at[0])
+    add_middle.start()
+    add_middle.wait()
+    total_of(0)
+    r.h_st[...] = r.acc[...].astype(BF)
+    keep_output = pltpu.make_async_copy(r.h_st, r.output, r.out_sem.at[0])
+    keep_output.start()
+    r.acc[...] = jnp.zeros_like(r.acc)
+    total_of(1)
+    keep_fi = pltpu.make_async_copy(r.acc, r.fi_out, r.out_sem.at[1])
+    keep_fi.start()
+    keep_output.wait()
+    keep_fi.wait()
 
     for w in range(3):
         for k in range(4):
             keep_total(w, k).wait()
-            stage_two(w, k).wait()
+            if w < 2:
+                stage_two(w, k).wait()
+            else:
+                keep_late(k).wait()
     for s in range(n):
         for to_right in (True, False):
             goes_on = t < n - 1 if to_right else t > 0
@@ -1536,20 +1648,21 @@
                         scatter(q, s, c, to_right).wait_send()
 
 
-def middle_call(n, own_rows, cot_part, w_gate, w_up, w_down):
+def middle_call(n, own_rows, cot_part, w_gate, w_up, w_down, middle):
     rows, width = own_rows.shape
     units = w_gate.shape[1]
     parts = rows // 64
     shape = jax.ShapeDtypeStruct
     wide = shape((n, rows, width), BF)
-    pieces = shape((3, 4, width // 8, units // 2), BF)
+    piece = (4, width // 8, units // 2)
     any_spec = pl.BlockSpec(memory_space=pl.ANY)
     dma = pltpu.SemaphoreType.DMA
     return pl.pallas_call(
         functools.partial(middle_kernel, n),
-        out_shape=[wide, shape((n, rows, units), BF), pieces, pieces] + [shape((rows, width), F32)] * 2,
-        in_specs=[any_spec] * 5,
-        out_specs=[any_spec] * 6,
+        out_shape=[wide, shape((n, rows, units), BF), shape((3, *piece), BF), shape((2, *piece), BF), shape(piece, BF)]
+        + [shape((rows, width), F32), shape((rows, width), BF)],
+        in_specs=[any_spec] * 6,
+        out_specs=[any_spec] * 7,
         input_output_aliases={1: 0},
         scratch_shapes=[
             pltpu.VMEM((width, units), BF),
@@ -1580,6 +1693,7 @@
             dma((3, 4)),
             dma((3, 4)),
             dma((3, 4)),
+            dma((4,)),
         ],
         compiler_params=pltpu.CompilerParams(
             vmem_limit_bytes=64 * 1024 * 1024 - 65536, collective_id=1, has_side_effects=True
@@ -1588,7 +1702,7 @@
             flops=18 * n * rows * width * units, bytes_accessed=6 * width * units, transcendentals=0
         ),
         name="middle",
-    )(own_rows, cot_part, w_gate, w_up, w_down)
+    )(own_rows, cot_part, w_gate, w_up, w_down, middle)
 
 
 def full_call(kernel, out_shapes, args, scratch=(), flops=0, name=None):
@@ -1693,10 +1807,9 @@
     w_out_all = w_out_all.reshape(n_t * q_cols, width)
     rows_wide = hidden_in.astype(F32)
     if fused:
-        unused_cot, unused_h, totals, twos, ffn_in_grad, fb_sum = middle_call(
-            n_t, normed_ffn, cot_all, w_gate, w_up, w_down
+        unused_cot, unused_h, totals, twos, late, ffn_in_grad, output = middle_call(
+            n_t, normed_ffn, cot_all, w_gate, w_up, w_down, middle
         )
-        output = (middle + fb_sum).astype(BF)
         arrays = dict(
             fi=ffn_in_grad,
             mid=middle,
@@ -1714,7 +1827,7 @@
             wk=w_key,
             wv=w_value,
         )
-        input_grad, project_wgrad, w_out_grad, gain_grads, threes = back_call(
+        input_grad, project_wgrad, out_grad, gain_grads, threes, late_twos = back_call(
             n_t,
             arrays,
             gain_attn[None],
@@ -1724,14 +1837,11 @@
             w_out_all.reshape(n_t, q_cols, width),
             totals,
             twos,
+            late,
         )
-        w_out_grad = w_out_grad.T
-        final = [totals[:, k].astype(F32) + twos[:, k].astype(F32) + threes[:, k // 2].astype(F32) for k in (0, 2)]
-        w_down_grad, w_gate_grad, w_up_grad = [jnp.concatenate([f[w] for f in final], axis=1) for w in range(3)]
-        w_down_grad = w_down_grad.T
-        w_query_grad = project_wgrad[:, :q_cols]
-        w_key_grad = project_wgrad[:, q_cols : q_cols + kv_cols]
-        w_value_grad = project_wgrad[:, q_cols + kv_cols :]
+        w_gate_grad, w_up_grad, w_down_grad, w_query_grad, w_key_grad, w_value_grad, w_out_grad, input_grad, output = (
+            finish_call(totals, twos, late_twos, threes, project_wgrad, out_grad, input_grad, output)
+        )
         gain_attn_grad, gain_ffn_grad = gain_grads[0], gain_grads[1]
     else:
         w_project = jnp.concatenate([w_query, w_key, w_value], axis=1)

time: 541 us -> 521 us (0.963)
  local copies, waits for them, and re-layouts: 17.5 us -> 5.49 us
  other arithmetic: 16.5 us -> 4.62 us
    pallas_call x1, Pallas kernels: 226 us -> 210 us  [middle_call(): pl.pallas_call(functools.partial(middle_kernel, n), out_shape=[wide, shap...]
    pallas_call x1, Pallas kernels: 127 us -> 138 us  [back_call(): pl.pallas_call(functools.partial(back_kernel, n), out_shape=[shape((rows,...]
    pallas_call x0 -> x1, Pallas kernels: none -> 8.13 us  [finish_call(): pl.pallas_call(finish_kernel, grid=(2,), in_specs=[spec((3, 1, chunk, hal...]
where the time goes in v3:
time: 521 us; the launch traced here: 512 us
  Pallas kernels  501 us (96%)
  local copies, waits for them, and re-layouts  5.49 us (1%)
    pallas_call x1, Pallas kernels, middle_call(): pl.pallas_call(functools.partial(middle_kernel, n), out_shape=[wide, shap...  210 us
    pallas_call x1, Pallas kernels, attn_call(): pl.pallas_call(functools.partial(attn_kernel, n_dp, n, one_hop), out_shap...  146 us
    pallas_call x1, Pallas kernels, back_call(): pl.pallas_call(functools.partial(back_kernel, n), out_shape=[shape((rows,...  138 us

profile of v3, /device:TPU:0, one launch (start us, length us, event | category | flops | bytes accessed | tf_op | source)
XLA Modules:
  0.0 512.4 jit_solution(1377528240792126974)
XLA Ops:
  0.6 0.8 slice_reduce_fusion
  1.4 0.2 select_reduce_fusion
  1.6 0.7 add.21
  2.3 0.1 fusion.5
  2.4 0.1 and_reduce_fusion.2
  2.5 0.1 and_reduce_fusion.1
  2.6 0.1 and_reduce_fusion
  2.7 0.1 fusion.7
  2.8 0.1 copy.25
  2.9 0.1 fusion.2
  2.9 1.3 broadcast_in_dim.24.gain_a_ref.refs_15_
  4.2 1.3 broadcast_in_dim.27.gain_f_ref.refs_16_
  5.5 0.7 broadcast_bitcast_fusion.bias_ref.refs_17_
  6.2 1.9 fusion
  8.1 1.3 pad_maximum_fusion
  9.4 145.6 %attn.1 = (bf16[4,256,2048]{2,1,0:T(8,128)(2,1)}, bf16[4,256,2048]{2,1,0:T(8,128)(2,1)}, bf16[4,512,2048]{2,1,0:T(8,128)(2,1)}, bf16[1024,512]{1,0:T(8,128)(2,1)...) custom-call(bf16[256,2048]{1,0:T(8,128)(2,1)} %refs_3_.3, ...), custom_call_target="tpu_custom_call" | custom-call | flops 4294967296 | bytes 33554432 | tf_op jit(solution)/shard_map/attn/pallas_call | solution.py:379
  155.0 209.9 %middle.1 = (bf16[4,256,2048]{2,1,0:T(8,128)(2,1)}, bf16[4,256,2048]{2,1,0:T(8,128)(2,1)}, bf16[3,4,256,1024]{3,2,1,0:T(8,128)(2,1)}, bf16[2,4,256,1024]{3,2,1,0...) custom-call(bf16[256,2048]{1,0:T(8,128)(2,1)} %get-tuple-element.42., ...), custom_call_target="tpu_custom_call", output_to_operand_aliasing={{0}: (1, {})} | custom-call | flops 77309411328 | bytes 25165824 | tf_op jit(solution)/shard_map/middle/pallas_call | solution.py:1660
  364.9 137.8 %back.1 = (bf16[256,2048]{1,0:T(8,128)(2,1)}, f32[256,1024]{1,0:T(8,128)}, f32[256,512]{1,0:T(8,128)}, f32[8,256]{1,0:T(8,128)}, bf16[3,2,256,1024]{3,2,1,0:T(8,128)(2,1)}, /*index=5*/bf16[4,256,1024]{2,1,0:T(8,128)(2,1)}) custom-call(f32[256,2048]{1,0:T(8,128)} %get-tuple-element.47.refs_0_, f32[256,2048]{1,0:T(8,128)} %get-tuple-element.44.refs_5_.refs_1_, ...), custom_call_target="tpu_custom_call" | custom-call | flops 68719476736 | bytes 67108864 | tf_op jit(solution)/shard_map/back/pallas_call | solution.py:908
  502.7 8.1 %finish.1 = (f32[256,2048]{1,0:T(8,128)}, f32[256,2048]{1,0:T(8,128)}, f32[2048,256]{1,0:T(8,128)}, f32[256,512]{1,0:T(8,128)}, f32[256,256]{1,0:T(8,128)}, /*in...) custom-call(bf16[3,4,256,1024]{3,2,1,0:T(8,128)(2,1)} %get-tuple-element.45.refs_20_, ...), custom_call_target="tpu_custom_call" | custom-call | tf_op jit(solution)/shard_map/finish/pallas_call | solution.py:1006
  510.9 1.3 fusion.8
  (2 shorter events, 0.0 us)

commit v4 on v3

--- a/solution.py
+++ b/solution.py
@@ -491,14 +491,15 @@
 BACK_INS = ("fi", "mid", "cot", "hid", "q", "k", "v", "m", "lse", "cos", "sin", "mixed", "wq", "wk", "wv")
 BACK_NAMES = (
     BACK_INS,
-    ("gain_a", "gain_f", "bias", "x_h", "wo_h", "tot_h", "two_h", "late_h"),
-    ("input_grad", "project_grad", "out_grad", "gain_grad", "three_h", "late_two"),
+    ("gain_a", "gain_f", "bias", "x_h", "wo_h", "tot_h", "two_h", "late_h", "far_h"),
+    ("input_grad", "project_grad", "out_grad", "gain_grad", "three_h", "late_two", "far_add"),
     tuple(name + "_b" for name in BACK_INS),
     ("wo", "bg", "mg", "do", "dqkv", "dk_acc", "dv_acc", "got", "one_o", "one_p", "two_o", "two_p"),
-    ("three_o", "three_p", "s3", "give", "zr", "gain_st", "gain_dp", "gain_line"),
+    ("three_o", "three_p", "s3", "give", "zr", "gain_st", "gain_dp", "gain_line", "far_land"),
     ("in_sem", "wo_sem", "x_sem", "s3_sem", "mg_send", "mg_recv", "th_send", "th_recv", "one_send", "one_recv"),
     ("stw_send", "stw_recv", "sth_send", "sth_recv", "z_send", "z_recv", "rs_send", "rs_recv"),
     ("gd_send", "gd_recv", "gl_send", "gl_recv", "lt_send", "lt_recv"),
+    ("late_sem", "far_sem", "far_send", "far_recv"),
 )
 
 
@@ -516,6 +517,7 @@
     part_rows = rows // parts
     order = arrival_order(t, n)
     is_mid = (t > 0) & (t < n - 1)
+    from_left = t * 2 < n - 1
     pairs_o = [(2 * y + x, 2 * y + 1 - x, 2), (2 * (1 - y) + x, 2 * (1 - y) + 1 - x, 2)]
     pairs_o += [(2 * y + x, 2 * (1 - y) + x, 4), (2 * y + 1 - x, 2 * (1 - y) + 1 - x, 4)]
 
@@ -526,26 +528,46 @@
     load_wo = [pltpu.make_async_copy(r.wo_h.at[s], r.wo.at[s], r.wo_sem.at[s]) for s in range(n)]
     load_x = [pltpu.make_async_copy(r.x_h.at[s], r.wo.at[s, pl.ds(0, rows)], r.x_sem.at[s]) for s in range(n)]
     half = r.s3.shape[3]
-    load_s3 = []
+    load_tot, load_two = {}, {}
     for w in range(3):
         for k in range(2):
-            load_s3.append(pltpu.make_async_copy(r.tot_h.at[w, 2 * k + 1], r.s3.at[w, k], r.s3_sem.at[0, w, k]))
-            landing = r.wo.at[w, pl.ds(rows, rows), pl.ds(k * half, half)]
-            other = r.two_h.at[w, 2 * k + 1] if w < 2 else r.late_two.at[2 * k + 1]
-            load_s3.append(pltpu.make_async_copy(other, landing, r.s3_sem.at[1, w, k]))
-
-    def late_stage(k):
-        src, dst = r.late_h.at[k], r.late_two.at[k]
-        return copy_to(src, dst, r.lt_send.at[k], r.lt_recv.at[k], dp=d ^ (2, 2, 4, 4)[k])
-
+            load_tot[w, k] = [pltpu.make_async_copy(r.tot_h.at[w, 2 * k + 1], r.s3.at[w, k], r.s3_sem.at[0, w, k])]
+            if w < 2:
+                landing = r.wo.at[w, pl.ds(rows, rows), pl.ds(k * half, half)]
+                load_two[w, k] = [pltpu.make_async_copy(r.two_h.at[w, 2 * k + 1], landing, r.s3_sem.at[1, w, k])]
+            else:
+                load_two[w, k] = [
+                    pltpu.make_async_copy(
+                        r.late_two.at[2 * k + 1, :, pl.ds(i * q_cols, q_cols)], r.mg.at[2 * k + i], r.late_sem.at[k, i]
+                    )
+                    for i in range(2)
+                ]
+
+    def late_stage(i):
+        k = i if i < 4 else 2 * (i - 4)
+        src, dst = r.late_h.at[i], r.late_two.at[i]
+        return copy_to(src, dst, r.lt_send.at[i], r.lt_recv.at[i], dp=d ^ (2, 2, 4, 4)[k])
+
+    def far_copy(i, c, src=None):
+        piece = pl.ds(c * part_rows, part_rows)
+        return copy_to(
+            r.far_land.at[piece] if src is None else src.at[i, piece],
+            r.far_land.at[piece],
+            r.far_send.at[i, c],
+            r.far_recv.at[i, c],
+            tensor=t + 1 if i else t - 1,
+        )
+
+    load_far = pltpu.make_async_copy(r.far_h.at[jnp.where(from_left, 0, 1)], r.bg, r.far_sem.at[0])
     for name in ("fi", "mid", "cot"):
         loads[name].start()
     for copy in load_wo:
         copy.start()
     for name in BACK_INS[3:]:
         loads[name].start()
-    for copy in load_s3[::2]:
-        copy.start()
+    for w in range(3):
+        for k in range(2):
+            load_tot[w, k][0].start()
     group_barrier(range(1, 8), n, d, t)
     for k in (1, 3, 0, 2):
         late_stage(k).start()
@@ -597,7 +619,10 @@
         heads_back(k).start()
     r.do[rows_of(t), :] = mm_bt(r.bg[...], r.wo[t]).astype(BF)
 
-    for copy in load_s3[1:8:2] + load_x:
+    for w in range(2):
+        for k in range(2):
+            load_two[w, k][0].start()
+    for copy in load_x:
         copy.start()
 
     def ffn_three(w, k):
@@ -605,9 +630,12 @@
 
     def start_ffn_three(w):
         for k in range(2):
-            for copy in load_s3[4 * w + 2 * k : 4 * w + 2 * k + 2]:
+            for copy in load_tot[w, k] + load_two[w, k]:
                 copy.wait()
-            other = r.wo[w, rows : 2 * rows, k * half : (k + 1) * half]
+            if w < 2:
+                other = r.wo[w, rows : 2 * rows, k * half : (k + 1) * half]
+            else:
+                other = jnp.concatenate([r.mg[2 * k], r.mg[2 * k + 1]], axis=1)
             r.s3[w, k] = (r.s3[w, k].astype(F32) + other.astype(F32)).astype(BF)
             ffn_three(w, k).start()
 
@@ -681,16 +709,16 @@
             yield slice(s * q_cols, (s + 1) * q_cols), mm_at(grads, r.mixed_b[s])
 
     dp_start(0, out_terms)
+    load_far.start()
 
     for name in BACK_INS[3:]:
         if name != "mixed":
             loads[name].wait()
-    for k in range(2):
-        late_stage(2 * k + 1).wait_recv()
-        load_s3[9 + 2 * k].start()
     for k in range(1, n):
         heads_back(k).wait_recv()
-    start_ffn_three(2)
+    for c in range(parts):
+        pl.when(is_mid & from_left)(lambda: far_copy(1, c, r.far_h).start())
+        pl.when(is_mid & jnp.logical_not(from_left))(lambda: far_copy(0, c, r.far_h).start())
 
     def turn_back(grad, part):
         return (grad * r.cos_b[part, :] - pltpu.roll(grad, HD // 2, 1) * r.sin_b[part, :]).astype(BF)
@@ -754,8 +782,6 @@
                 scatter(n - 2 - i, c, False).wait_send()
                 scatter(n - 1 - i, c, False).start()
 
-    from_left = t * 2 < n - 1
-
     def pass_on(index, near):
         for c in range(parts):
             piece = pl.ds(c * part_rows, part_rows)
@@ -795,16 +821,37 @@
             part = slice(first, first + 512)
             yield part, mm_at(normed, r.dqkv[:, part])
 
+    def far_on():
+        for i in range(2):
+            for c in range(parts):
+                piece = pl.ds(c * part_rows, part_rows)
+
+                @pl.when(is_mid & (from_left == (i == 0)))
+                def _():
+                    far_copy(i, c).wait_recv()
+                    total = r.far_land[piece].astype(F32) + r.bg[piece].astype(F32)
+                    r.far_land[piece] = total.astype(BF)
+                    far_copy(i, c).start()
+
+    for k in range(1, n):
+        heads_back(k).wait_send()
+    for k in range(2):
+        late_stage(2 * k + 1).wait_recv()
+        for copy in load_two[2, k]:
+            copy.start()
     dp_start(1, project_terms)
+    start_ffn_three(2)
     start_three(0)
+    load_far.wait()
     next_sends(2)
     pass_on(3, True)
     start_three(1)
+    for i in (4, 5):
+        late_stage(i).start()
+    far_on()
     next_sends(1)
     pass_on(3, False)
     pass_on(2, True)
-    for k in range(1, n):
-        heads_back(k).wait_send()
 
     def out_piece(k):
         s = lax.rem(t + k, n)
@@ -872,10 +919,29 @@
 
     for k in range(1, n):
         out_piece(k).wait_send()
-    for k in range(4):
-        late_stage(k).wait_send()
-    for k in (0, 2):
-        late_stage(k).wait_recv()
+    for i in range(6):
+        late_stage(i).wait_send()
+    for i in (0, 2, 4, 5):
+        late_stage(i).wait_recv()
+    for i, last in ((0, 0), (1, n - 1)):
+
+        @pl.when(t == last)
+        def _():
+            for c in range(parts):
+                far_copy(i, c).wait_recv()
+
+        @pl.when(is_mid)
+        def _():
+            for c in range(parts):
+                far_copy(i, c).wait_send()
+
+    @pl.when(is_mid)
+    def _():
+        r.far_land[...] = jnp.zeros_like(r.far_land)
+
+    keep_far = pltpu.make_async_copy(r.far_land, r.far_add, r.far_sem.at[0])
+    keep_far.start()
+    keep_far.wait()
     for w in range(3):
         for k in range(2):
             ffn_three(w, k).wait()
@@ -894,7 +960,7 @@
                     scatter(s, c, to_right).wait_send()
 
 
-def back_call(n, arrays, gain_a, gain_f, bias, x_all, w_out_all, totals, twos, late):
+def back_call(n, arrays, gain_a, gain_f, bias, x_all, w_out_all, totals, twos, late, far):
     rows, width = arrays["hid"].shape
     q_cols, kv_cols = arrays["q"].shape[1], arrays["k"].shape[1]
     all_cols = q_cols + 2 * kv_cols
@@ -913,10 +979,11 @@
             shape((chunk, q_cols), F32),
             shape((8, chunk), F32),
             shape((3, 2, chunk, width // 2), BF),
-            shape((4, chunk, width // 2), BF),
+            shape((6, chunk, width // 2), BF),
+            shape((rows, width), BF),
         ],
-        in_specs=[any_spec] * len(BACK_INS) + [vmem_spec] * 3 + [any_spec] * 5,
-        out_specs=[vmem_spec] * 4 + [any_spec] * 2,
+        in_specs=[any_spec] * len(BACK_INS) + [vmem_spec] * 3 + [any_spec] * 6,
+        out_specs=[vmem_spec] * 4 + [any_spec] * 3,
         scratch_shapes=[pltpu.VMEM(arrays[name].shape, arrays[name].dtype) for name in BACK_INS]
         + [
             pltpu.VMEM((n, q_cols, width), BF),
@@ -939,6 +1006,7 @@
             pltpu.VMEM((9, 16, chunk), F32),
             pltpu.VMEM((7, 8, chunk), F32),
             pltpu.VMEM((n - 1, 16, chunk), F32),
+            pltpu.VMEM((rows, width), BF),
             dma((len(BACK_INS),)),
             dma((n,)),
             dma((n,)),
@@ -961,20 +1029,24 @@
             dma((7,)),
             dma((n - 1,)),
             dma((n - 1,)),
-            dma((4,)),
-            dma((4,)),
+            dma((6,)),
+            dma((6,)),
+            dma((2, 2)),
+            dma((1,)),
+            dma((2, parts)),
+            dma((2, parts)),
         ],
         compiler_params=pltpu.CompilerParams(
-            vmem_limit_bytes=63 * 1024 * 1024, collective_id=3, has_side_effects=True
+            vmem_limit_bytes=64 * 1024 * 1024 - 65536, collective_id=3, has_side_effects=True
         ),
         cost_estimate=pl.CostEstimate(flops=1 << 36, bytes_accessed=1 << 26, transcendentals=0),
         name="back",
-    )(*[arrays[name] for name in BACK_INS], gain_a, gain_f, bias, x_all, w_out_all, totals, twos, late)
-
-
-def finish_kernel(tot, two, late, three, proj, out, ig, oo, gate, up, down, wq, wk, wv, wo, ig_out, oo_out):
+    )(*[arrays[name] for name in BACK_INS], gain_a, gain_f, bias, x_all, w_out_all, totals, twos, late, far)
+
+
+def finish_kernel(tot, two, near, late, three, proj, out, ig, base, far, gate, up, down, wq, wk, wv, wo, ig_out, oo_out):
     def total(w):
-        other = two[w, 0] if w < 2 else late[0]
+        other = (two[0, 0], near[0], late[0])[w]
         return tot[w, 0].astype(F32) + other.astype(F32) + three[w, 0].astype(F32)
 
     down[...] = total(0).T
@@ -982,7 +1054,7 @@
     up[...] = total(2)
     wo[...] = out[...].T
     ig_out[...] = ig[...]
-    oo_out[...] = oo[...]
+    oo_out[...] = (base[...] + far[...].astype(F32)).astype(BF)
 
     @pl.when(pl.program_id(0) == 0)
     def _():
@@ -994,7 +1066,7 @@
         wv[...] = proj[:, wk.shape[1] :]
 
 
-def finish_call(totals, twos, late, threes, project_grad, out_grad, input_grad, output):
+def finish_call(totals, twos, late, threes, project_grad, out_grad, input_grad, base, far):
     chunk, half = totals.shape[2:]
     rows, width = input_grad.shape
     all_cols, q_cols = project_grad.shape[1], out_grad.shape[1]
@@ -1008,11 +1080,13 @@
         grid=(2,),
         in_specs=[
             spec((3, 1, chunk, half), lambda k: (0, 2 * k, 0, 0)),
-            spec((2, 1, chunk, half), lambda k: (0, 2 * k, 0, 0)),
+            spec((1, 1, chunk, half), lambda k: (0, 2 * k, 0, 0)),
+            spec((1, chunk, half), lambda k: (4 + k, 0, 0)),
             spec((1, chunk, half), lambda k: (2 * k, 0, 0)),
             spec((3, 1, chunk, half), lambda k: (0, k, 0, 0)),
             spec((chunk, all_cols // 2), side),
             spec((chunk, q_cols // 2), side),
+            spec((rows, width // 2), side),
             spec((rows, width // 2), side),
             spec((rows, width // 2), side),
         ],
@@ -1040,7 +1114,7 @@
         ],
         compiler_params=pltpu.CompilerParams(vmem_limit_bytes=VMEM_LIMIT),
         name="finish",
-    )(totals, twos, late, threes, project_grad, out_grad, input_grad, output)
+    )(totals, twos, late, late, threes, project_grad, out_grad, input_grad, base, far)
 
 
 def ffn_kernel(
@@ -1298,11 +1372,11 @@
 
 MID_NAMES = (
     ("own", "cot_in", "wg_h", "wu_h", "wd_h", "middle_h"),
-    ("cot", "h_out", "tot", "two", "late", "fi_out", "output"),
+    ("cot", "h_out", "tot", "two", "late", "fi_out", "base", "far"),
     ("wg", "wu", "wd", "n_buf", "gu", "h_st", "c_buf", "part", "land", "acc"),
     ("w_sem", "own_sem", "c_sem", "h_sem", "re_sem", "tot_sem", "out_sem", "ready"),
     ("ag_send", "ag_recv", "ct_send", "ct_recv", "rs_send", "rs_recv"),
-    ("one_send", "one_recv", "two_send", "two_recv", "late_sem"),
+    ("one_send", "one_recv", "two_send", "two_recv", "late_sem", "far_sem"),
 )
 
 
@@ -1423,7 +1497,7 @@
         lax.fori_loop(0, tiles, one_tile, 0)
         keep_h(i).start()
         r.part[0, s] = r.acc[...].astype(BF)
-        if i:
+        if 0 < i < n - 1:
             end_sends(0, i, range(parts))
 
     def backward(i, chunks):
@@ -1533,10 +1607,16 @@
             block(w, j).at[:, cols], r.two.at[w, k], r.two_send.at[w, k], r.two_recv.at[w, k], dp=d ^ (2, 2, 4, 4)[k]
         )
 
-    def keep_late(k):
+    def keep_late(i):
+        k = i if i < 4 else 2 * (i - 4)
         j = (2 * y + 1 - x, 2 * (1 - y) + 1 - x, 2 * (1 - y) + x, 2 * (1 - y) + 1 - x)[k]
         cols = pl.ds((k // 2) * halves, halves)
-        return pltpu.make_async_copy(block(2, j).at[:, cols], r.late.at[k], r.late_sem.at[k])
+        return pltpu.make_async_copy(block(2 if i < 4 else 1, j).at[:, cols], r.late.at[i], r.late_sem.at[i])
+
+    def leave(w, k):
+        if w == 0 or (w == 1 and k % 2):
+            return stage_two(w, k)
+        return keep_late(k if w == 2 else 4 + k // 2)
 
     def keep_total(w, k):
         j = (2 * y + x, 2 * (1 - y) + x, 2 * y + x, 2 * y + 1 - x)[k]
@@ -1578,23 +1658,16 @@
         for j in (2, 3):
             stage_one(w, j).wait_send()
         for k in range(4):
-            if w < 2:
-                stage_two(w, k).start()
-            else:
-                keep_late(k).start()
+            leave(w, k).start()
             keep_total(w, k).start()
         if w == 0:
             pass_on(0, 2, True)
-    pass_on(0, 3, True)
-    pass_on(0, 3, False)
-    pass_on(1, 2, True)
-    pass_on(1, 3, True)
-    pass_on(1, 3, False)
-
+        if w == 1:
+            end_sends(0, n - 1, everything)
     def total_of(q):
         r.acc[...] += r.part[q, t].astype(F32)
         for to_right in (True, False):
-            has_source = t > 0 if to_right else t < n - 1
+            has_source = (t > 0 if to_right else t < n - 1) if q else is_mid
 
             @pl.when(has_source)
             def _():
@@ -1612,23 +1685,37 @@
     add_middle.start()
     add_middle.wait()
     total_of(0)
-    r.h_st[...] = r.acc[...].astype(BF)
-    keep_output = pltpu.make_async_copy(r.h_st, r.output, r.out_sem.at[0])
-    keep_output.start()
+    keep_base = pltpu.make_async_copy(r.acc, r.base, r.out_sem.at[0])
+    keep_base.start()
+    pass_on(1, 2, True)
+    pass_on(1, 3, True)
+    pass_on(1, 3, False)
+    keep_base.wait()
+
+    for to_right in (True, False):
+        s = n - 1 if to_right else 0
+
+        @pl.when(is_mid & (from_left == to_right))
+        def _():
+            for c in range(parts):
+                scatter(0, s, c, to_right).wait_recv()
+            r.part[0, s] = (r.part[0, s].astype(F32) + r.land[0, s].astype(F32)).astype(BF)
+
+    keep_far = [pltpu.make_async_copy(r.part.at[0, s], r.far.at[i], r.far_sem.at[i]) for i, s in ((0, 0), (1, n - 1))]
+    for copy in keep_far:
+        copy.start()
+
     r.acc[...] = jnp.zeros_like(r.acc)
     total_of(1)
     keep_fi = pltpu.make_async_copy(r.acc, r.fi_out, r.out_sem.at[1])
     keep_fi.start()
-    keep_output.wait()
     keep_fi.wait()
-
+    for copy in keep_far:
+        copy.wait()
     for w in range(3):
         for k in range(4):
             keep_total(w, k).wait()
-            if w < 2:
-                stage_two(w, k).wait()
-            else:
-                keep_late(k).wait()
+            leave(w, k).wait()
     for s in range(n):
         for to_right in (True, False):
             goes_on = t < n - 1 if to_right else t > 0
@@ -1643,9 +1730,12 @@
 
             @pl.when(goes_on & (s > t if to_right else s < t))
             def _():
-                for q in range(2):
-                    for c in range(parts):
-                        scatter(q, s, c, to_right).wait_send()
+                for c in range(parts):
+                    scatter(1, s, c, to_right).wait_send()
+                    if 0 < s < n - 1:
+                        scatter(0, s, c, to_right).wait_send()
+                    else:
+                        pl.when(is_end)(lambda: scatter(0, s, c, to_right).wait_send())
 
 
 def middle_call(n, own_rows, cot_part, w_gate, w_up, w_down, middle):
@@ -1659,10 +1749,11 @@
     dma = pltpu.SemaphoreType.DMA
     return pl.pallas_call(
         functools.partial(middle_kernel, n),
-        out_shape=[wide, shape((n, rows, units), BF), shape((3, *piece), BF), shape((2, *piece), BF), shape(piece, BF)]
-        + [shape((rows, width), F32), shape((rows, width), BF)],
+        out_shape=[wide, shape((n, rows, units), BF), shape((3, *piece), BF), shape((2, *piece), BF)]
+        + [shape((6, *piece[1:]), BF), shape((rows, width), F32), shape((rows, width), F32)]
+        + [shape((2, rows, width), BF)],
         in_specs=[any_spec] * 6,
-        out_specs=[any_spec] * 7,
+        out_specs=[any_spec] * 8,
         input_output_aliases={1: 0},
         scratch_shapes=[
             pltpu.VMEM((width, units), BF),
@@ -1693,7 +1784,8 @@
             dma((3, 4)),
             dma((3, 4)),
             dma((3, 4)),
-            dma((4,)),
+            dma((6,)),
+            dma((2,)),
         ],
         compiler_params=pltpu.CompilerParams(
             vmem_limit_bytes=64 * 1024 * 1024 - 65536, collective_id=1, has_side_effects=True
@@ -1807,7 +1899,7 @@
     w_out_all = w_out_all.reshape(n_t * q_cols, width)
     rows_wide = hidden_in.astype(F32)
     if fused:
-        unused_cot, unused_h, totals, twos, late, ffn_in_grad, output = middle_call(
+        unused_cot, unused_h, totals, twos, late, ffn_in_grad, base, far = middle_call(
             n_t, normed_ffn, cot_all, w_gate, w_up, w_down, middle
         )
         arrays = dict(
@@ -1827,7 +1919,7 @@
             wk=w_key,
             wv=w_value,
         )
-        input_grad, project_wgrad, out_grad, gain_grads, threes, late_twos = back_call(
+        input_grad, project_wgrad, out_grad, gain_grads, threes, late_twos, far_sum = back_call(
             n_t,
             arrays,
             gain_attn[None],
@@ -1838,9 +1930,10 @@
             totals,
             twos,
             late,
+            far,
         )
         w_gate_grad, w_up_grad, w_down_grad, w_query_grad, w_key_grad, w_value_grad, w_out_grad, input_grad, output = (
-            finish_call(totals, twos, late_twos, threes, project_wgrad, out_grad, input_grad, output)
+            finish_call(totals, twos, late_twos, threes, project_wgrad, out_grad, input_grad, base, far_sum)
         )
         gain_attn_grad, gain_ffn_grad = gain_grads[0], gain_grads[1]
     else:

time: 521 us -> 502 us (0.964)
  Pallas kernels: 501 us -> 484 us
    pallas_call x1, Pallas kernels: 210 us -> 185 us  [middle_call(): pl.pallas_call(functools.partial(middle_kernel, n), out_shape=[wide, shap...]
    pallas_call x1, Pallas kernels: 138 us -> 144 us  [back_call(): pl.pallas_call(functools.partial(back_kernel, n), out_shape=[shape((rows,...]
where the time goes in v4:
time: 502 us; the launch traced here: 495 us
  Pallas kernels  484 us (96%)
  local copies, waits for them, and re-layouts  5.49 us (1%)
    pallas_call x1, Pallas kernels, middle_call(): pl.pallas_call(functools.partial(middle_kernel, n), out_shape=[wide, shap...  185 us
    pallas_call x1, Pallas kernels, attn_call(): pl.pallas_call(functools.partial(attn_kernel, n_dp, n, one_hop), out_shap...  146 us
    pallas_call x1, Pallas kernels, back_call(): pl.pallas_call(functools.partial(back_kernel, n), out_shape=[shape((rows,...  144 us

profile of v4, /device:TPU:0, one launch (start us, length us, event | category | flops | bytes accessed | tf_op | source)
XLA Modules:
  0.0 495.4 jit_solution(15742200201500770599)
XLA Ops:
  0.6 0.8 slice_reduce_fusion
  1.4 0.2 select_reduce_fusion
  1.6 0.7 add.21
  2.3 0.1 fusion.5
  2.4 0.1 and_reduce_fusion.2
  2.5 0.1 and_reduce_fusion.1
  2.6 0.1 and_reduce_fusion
  2.7 0.1 fusion.7
  2.8 0.1 copy.25
  2.9 0.1 fusion.2
  2.9 1.3 broadcast_in_dim.24.gain_a_ref.refs_15_
  4.2 1.3 broadcast_in_dim.27.gain_f_ref.refs_16_
  5.5 0.7 broadcast_bitcast_fusion.bias_ref.refs_17_
  6.2 1.9 fusion
  8.1 1.3 pad_maximum_fusion
  9.4 145.5 %attn.1 = (bf16[4,256,2048]{2,1,0:T(8,128)(2,1)}, bf16[4,256,2048]{2,1,0:T(8,128)(2,1)}, bf16[4,512,2048]{2,1,0:T(8,128)(2,1)}, bf16[1024,512]{1,0:T(8,128)(2,1)...) custom-call(bf16[256,2048]{1,0:T(8,128)(2,1)} %refs_3_.3, ...), custom_call_target="tpu_custom_call" | custom-call | flops 4294967296 | bytes 33554432 | tf_op jit(solution)/shard_map/attn/pallas_call | solution.py:379
  155.0 185.4 %middle.1 = (bf16[4,256,2048]{2,1,0:T(8,128)(2,1)}, bf16[4,256,2048]{2,1,0:T(8,128)(2,1)}, bf16[3,4,256,1024]{3,2,1,0:T(8,128)(2,1)}, bf16[2,4,256,1024]{3,2,1,0...) custom-call(bf16[256,2048]{1,0:T(8,128)(2,1)} %get-tuple-element.44., ...), custom_call_target="tpu_custom_call", output_to_operand_aliasing={{0}: (1, {})} | custom-call | flops 77309411328 | bytes 25165824 | tf_op jit(solution)/shard_map/middle/pallas_call | solution.py:1750
  340.3 144.4 %back.1 = (bf16[256,2048]{1,0:T(8,128)(2,1)}, f32[256,1024]{1,0:T(8,128)}, f32[256,512]{1,0:T(8,128)}, f32[8,256]{1,0:T(8,128)}, bf16[3,2,256,1024]{3,2,1,0:T(8,...) custom-call(f32[256,2048]{1,0:T(8,128)} %get-tuple-element.49.refs_0_, ...), custom_call_target="tpu_custom_call" | custom-call | flops 68719476736 | bytes 67108864 | tf_op jit(solution)/shard_map/back/pallas_call | solution.py:974
  484.8 9.1 %finish.1 = (f32[256,2048]{1,0:T(8,128)}, f32[256,2048]{1,0:T(8,128)}, f32[2048,256]{1,0:T(8,128)}, f32[256,512]{1,0:T(8,128)}, f32[256,256]{1,0:T(8,128)}, /*in...) custom-call(bf16[3,4,256,1024]{3,2,1,0:T(8,128)(2,1)} %get-tuple-element.47.refs_20_, ...), custom_call_target="tpu_custom_call" | custom-call | tf_op jit(solution)/shard_map/finish/pallas_call | solution.py:1078
  493.9 1.3 fusion.8
  (2 shorter events, 0.0 us)

commit v5 on v4

--- a/solution.py
+++ b/solution.py
@@ -47,17 +47,6 @@
         step = jnp.any(step[:, :, None] & step[None, :, :], axis=1)
     ancestry = step.astype(F32)
     return ancestry, jnp.sum(ancestry, axis=1) - 1.0
-
-
-def rope_tables(depth):
-    token_total = depth.shape[0] * BLK
-    offsets = (jnp.arange(token_total, dtype=jnp.int32) % BLK).astype(F32)
-    places = jnp.repeat(depth, BLK) * BLK + offsets
-    freq_index = jnp.arange(HD // 2, dtype=jnp.int32).astype(F32)
-    inverse_freq = ROPE_BASE ** (-2.0 * freq_index / HD)
-    angles = places[:, None] * inverse_freq[None, :]
-    cosine, sine = jnp.cos(angles), jnp.sin(angles)
-    return jnp.concatenate([cosine, cosine], axis=1), jnp.concatenate([-sine, sine], axis=1)
 
 
 def head_cols(h):
@@ -129,14 +118,11 @@
     one_hop,
     hidden_ref,
     cot_ref,
-    gain_a_ref,
-    gain_f_ref,
+    gains_ref,
     wq_hbm,
     wk_hbm,
     wv_hbm,
     wo_hbm,
-    cos_ref,
-    sin_ref,
     bias_ref,
     x_out,
     cot_out,
@@ -149,6 +135,8 @@
     mixed_ref,
     middle_ref,
     normed_ref,
+    cos_ref,
+    sin_ref,
     own_buf,
     x_buf,
     wq_ref,
@@ -179,6 +167,7 @@
     share = q_cols // n_dp
     half = q_cols // 2
     order = arrival_order(t, n)
+    gain_a_ref, gain_f_ref = gains_ref.at[pl.ds(0, 1)], gains_ref.at[pl.ds(1, 1)]
     is_mid = (t > 0) & (t < n - 1)
     core, plane = lax.rem(d, 2), d // 2
     masks = list(range(2, n_dp, 2))
@@ -260,6 +249,17 @@
     for k in range(1, n):
         wo_line(k).start()
     keep_rows(0).start()
+
+    lane = lax.broadcasted_iota(jnp.int32, (BLK, HD), 1)
+    low = lane < HD // 2
+    index = jnp.where(low, lane, lane - HD // 2).astype(F32)
+    frequency = jnp.exp(index * (-2.0 * math.log(ROPE_BASE) / HD))
+    offset = lax.broadcasted_iota(jnp.int32, (BLK, HD), 0).astype(F32)
+    for b in range(n * rows // BLK):
+        angles = (bias_ref[b : b + 1, n * rows :] + offset) * frequency
+        sine = jnp.sin(angles)
+        cos_ref[b * BLK : (b + 1) * BLK, :] = jnp.cos(angles)
+        sin_ref[b * BLK : (b + 1) * BLK, :] = jnp.where(low, -sine, sine)
 
     for copy in load_w:
         copy.wait()
@@ -367,7 +367,7 @@
                     gather_cot(s, to_right).wait_send()
 
 
-def attn_call(n_dp, n, one_hop, hidden, cot, gain_a, gain_f, wq, wk, wv, wo, cosine, sine, bias):
+def attn_call(n_dp, n, one_hop, hidden, cot, gains, wq, wk, wv, wo, bias):
     rows, width = hidden.shape
     q_cols, kv_cols = wq.shape[1], wk.shape[1]
     tokens = n * rows
@@ -390,9 +390,11 @@
             shape((n, rows, q_cols), BF),
             shape((rows, width), F32),
             shape((rows, width), BF),
+            shape((tokens, HD), F32),
+            shape((tokens, HD), F32),
         ],
-        in_specs=[vmem_spec, any_spec, vmem_spec, vmem_spec] + [any_spec] * 4 + [vmem_spec] * 3,
-        out_specs=[any_spec] * 3 + [vmem_spec] * 8,
+        in_specs=[vmem_spec, any_spec, vmem_spec] + [any_spec] * 4 + [vmem_spec],
+        out_specs=[any_spec] * 3 + [vmem_spec] * 10,
         scratch_shapes=[
             pltpu.VMEM((rows, width), BF),
             pltpu.VMEM((n, rows, width), BF),
@@ -423,7 +425,7 @@
             flops=2 * tokens * width * (q_cols + 2 * kv_cols), bytes_accessed=1 << 25, transcendentals=0
         ),
         name="attn",
-    )(hidden, cot, gain_a, gain_f, wq, wk, wv, wo, cosine, sine, bias)
+    )(hidden, cot, gains, wq, wk, wv, wo, bias)
 
 
 def arrival_order(t, n):
@@ -491,7 +493,7 @@
 BACK_INS = ("fi", "mid", "cot", "hid", "q", "k", "v", "m", "lse", "cos", "sin", "mixed", "wq", "wk", "wv")
 BACK_NAMES = (
     BACK_INS,
-    ("gain_a", "gain_f", "bias", "x_h", "wo_h", "tot_h", "two_h", "late_h", "far_h"),
+    ("gains", "bias", "x_h", "wo_h", "tot_h", "two_h", "late_h", "far_h"),
     ("input_grad", "project_grad", "out_grad", "gain_grad", "three_h", "late_two", "far_add"),
     tuple(name + "_b" for name in BACK_INS),
     ("wo", "bg", "mg", "do", "dqkv", "dk_acc", "dv_acc", "got", "one_o", "one_p", "two_o", "two_p"),
@@ -506,6 +508,7 @@
 def back_kernel(n, *refs):
     names = [name for group in BACK_NAMES for name in group]
     r = types.SimpleNamespace(**dict(zip(names, refs, strict=True)))
+    r.gain_a, r.gain_f = r.gains.at[pl.ds(0, 1)], r.gains.at[pl.ds(1, 1)]
     t, d = lax.axis_index("tensor"), lax.axis_index("dp")
     rows, width = r.bg.shape
     q_cols, kv_cols = r.q_b.shape[1], r.k_b.shape[1]
@@ -960,7 +963,7 @@
                     scatter(s, c, to_right).wait_send()
 
 
-def back_call(n, arrays, gain_a, gain_f, bias, x_all, w_out_all, totals, twos, late, far):
+def back_call(n, arrays, gains, bias, x_all, w_out_all, totals, twos, late, far):
     rows, width = arrays["hid"].shape
     q_cols, kv_cols = arrays["q"].shape[1], arrays["k"].shape[1]
     all_cols = q_cols + 2 * kv_cols
@@ -982,7 +985,7 @@
             shape((6, chunk, width // 2), BF),
             shape((rows, width), BF),
         ],
-        in_specs=[any_spec] * len(BACK_INS) + [vmem_spec] * 3 + [any_spec] * 6,
+        in_specs=[any_spec] * len(BACK_INS) + [vmem_spec] * 2 + [any_spec] * 6,
         out_specs=[vmem_spec] * 4 + [any_spec] * 3,
         scratch_shapes=[pltpu.VMEM(arrays[name].shape, arrays[name].dtype) for name in BACK_INS]
         + [
@@ -1041,7 +1044,7 @@
         ),
         cost_estimate=pl.CostEstimate(flops=1 << 36, bytes_accessed=1 << 26, transcendentals=0),
         name="back",
-    )(*[arrays[name] for name in BACK_INS], gain_a, gain_f, bias, x_all, w_out_all, totals, twos, late, far)
+    )(*[arrays[name] for name in BACK_INS], gains, bias, x_all, w_out_all, totals, twos, late, far)
 
 
 def finish_kernel(tot, two, near, late, three, proj, out, ig, base, far, gate, up, down, wq, wk, wv, wo, ig_out, oo_out):
@@ -1889,11 +1892,12 @@
         return lax.ppermute(value, "tensor", [(i, (i + shift) % n_t) for i in range(n_t)])
 
     ancestry, depth = tree_tables(segments, parents)
-    cosine, sine = rope_tables(depth)
     bias = jnp.where(jnp.repeat(ancestry, BLK, axis=1) > 0.5, 0.0, NEG)
+    bias = jnp.concatenate([bias, jnp.broadcast_to(depth[:, None] * BLK, (depth.shape[0], HD))], axis=1)
+    gains = jnp.stack([gain_attn_wide, gain_ffn_wide])
     fused = n_dp == 8 and n_t == 4 and units == width and q_cols == 2 * own and tokens * 2 == width
-    x_all, cot_all, w_out_all, queries, keys, values, mixed, lse, mixed_own, middle, normed_ffn = attn_call(
-        n_dp, n_t, fused, hidden_in, cotangent, gain_attn[None], gain_ffn[None], w_query, w_key, w_value, w_out, cosine, sine, bias
+    x_all, cot_all, w_out_all, queries, keys, values, mixed, lse, mixed_own, middle, normed_ffn, cosine, sine = attn_call(
+        n_dp, n_t, fused, hidden_in, cotangent, gains, w_query, w_key, w_value, w_out, bias
     )
     x_all = x_all.reshape(tokens, width)
     w_out_all = w_out_all.reshape(n_t * q_cols, width)
@@ -1922,8 +1926,7 @@
         input_grad, project_wgrad, out_grad, gain_grads, threes, late_twos, far_sum = back_call(
             n_t,
             arrays,
-            gain_attn[None],
-            gain_ffn[None],
+            gains,
             bias,
             x_all.reshape(n_t, own, width),
             w_out_all.reshape(n_t, q_cols, width),

time: 502 us -> 498 us (level)
  no operation moved by 1% of the time
where the time goes in v5:
time: 498 us; the launch traced here: 491 us
  Pallas kernels  484 us (97%)
    pallas_call x1, Pallas kernels, middle_call(): pl.pallas_call(functools.partial(middle_kernel, n), out_shape=[wide, shap...  185 us
    pallas_call x1, Pallas kernels, attn_call(): pl.pallas_call(functools.partial(attn_kernel, n_dp, n, one_hop), out_shap...  145 us
    pallas_call x1, Pallas kernels, back_call(): pl.pallas_call(functools.partial(back_kernel, n), out_shape=[shape((rows,...  144 us

profile of v5, /device:TPU:0, one launch (start us, length us, event | category | flops | bytes accessed | tf_op | source)
XLA Modules:
  0.0 491.5 jit_solution(4735679827258567900)
XLA Ops:
  0.6 0.8 slice_reduce_fusion
  1.4 0.2 select_reduce_fusion
  1.6 0.7 add.8
  2.3 0.1 fusion
  2.4 0.1 and_reduce_fusion.2
  2.5 0.1 and_reduce_fusion.1
  2.6 0.1 and_reduce_fusion
  2.7 0.1 fusion.1
  2.8 0.1 copy.25
  2.9 0.1 broadcast_in_dim.26
  2.9 0.7 stack.13
  3.6 0.7 stack.14
  4.3 0.6 maximum_convert_fusion.gains_ref.refs_15_
  4.9 0.1 broadcast_bitcast_fusion
  5.0 0.6 pad_maximum_fusion.bias_ref.refs_16_
  5.6 145.5 %attn.1 = (bf16[4,256,2048]{2,1,0:T(8,128)(2,1)}, bf16[4,256,2048]{2,1,0:T(8,128)(2,1)}, bf16[4,512,2048]{2,1,0:T(8,128)(2,1)}, bf16[1024,512]{1,0:T(8,128)(2,1)...) custom-call(bf16[256,2048]{1,0:T(8,128)(2,1)} %refs_3_.3, ...), custom_call_target="tpu_custom_call" | custom-call | flops 4294967296 | bytes 33554432 | tf_op jit(solution)/shard_map/attn/pallas_call | solution.py:379
  151.1 185.3 %middle.1 = (bf16[4,256,2048]{2,1,0:T(8,128)(2,1)}, bf16[4,256,2048]{2,1,0:T(8,128)(2,1)}, bf16[3,4,256,1024]{3,2,1,0:T(8,128)(2,1)}, bf16[2,4,256,1024]{3,2,1,0...) custom-call(bf16[256,2048]{1,0:T(8,128)(2,1)} %get-tuple-element.46., ...), custom_call_target="tpu_custom_call", output_to_operand_aliasing={{0}: (1, {})} | custom-call | flops 77309411328 | bytes 25165824 | tf_op jit(solution)/shard_map/middle/pallas_call | solution.py:1753
  336.5 144.4 %back.1 = (bf16[256,2048]{1,0:T(8,128)(2,1)}, f32[256,1024]{1,0:T(8,128)}, f32[256,512]{1,0:T(8,128)}, f32[8,256]{1,0:T(8,128)}, bf16[3,2,256,1024]{3,2,1,0:T(8,...) custom-call(f32[256,2048]{1,0:T(8,128)} %get-tuple-element.51.refs_0_, ...), custom_call_target="tpu_custom_call" | custom-call | flops 68719476736 | bytes 67108864 | tf_op jit(solution)/shard_map/back/pallas_call | solution.py:977
  480.9 9.1 %finish.1 = (f32[256,2048]{1,0:T(8,128)}, f32[256,2048]{1,0:T(8,128)}, f32[2048,256]{1,0:T(8,128)}, f32[256,512]{1,0:T(8,128)}, f32[256,256]{1,0:T(8,128)}, /*in...) custom-call(bf16[3,4,256,1024]{3,2,1,0:T(8,128)(2,1)} %get-tuple-element.49.refs_19_, ...), custom_call_target="tpu_custom_call" | custom-call | tf_op jit(solution)/shard_map/finish/pallas_call | solution.py:1081
  490.0 1.3 fusion.2
  (1 shorter events, 0.0 us)
